TPU v7x, 32 devices: a whole 2x2x4 slice. The times are simulated.
32 devices in a mesh: head: 4 (over y, x), seq: 8 (over z, core).
Axes of the slice: x: 2, y: 2, z: 4, core: 2. Of those that a mesh axis runs over, the one named last changes fastest.
Arguments:
- tokens: bfloat16 [4, 1024, 1024], P('head', 'seq'), may hold values from -6 to 6
- w_query: bfloat16 [1024, 1024], P(('head', 'seq')), may hold values from -0.1875 to 0.1875
- w_key: bfloat16 [1024, 1024], P(('head', 'seq')), may hold values from -0.1875 to 0.1875
- w_value: bfloat16 [1024, 1024], P(('head', 'seq')), may hold values from -0.1875 to 0.1875
- w_out: bfloat16 [1024, 1024], P(('head', 'seq')), may hold values from -0.75 to 0.75
- w_gate: bfloat16 [1024, 1024], P(('head', 'seq')), may hold values from -0.1875 to 0.1875
- persist_keys: bfloat16 [16, 1024], P(None, ('head', 'seq')), may hold values from -5 to 5
- persist_values: bfloat16 [16, 1024], P(None, ('head', 'seq')), may hold values from -5 to 5
- norm_gain: bfloat16 [1024], P(('head', 'seq')), may hold values from 0.5 to 1.5
- ff_gate: bfloat16 [1024, 2816], P(('head', 'seq')), may hold values from -0.1875 to 0.1875
- ff_up: bfloat16 [1024, 2816], P(('head', 'seq')), may hold values from -0.1875 to 0.1875
- ff_down: bfloat16 [2816, 1024], P(('head', 'seq')), may hold values from -0.109375 to 0.109375
- retention: float32 [4, 1024, 8], P(None, 'seq', 'head'), may hold values from 0.4 to 1
- doc_starts: int32 [4, 6], replicated, may hold values from 0 to 1024, as said below
- valid: int32 [4, 1024], P('head', 'seq'), may hold values from 0 to 1
- teacher: bfloat16 [4, 1024, 1024], P('head', 'seq'), may hold values from -4 to 4
Outputs:
- output: bfloat16 [4, 1024, 1024], P('head', 'seq')
- loss: float32 [], replicated
- grad_tokens: float32 [4, 1024, 1024], P('head', 'seq')
- grad_w_query: float32 [1024, 1024], P(('head', 'seq'))
- grad_w_key: float32 [1024, 1024], P(('head', 'seq'))
- grad_w_value: float32 [1024, 1024], P(('head', 'seq'))
- grad_w_out: float32 [1024, 1024], P(('head', 'seq'))
- grad_w_gate: float32 [1024, 1024], P(('head', 'seq'))
- grad_persist_keys: float32 [16, 1024], P(None, ('head', 'seq'))
- grad_persist_values: float32 [16, 1024], P(None, ('head', 'seq'))
- grad_norm_gain: float32 [1024], P(('head', 'seq'))
- grad_ff_gate: float32 [1024, 2816], P(('head', 'seq'))
- grad_ff_up: float32 [1024, 2816], P(('head', 'seq'))
- grad_ff_down: float32 [2816, 1024], P(('head', 'seq'))
Inputs may be any that keep to these rules, and one draw needn't show every extreme that they name: `doc_starts`: per sequence the starts of its documents in increasing order, beginning with 0; unused entries equal 1024. Every document except a sequence's last has 200 to max(512, 200) positions; one sequence is a single document.
All inputs are finite; a program needn't handle non-finite values.
Results may differ from a plain program's by a relative error of at most 0.018.
Values may be sent and summed in bfloat16 or wider, within the bound.
A program may use at most 256 MiB of HBM per device.

v0:
```python
import jax
import jax.numpy as jnp
from jax import lax
from jax.sharding import PartitionSpec as P

HEAD_COUNT = 8
HD = 128
P_SIZE = 16


HIGHEST = lax.Precision.HIGHEST
MASKED = -1e30
EPSILON = 1e-06


def entering(value, axis, join, neutral, backward):
    count = lax.axis_size(axis)
    place = lax.axis_index(axis)
    ahead = count - 1 - place if backward else place
    gathered = jax.tree.map(
        lambda a, kind: lax.all_gather(a.astype(kind), axis), value, (jnp.bfloat16, jnp.bfloat16)
    )
    state = jax.tree.map(lambda a, e: jnp.zeros_like(a) + jnp.asarray(e, a.dtype), value, neutral)

    def one(hop, state):
        source = count - 1 - hop if backward else hop
        return join(
            state,
            jax.tree.map(
                lambda a, own: lax.dynamic_index_in_dim(a, source, 0, False).astype(own.dtype),
                gathered,
                value,
            ),
        )

    return lax.fori_loop(0, ahead, one, state)


def passed_along(value, axis, by):
    peers = lax.axis_size(axis)
    pairs = [(i, i + by) for i in range(peers) if 0 <= i + by < peers]
    return lax.ppermute(value, axis, pairs)


def from_behind(block, axis, distance):
    devices = range(lax.axis_size(axis))
    route = [((i - distance) % len(devices), i) for i in devices]
    return lax.ppermute(block, axis, route)


def product(left, right):
    return jnp.dot(left, right, preferred_element_type=jnp.float32)


def rows_outer(left, right):
    return jnp.einsum("nd,ne->de", left, right, preferred_element_type=jnp.float32)


def back_product(grad, weight):
    return jnp.einsum("ne,de->nd", grad, weight, preferred_element_type=jnp.float32)


def doc_index(starts, positions):
    return jnp.sum((starts[:, None, :] <= positions[None, :, None]).astype(jnp.int32), axis=-1) - 1


def doc_begin(starts, positions):
    return jnp.any(starts[:, None, :] == positions[None, :, None], axis=-1)


def chain_forward(earlier, later):
    return (earlier[0] * later[0], later[0][..., None, None] * earlier[1] + later[1])


def chain_backward(earlier, later):
    return (earlier[0] * later[0], later[1] + later[0][..., None, None] * earlier[1])


def masked_scores(query_rows, key_rows, query_pos, key_pos, query_seg, key_seg, scale):
    raw = (
        jnp.einsum("sqhd,skhd->sqhk", query_rows, key_rows, preferred_element_type=jnp.float32)
        * scale
    )
    allowed = (key_pos[None, None, :] <= query_pos[None, :, None]) & (
        key_seg[:, None, :] == query_seg[:, :, None]
    )
    return jnp.where(allowed[:, :, None, :], raw, MASKED)


def softmax_grads(
    query_rows,
    key_rows,
    value_rows,
    dout_rows,
    query_pos,
    key_pos,
    query_seg,
    key_seg,
    query_lse,
    query_delta,
    scale,
):
    scores = masked_scores(query_rows, key_rows, query_pos, key_pos, query_seg, key_seg, scale)
    probs = jnp.exp(scores - query_lse[..., None])
    prob_grad = jnp.einsum(
        "sqhd,skhd->sqhk", dout_rows, value_rows, preferred_element_type=jnp.float32
    )
    score_grad = (probs * (prob_grad - query_delta[..., None])).astype(jnp.bfloat16)
    return (probs.astype(jnp.bfloat16), score_grad)


def local(
    tokens,
    w_query,
    w_key,
    w_value,
    w_out,
    w_gate,
    persist_keys,
    persist_values,
    norm_gain,
    ff_gate,
    ff_up,
    ff_down,
    retention,
    doc_starts,
    valid,
    teacher,
):
    gathered = (
        lax.all_gather(w_query, ("head", "seq"), axis=0, tiled=True),
        lax.all_gather(w_key, ("head", "seq"), axis=0, tiled=True),
        lax.all_gather(w_value, ("head", "seq"), axis=0, tiled=True),
        lax.all_gather(w_out, ("head", "seq"), axis=0, tiled=True),
        lax.all_gather(w_gate, ("head", "seq"), axis=0, tiled=True),
        lax.all_gather(jnp.transpose(persist_keys), ("head", "seq"), axis=0, tiled=True),
        lax.all_gather(jnp.transpose(persist_values), ("head", "seq"), axis=0, tiled=True),
        lax.all_gather(norm_gain, ("head", "seq"), axis=0, tiled=True),
        lax.all_gather(ff_gate, ("head", "seq"), axis=0, tiled=True),
        lax.all_gather(ff_up, ("head", "seq"), axis=0, tiled=True),
        lax.all_gather(ff_down, ("head", "seq"), axis=0, tiled=True),
    )
    (
        query_weight,
        key_weight,
        value_weight,
        out_weight,
        gate_weight,
        fixed_key_cols,
        fixed_value_cols,
        gain_weight,
        ffn_gate,
        ffn_up,
        ffn_down,
    ) = gathered
    fixed_key_all = jnp.transpose(fixed_key_cols)
    fixed_value_all = jnp.transpose(fixed_value_cols)
    local_seqs, block, width = tokens.shape
    groups = lax.axis_size("head")
    heads = HEAD_COUNT // groups
    head_place = lax.axis_index("head")
    seq_place = lax.axis_index("seq")
    seq_count = lax.axis_size("seq")
    all_seqs = local_seqs * groups
    length = block * seq_count
    token_count = local_seqs * block
    scale = HD ** (-0.5)
    mem_scale = 0.125 / HD
    token_rows = tokens.reshape(token_count, width)
    query_tok = (
        product(token_rows, query_weight)
        .astype(jnp.bfloat16)
        .reshape(local_seqs, block, HEAD_COUNT, HD)
    )
    key_tok = (
        product(token_rows, key_weight)
        .astype(jnp.bfloat16)
        .reshape(local_seqs, block, HEAD_COUNT, HD)
    )
    value_tok = (
        product(token_rows, value_weight)
        .astype(jnp.bfloat16)
        .reshape(local_seqs, block, HEAD_COUNT, HD)
    )
    gate_pre = product(token_rows, gate_weight)
    query_heads, key_heads, value_heads = (
        lax.all_to_all(query_tok, "head", split_axis=2, concat_axis=0, tiled=True),
        lax.all_to_all(key_tok, "head", split_axis=2, concat_axis=0, tiled=True),
        lax.all_to_all(value_tok, "head", split_axis=2, concat_axis=0, tiled=True),
    )
    fixed_keys = lax.dynamic_slice_in_dim(
        fixed_key_all.reshape(P_SIZE, HEAD_COUNT, HD), head_place * heads, heads, 1
    )
    fixed_values = lax.dynamic_slice_in_dim(
        fixed_value_all.reshape(P_SIZE, HEAD_COUNT, HD), head_place * heads, heads, 1
    )
    own_start = seq_place * block
    own_pos = own_start + jnp.arange(block, dtype=jnp.int32)
    own_seg = doc_index(doc_starts, own_pos)
    own_begin = doc_begin(doc_starts, own_pos)
    last_row = own_start + block - 1
    fixed_scores = (
        jnp.einsum("sqhd,phd->sqhp", query_heads, fixed_keys, preferred_element_type=jnp.float32)
        * scale
    )
    top_start = jnp.max(fixed_scores, axis=-1)
    fixed_exp = jnp.exp(fixed_scores - top_start[..., None])
    acc_start = jnp.einsum(
        "sqhp,phd->sqhd",
        fixed_exp.astype(jnp.bfloat16),
        fixed_values,
        preferred_element_type=jnp.float32,
    )
    key_rows = lax.all_gather(key_heads, "seq", axis=1, tiled=True)
    value_rows = lax.all_gather(value_heads, "seq", axis=1, tiled=True)
    piece_keys = key_rows.shape[1]

    def attend_compute(state):
        running_top, running_total, running_acc = state
        key_pos = jnp.arange(piece_keys, dtype=jnp.int32)
        scores = masked_scores(
            query_heads, key_rows, own_pos, key_pos, own_seg, doc_index(doc_starts, key_pos), scale
        )
        new_top = jnp.maximum(running_top, jnp.max(scores, axis=-1))
        shrink = jnp.exp(running_top - new_top)
        weights_exp = jnp.exp(scores - new_top[..., None])
        new_total = running_total * shrink + jnp.sum(weights_exp, axis=-1)
        new_acc = running_acc * shrink[..., None] + jnp.einsum(
            "sqhk,skhd->sqhd",
            weights_exp.astype(jnp.bfloat16),
            value_rows,
            preferred_element_type=jnp.float32,
        )
        return (new_top, new_total, new_acc)

    final_top, final_total, final_acc = lax.cond(
        jnp.int32(0) <= last_row,
        attend_compute,
        lambda state: state,
        (top_start, jnp.sum(fixed_exp, axis=-1), acc_start),
    )
    attn_rows = final_acc / final_total[..., None]
    lse = final_top + jnp.log(final_total)
    log_retention = jnp.log(retention)
    running = jnp.cumsum(log_retention, axis=1)
    lane = jnp.transpose(running, (0, 2, 1))
    index = jnp.arange(block)
    linked = (index[None, :] <= index[:, None])[None] & (own_seg[:, None, :] == own_seg[:, :, None])
    decay = jnp.where(
        linked[:, None], jnp.exp(jnp.minimum(lane[:, :, :, None] - lane[:, :, None, :], 0.0)), 0.0
    )
    intersection = jnp.einsum(
        "sthd,suhd->shtu", query_heads, key_heads, preferred_element_type=jnp.float32
    )
    mixing = (mem_scale * intersection * decay).astype(jnp.bfloat16)
    inner_mem = jnp.einsum(
        "shtu,suhd->sthd", mixing, value_heads, preferred_element_type=jnp.float32
    )
    carried = ((own_seg == own_seg[:, :1]) & jnp.logical_not(own_begin[:, :1])).astype(jnp.float32)
    lead = jnp.exp(running) * carried[..., None]
    trail = jnp.where(
        (own_seg == own_seg[:, -1:])[..., None], jnp.exp(running[:, -1:, :] - running), 0.0
    )
    query_full = query_heads.astype(jnp.float32)
    key_full = key_heads.astype(jnp.float32)
    value_full = value_heads.astype(jnp.float32)
    block_state = jnp.einsum(
        "suhd,suhe->shde", key_full * trail[..., None], value_full, precision=HIGHEST
    )
    block_keep = lead[:, -1, :]
    identity = (jnp.ones_like(block_keep), jnp.zeros_like(block_state))
    chained = entering((block_keep, block_state), "seq", chain_forward, identity, False)
    state_in = chained[1]
    outer_mem = (
        mem_scale
        * lead[..., None]
        * jnp.einsum("sthd,shde->sthe", query_full, state_in, precision=HIGHEST)
    )
    mixed_heads = (attn_rows + inner_mem + outer_mem).astype(jnp.bfloat16)
    mixed_rows = lax.all_to_all(
        mixed_heads, "head", split_axis=0, concat_axis=2, tiled=True
    ).reshape(token_count, width)
    branch = product(mixed_rows, out_weight)
    gate_sigmoid = jax.nn.sigmoid(gate_pre)
    hidden = token_rows.astype(jnp.float32) + gate_sigmoid * branch
    inv_rms = lax.rsqrt(jnp.mean(hidden * hidden, axis=-1, keepdims=True) + EPSILON)
    normed = hidden * inv_rms
    gain_full = gain_weight.astype(jnp.float32)
    scaled = (normed * gain_full).astype(jnp.bfloat16)
    gate_act = product(scaled, ffn_gate)
    up_act = product(scaled, ffn_up)
    act_sigmoid = jax.nn.sigmoid(gate_act)
    silu_act = gate_act * act_sigmoid
    inner = (silu_act * up_act).astype(jnp.bfloat16)
    final = hidden + product(inner, ffn_down)
    output = final.astype(jnp.bfloat16).reshape(local_seqs, block, width)
    valid_rows = valid.reshape(token_count).astype(jnp.float32)
    error = final - teacher.reshape(token_count, width).astype(jnp.float32)
    sums = lax.psum(
        (jnp.sum(valid_rows * jnp.sum(error * error, axis=-1)), jnp.sum(valid_rows)),
        ("head", "seq"),
    )
    loss = sums[0] / (2.0 * width * sums[1])
    total_tokens = all_seqs * length
    d_out = valid_rows[:, None] * error * (total_tokens / sums[1])
    d_ffn = d_out.astype(jnp.bfloat16)
    grad_down = rows_outer(inner, d_ffn)
    d_inner = back_product(d_ffn, ffn_down)
    d_gate_act = (d_inner * up_act * act_sigmoid * (1.0 + gate_act * (1.0 - act_sigmoid))).astype(
        jnp.bfloat16
    )
    d_up_act = (d_inner * silu_act).astype(jnp.bfloat16)
    grad_ffn_gate = rows_outer(scaled, d_gate_act)
    grad_ffn_up = rows_outer(scaled, d_up_act)
    d_scaled = back_product(d_gate_act, ffn_gate) + back_product(d_up_act, ffn_up)
    grad_gain = jnp.sum(d_scaled * normed, axis=0)
    d_normed = d_scaled * gain_full
    d_hidden = d_out + inv_rms * (
        d_normed - normed * jnp.mean(d_normed * normed, axis=-1, keepdims=True)
    )
    d_branch = (d_hidden * gate_sigmoid).astype(jnp.bfloat16)
    d_gate = (d_hidden * branch * gate_sigmoid * (1.0 - gate_sigmoid)).astype(jnp.bfloat16)
    grad_out_weight = rows_outer(mixed_rows, d_branch)
    grad_gate_weight = rows_outer(token_rows, d_gate)
    d_mixed = (
        back_product(d_branch, out_weight)
        .astype(jnp.bfloat16)
        .reshape(local_seqs, block, HEAD_COUNT, HD)
    )
    dout_heads = lax.all_to_all(d_mixed, "head", split_axis=2, concat_axis=0, tiled=True)
    dout_full = dout_heads.astype(jnp.float32)
    delta = jnp.sum(dout_full * attn_rows, axis=-1)
    fixed_probs = jnp.exp(fixed_scores - lse[..., None])
    fixed_prob_grad = jnp.einsum(
        "sqhd,phd->sqhp", dout_heads, fixed_values, preferred_element_type=jnp.float32
    )
    fixed_score_grad = (fixed_probs * (fixed_prob_grad - delta[..., None])).astype(jnp.bfloat16)
    fixed_key_grad = (
        jnp.einsum(
            "sqhp,sqhd->phd", fixed_score_grad, query_heads, preferred_element_type=jnp.float32
        )
        * scale
    )
    fixed_value_grad = jnp.einsum(
        "sqhp,sqhd->phd",
        fixed_probs.astype(jnp.bfloat16),
        dout_heads,
        preferred_element_type=jnp.float32,
    )
    query_grad_start = (
        jnp.einsum(
            "sqhp,phd->sqhd", fixed_score_grad, fixed_keys, preferred_element_type=jnp.float32
        )
        * scale
    )
    fold_start = (query_grad_start,)
    back_key_rows = lax.all_gather(key_heads, "seq", axis=1, tiled=True)
    back_value_rows = lax.all_gather(value_heads, "seq", axis=1, tiled=True)
    back_piece_keys = back_key_rows.shape[1]

    def back_compute(state):
        key_pos = jnp.arange(back_piece_keys, dtype=jnp.int32)
        probs_low, score_grad = softmax_grads(
            query_heads,
            back_key_rows,
            back_value_rows,
            dout_heads,
            own_pos,
            key_pos,
            own_seg,
            doc_index(doc_starts, key_pos),
            lse,
            delta,
            scale,
        )
        query_grad = (
            state[0]
            + jnp.einsum(
                "sqhk,skhd->sqhd", score_grad, back_key_rows, preferred_element_type=jnp.float32
            )
            * scale
        )
        return (query_grad,)

    folded = lax.cond(jnp.int32(0) <= last_row, back_compute, lambda state: state, fold_start)
    query_att = folded[0]
    empty_local = jnp.zeros((all_seqs, block, heads, HD), jnp.float32)

    def visit(turn, state):
        key_rows, value_rows, key_acc, value_acc = state
        owner = (seq_place - turn) % seq_count
        start = owner * block

        def visit_compute(accs):
            key_pos = start + jnp.arange(block, dtype=jnp.int32)
            probs_low, score_grad = softmax_grads(
                query_heads,
                key_rows,
                value_rows,
                dout_heads,
                own_pos,
                key_pos,
                own_seg,
                doc_index(doc_starts, key_pos),
                lse,
                delta,
                scale,
            )
            key_next = (
                accs[0]
                + jnp.einsum(
                    "sqhk,sqhd->skhd", score_grad, query_heads, preferred_element_type=jnp.float32
                )
                * scale
            )
            value_next = accs[1] + jnp.einsum(
                "sqhk,sqhd->skhd", probs_low, dout_heads, preferred_element_type=jnp.float32
            )
            return (key_next, value_next)

        key_acc, value_acc = lax.cond(
            start <= last_row, visit_compute, lambda accs: accs, (key_acc, value_acc)
        )
        key_rows, value_rows = passed_along((key_rows, value_rows), "seq", 1)
        key_acc, value_acc = (
            from_behind(key_acc.astype(jnp.bfloat16), "seq", 1).astype(key_acc.dtype),
            from_behind(value_acc.astype(jnp.bfloat16), "seq", 1).astype(value_acc.dtype),
        )
        return (key_rows, value_rows, key_acc, value_acc)

    travelled = lax.fori_loop(
        0, seq_count, visit, (key_heads, value_heads, empty_local, empty_local)
    )
    key_att = travelled[2]
    value_att = travelled[3]
    mix_grad_raw = jnp.einsum(
        "sthe,suhe->shtu", dout_heads, value_heads, preferred_element_type=jnp.float32
    )
    intersection_grad = (mem_scale * mix_grad_raw * decay).astype(jnp.bfloat16)
    local_grad = mem_scale * jnp.einsum(
        "sthd,sthe->shde", query_full * lead[..., None], dout_full, precision=HIGHEST
    )
    state_grads = entering((block_keep, local_grad), "seq", chain_backward, identity, True)
    carry_grad = state_grads[1]
    query_mem = jnp.einsum(
        "shtu,suhd->sthd", intersection_grad, key_heads, preferred_element_type=jnp.float32
    )
    query_mem = query_mem + mem_scale * lead[..., None] * jnp.einsum(
        "sthe,shde->sthd", dout_full, state_in, precision=HIGHEST
    )
    key_mem = jnp.einsum(
        "shtu,sthd->suhd", intersection_grad, query_heads, preferred_element_type=jnp.float32
    )
    key_mem = key_mem + trail[..., None] * jnp.einsum(
        "suhe,shde->suhd", value_full, carry_grad, precision=HIGHEST
    )
    value_mem = jnp.einsum(
        "shtu,sthe->suhe", mixing, dout_heads, preferred_element_type=jnp.float32
    )
    value_mem = value_mem + jnp.einsum(
        "suhd,shde->suhe", key_full * trail[..., None], carry_grad, precision=HIGHEST
    )
    query_grad_heads = (query_att + query_mem).astype(jnp.bfloat16)
    key_grad_heads = (key_att + key_mem).astype(jnp.bfloat16)
    value_grad_heads = (value_att + value_mem).astype(jnp.bfloat16)
    query_back, key_back, value_back = (
        lax.all_to_all(query_grad_heads, "head", split_axis=0, concat_axis=2, tiled=True),
        lax.all_to_all(key_grad_heads, "head", split_axis=0, concat_axis=2, tiled=True),
        lax.all_to_all(value_grad_heads, "head", split_axis=0, concat_axis=2, tiled=True),
    )
    query_back = query_back.reshape(token_count, width)
    key_back = key_back.reshape(token_count, width)
    value_back = value_back.reshape(token_count, width)
    grad_query_weight = rows_outer(token_rows, query_back)
    grad_key_weight = rows_outer(token_rows, key_back)
    grad_value_weight = rows_outer(token_rows, value_back)
    token_grad = (
        d_hidden + back_product(d_gate, gate_weight) + back_product(query_back, query_weight)
    )
    token_grad = (
        token_grad + back_product(key_back, key_weight) + back_product(value_back, value_weight)
    )
    fixed_key_full = lax.dynamic_update_slice_in_dim(
        jnp.zeros((P_SIZE, HEAD_COUNT, HD), jnp.float32), fixed_key_grad, head_place * heads, 1
    ).reshape(P_SIZE, width)
    fixed_value_full = lax.dynamic_update_slice_in_dim(
        jnp.zeros((P_SIZE, HEAD_COUNT, HD), jnp.float32), fixed_value_grad, head_place * heads, 1
    ).reshape(P_SIZE, width)
    shards = (
        lax.psum_scatter(grad_query_weight, ("head", "seq"), scatter_dimension=0, tiled=True),
        lax.psum_scatter(grad_key_weight, ("head", "seq"), scatter_dimension=0, tiled=True),
        lax.psum_scatter(grad_value_weight, ("head", "seq"), scatter_dimension=0, tiled=True),
        lax.psum_scatter(grad_out_weight, ("head", "seq"), scatter_dimension=0, tiled=True),
        lax.psum_scatter(grad_gate_weight, ("head", "seq"), scatter_dimension=0, tiled=True),
        lax.psum_scatter(
            jnp.transpose(fixed_key_full), ("head", "seq"), scatter_dimension=0, tiled=True
        ),
        lax.psum_scatter(
            jnp.transpose(fixed_value_full), ("head", "seq"), scatter_dimension=0, tiled=True
        ),
        lax.psum_scatter(grad_gain, ("head", "seq"), scatter_dimension=0, tiled=True),
        lax.psum_scatter(grad_ffn_gate, ("head", "seq"), scatter_dimension=0, tiled=True),
        lax.psum_scatter(grad_ffn_up, ("head", "seq"), scatter_dimension=0, tiled=True),
        lax.psum_scatter(grad_down, ("head", "seq"), scatter_dimension=0, tiled=True),
    )
    return (
        output,
        loss,
        token_grad.reshape(local_seqs, block, width),
        shards[0],
        shards[1],
        shards[2],
        shards[3],
        shards[4],
        jnp.transpose(shards[5]),
        jnp.transpose(shards[6]),
        shards[7],
        shards[8],
        shards[9],
        shards[10],
    )


def solution(mesh):
    in_specs = (
        P("head", "seq", None),
        P(("head", "seq"), None),
        P(("head", "seq"), None),
        P(("head", "seq"), None),
        P(("head", "seq"), None),
        P(("head", "seq"), None),
        P(None, ("head", "seq")),
        P(None, ("head", "seq")),
        P(("head", "seq")),
        P(("head", "seq"), None),
        P(("head", "seq"), None),
        P(("head", "seq"), None),
        P(None, "seq", "head"),
        P(),
        P("head", "seq"),
        P("head", "seq", None),
    )
    out_specs = (
        P("head", "seq", None),
        P(),
        P("head", "seq", None),
        P(("head", "seq"), None),
        P(("head", "seq"), None),
        P(("head", "seq"), None),
        P(("head", "seq"), None),
        P(("head", "seq"), None),
        P(None, ("head", "seq")),
        P(None, ("head", "seq")),
        P(("head", "seq")),
        P(("head", "seq"), None),
        P(("head", "seq"), None),
        P(("head", "seq"), None),
    )
    return jax.shard_map(local, mesh=mesh, in_specs=in_specs, out_specs=out_specs, check_vma=False)
```

profile of v0, /device:TPU:0, one launch (start us, length us, event | category | flops | bytes accessed | tf_op | source)
XLA Modules:
  0.0 2135.9 jit_solution(8159322240170416023)
XLA Ops:
  9.5 60.8 %all-gather.24.cloned.1.call-done = bf16[1024,1024]{1,0:T(8,128)(2,1)} async-done(((bf16[32,1024]{1,0:T(8,128)(2,1)}), bf16[1024,1024]{1,0:T(8,128)(2,1)}) %all-gather.24.cloned.1.call-update) | async-done | bytes 2097168 | tf_op jit(solution)/shard_map/all_gather | solution.py:132
  72.4 9.5 all_to_all.132
  82.0 46.5 %all-gather.26.cloned.1.call-done = bf16[1024,1024]{1,0:T(8,128)(2,1)} async-done(((bf16[32,1024]{1,0:T(8,128)(2,1)}), bf16[1024,1024]{1,0:T(8,128)(2,1)}) %all-gather.26.cloned.1.call-update) | async-done | bytes 2097168 | tf_op jit(solution)/shard_map/all_gather | solution.py:133
  130.7 8.9 all_to_all.133
  147.7 38.6 %psum.15 = f32[]{:T(128)} all-reduce(f32[]{:T(128)} %convert_reduce_fusion.4), channel_id=1, replica_groups=mesh['head'=4,'seq'=8] {'head','seq'}, use_global_device_ids=true, to_apply=%region_17.18 | all-reduce | flops 1 | bytes 8 | tf_op jit(solution)/shard_map/psum | solution.py:299
  186.4 12.7 all-gather.2
  199.5 40.2 %all-gather.6 = bf16[32,32,16]{1,2,0:T(8,128)(2,1)S(1)} all-gather(bf16[1,32,16]{1,2,0:T(8,128)(2,1)S(1)} %bitcast.480), channel_id=1, replica_groups=mesh['head'=4,'seq'=8] {'head','seq'}, dimensions={0}, use_global_device_ids=true | all-gather | bytes 33792 | tf_op jit(solution)/shard_map/all_gather | solution.py:137
  240.0 37.8 %all-gather.5 = bf16[32,32,16]{1,2,0:T(8,128)(2,1)S(1)} all-gather(bf16[1,32,16]{1,2,0:T(8,128)(2,1)S(1)} %bitcast.481), channel_id=1, replica_groups=mesh['head'=4,'seq'=8] {'head','seq'}, dimensions={0}, use_global_device_ids=true | all-gather | bytes 33792 | tf_op jit(solution)/shard_map/all_gather | solution.py:136
  278.2 39.4 %all-reduce = bf16[1024]{0:T(1024)(128)(2,1)S(1)} all-reduce(bf16[1024]{0:T(1024)(128)(2,1)S(1)} %dynamic-update-slice), channel_id=1, replica_groups=mesh['head'=4,'seq'=8] {'head','seq'}, use_global_device_ids=true, to_apply=%add | all-reduce | flops 1024 | bytes 4096
  325.6 7.6 all-to-all-done
  334.8 10.3 conditional.3
  351.2 5.6 all-to-all-done.3
  358.8 40.6 %all-gather.20.cloned.1.call-done = bf16[1024,1024]{1,0:T(8,128)(2,1)} async-done(((bf16[32,1024]{1,0:T(8,128)(2,1)}), bf16[1024,1024]{1,0:T(8,128)(2,1)}) %all-gather.20.cloned.1.call-update) | async-done | bytes 2097168 | tf_op jit(solution)/shard_map/all_gather | solution.py:135
  402.4 66.0 %all-gather.30.cloned.1.call-done = bf16[1024,2816]{1,0:T(8,128)(2,1)} async-done(((bf16[32,2816]{1,0:T(8,128)(2,1)}), bf16[1024,2816]{1,0:T(8,128)(2,1)}) %all-gather.30.cloned.1.call-update) | async-done | bytes 5767184 | tf_op jit(solution)/shard_map/all_gather | solution.py:139
  473.1 64.4 %all-gather.32.cloned.1.call-done = bf16[1024,2816]{1,0:T(8,128)(2,1)} async-done(((bf16[32,2816]{1,0:T(8,128)(2,1)}), bf16[1024,2816]{1,0:T(8,128)(2,1)}) %all-gather.32.cloned.1.call-update) | async-done | bytes 5767184 | tf_op jit(solution)/shard_map/all_gather | solution.py:140
  537.5 5.3 multiply_convert_fusion.2
  542.8 63.8 %all-gather.34.cloned.1.call-done = bf16[2816,1024]{1,0:T(8,128)(2,1)} async-done(((bf16[88,1024]{1,0:T(8,128)(2,1)}), bf16[2816,1024]{1,0:T(8,128)(2,1)}) %all-gather.34.cloned.1.call-update) | async-done | bytes 5767184 | tf_op jit(solution)/shard_map/all_gather | solution.py:141
  610.5 6.2 multiply_convert_fusion
  629.2 4.9 all-to-all-done.4
  646.4 5.4 copy.356
  652.4 11.7 conditional.4
  658.1 5.8 fusion.9
  665.2 8.1 all_to_all.134
  676.0 5.4 copy.350
  681.8 8.6 while.49
  692.0 137.1 %while.50 = (s32[]{:T(128)}, bf16[4,128,2,128]{3,1,2,0:T(8,128)(2,1)S(1)}, bf16[4,128,2,128]{3,1,2,0:T(8,128)(2,1)S(1)}, f32[4,128,2,128]{3,1,2,0:T(8,128)S(1)},...) while((s32[]{:T(128)}, ...), condition=%wide.region_27.28_spmd.clone, body=%wide.region_23.27_spmd.clone.sunk | while | flops 136471824 | bytes 15915234 | solution.py:431
  722.3 5.7 collective-permute-start.2
  739.9 7.2 collective-permute-start.2
  757.7 6.2 collective-permute-start.2
  768.4 5.0 collective-permute-start.1
  793.3 5.7 collective-permute-start.2
  818.2 5.3 collective-permute-start
  830.5 8.1 all_to_all.135
  841.5 5.4 copy.352
  849.6 8.4 all_to_all.136
  860.7 5.3 copy.354
  867.3 5.9 fusion.108
  874.3 5.9 fusion.109
  881.3 5.9 fusion.110
  888.6 47.5 %all-reduce.2 = (f32[]{:T(128)}, f32[1024]{0:T(1024)S(1)}) all-reduce(f32[]{:T(128)} %multiply_reduce_fusion.5, f32[1024]{0:T(1024)S(1)} %copy-done.42), channel_id=1, replica_groups=mesh['head'=4,'seq'=8] {'head','seq'}, use_global_device_ids=true, to_apply=%region_15.16 | all-reduce | flops 1025 | bytes 8200 | tf_op jit(solution)/shard_map/psum | solution.py:299
  949.3 126.7 %reduce-scatter.23.cloned.1.call-done = f32[32,1024]{1,0:T(8,128)} async-done(((f32[1024,1024]{1,0:T(8,128)}), f32[32,1024]{1,0:T(8,128)}) %reduce-scatter.23.cloned.1.call-update) | async-done | bytes 131088 | tf_op jit(solution)/shard_map/reduce_scatter | solution.py:493
  1075.9 142.0 %reduce-scatter.37.cloned.1.call-done = f32[32,1024]{1,0:T(8,128)} async-done(((f32[1024,1024]{1,0:T(8,128)}), f32[32,1024]{1,0:T(8,128)}) %reduce-scatter.37.cloned.1.call-update) | async-done | bytes 131088
  1217.9 142.8 %reduce-scatter.31.cloned.1.call-done = f32[32,1024]{1,0:T(8,128)} async-done(((f32[1024,1024]{1,0:T(8,128)}), f32[32,1024]{1,0:T(8,128)}) %reduce-scatter.31.cloned.1.call-update) | async-done | bytes 131088
  1360.7 141.9 %reduce-scatter.33.cloned.1.call-done = f32[32,1024]{1,0:T(8,128)} async-done(((f32[1024,1024]{1,0:T(8,128)}), f32[32,1024]{1,0:T(8,128)}) %reduce-scatter.33.cloned.1.call-update) | async-done | bytes 131088
  1502.6 142.3 %reduce-scatter.35.cloned.1.call-done = f32[32,1024]{1,0:T(8,128)} async-done(((f32[1024,1024]{1,0:T(8,128)}), f32[32,1024]{1,0:T(8,128)}) %reduce-scatter.35.cloned.1.call-update) | async-done | bytes 131088
  1645.0 160.2 %reduce-scatter.25.cloned.1.call-done = f32[32,2816]{1,0:T(8,128)} async-done(((f32[1024,2816]{1,0:T(8,128)}), f32[32,2816]{1,0:T(8,128)}) %reduce-scatter.25.cloned.1.call-update) | async-done | bytes 360464 | tf_op jit(solution)/shard_map/reduce_scatter | solution.py:502
  1805.2 161.1 %reduce-scatter.27.cloned.1.call-done = f32[32,2816]{1,0:T(8,128)} async-done(((f32[1024,2816]{1,0:T(8,128)}), f32[32,2816]{1,0:T(8,128)}) %reduce-scatter.27.cloned.1.call-update) | async-done | bytes 360464 | tf_op jit(solution)/shard_map/reduce_scatter | solution.py:503
  1966.2 161.5 %reduce-scatter.29.cloned.1.call-done = f32[88,1024]{1,0:T(8,128)} async-done(((f32[2816,1024]{1,0:T(8,128)}), f32[88,1024]{1,0:T(8,128)}) %reduce-scatter.29.cloned.1.call-update) | async-done | bytes 360464 | tf_op jit(solution)/shard_map/reduce_scatter | solution.py:504
  (471 shorter events, 228.6 us)
Async XLA Ops:
  7.2 63.0 %all-gather.24.cloned.1.call-start = ((), (), s32[]{:S(2)}) async-start(), calls=%async_computation.20 | async-start | bytes 2162688 | tf_op jit(solution)/shard_map/all_gather | solution.py:132
  7.9 120.6 %all-gather.26.cloned.1.call-start = ((), (), s32[]{:S(2)}) async-start(), calls=%async_computation.21 | async-start | bytes 2162688 | tf_op jit(solution)/shard_map/all_gather | solution.py:133
  8.7 309.8 %all-gather.22.cloned.1.call-start = ((), (), s32[]{:S(2)}) async-start(), calls=%async_computation.19 | async-start | bytes 2162688 | tf_op jit(solution)/shard_map/all_gather | solution.py:131
  9.4 325.3 %all-gather.36.cloned.1.call-start = ((), (), s32[]{:S(2)}) async-start(), calls=%async_computation.30 | async-start | bytes 2359296 | tf_op jit(solution)/shard_map/all_gather | solution.py:214
  82.0 252.8 %all-gather.38.cloned.1.call-start = ((), (), s32[]{:S(2)}) async-start(), calls=%async_computation.31 | async-start | bytes 2359296 | tf_op jit(solution)/shard_map/all_gather | solution.py:215
  140.5 204.7 %all-gather.40.cloned.1.call-start = ((), (), s32[]{:S(2)}) async-start(), calls=%async_computation.32 | async-start | bytes 2359296 | tf_op jit(solution)/shard_map/all_gather | solution.py:21
  143.6 207.6 %all-gather.28.cloned.1.call-start = ((), (), s32[]{:S(2)}) async-start(), calls=%async_computation.22 | async-start | bytes 2162688 | tf_op jit(solution)/shard_map/all_gather | solution.py:134
  144.3 255.1 %all-gather.20.cloned.1.call-start = ((), (), s32[]{:S(2)}) async-start(), calls=%async_computation.18 | async-start | bytes 2162688 | tf_op jit(solution)/shard_map/all_gather | solution.py:135
  145.1 323.4 %all-gather.30.cloned.1.call-start = ((), (), s32[]{:S(2)}) async-start(), calls=%async_computation.23 | async-start | bytes 5947392 | tf_op jit(solution)/shard_map/all_gather | solution.py:139
  145.8 391.7 %all-gather.32.cloned.1.call-start = ((), (), s32[]{:S(2)}) async-start(), calls=%async_computation.24 | async-start | bytes 5947392 | tf_op jit(solution)/shard_map/all_gather | solution.py:140
  146.4 460.3 %all-gather.34.cloned.1.call-start = ((), (), s32[]{:S(2)}) async-start(), calls=%async_computation.25 | async-start | bytes 5947392 | tf_op jit(solution)/shard_map/all_gather | solution.py:141
  321.3 11.8 all-to-all-start
  347.3 9.4 all-to-all-start.3
  624.7 9.4 all-to-all-start.4
  628.1 53.6 %all-gather.42.cloned.1.call-start = ((), (), s32[]{:S(2)}) async-start(), calls=%async_computation.33 | async-start | bytes 2359296 | tf_op jit(solution)/shard_map/all_gather | solution.py:21
  635.7 304.9 %reduce-scatter.39.cloned.1.call-start = ((), (), s32[]{:S(2)}) async-start(), calls=%async_computation.38 | async-start | bytes 540672
  637.5 304.6 %reduce-scatter.41.cloned.1.call-start = ((), (), s32[]{:S(2)}) async-start(), calls=%async_computation.39 | async-start | bytes 540672
  638.7 437.3 %reduce-scatter.23.cloned.1.call-start = ((), (), s32[]{:S(2)}) async-start(), calls=%async_computation.26 | async-start | bytes 4325376 | tf_op jit(solution)/shard_map/reduce_scatter | solution.py:493
  641.4 576.5 %reduce-scatter.37.cloned.1.call-start = ((), (), s32[]{:S(2)}) async-start(), calls=%async_computation.37 | async-start | bytes 4325376
  651.8 708.9 %reduce-scatter.31.cloned.1.call-start = ((), (), s32[]{:S(2)}) async-start(), calls=%async_computation.34 | async-start | bytes 4325376
  681.5 821.2 %reduce-scatter.33.cloned.1.call-start = ((), (), s32[]{:S(2)}) async-start(), calls=%async_computation.35 | async-start | bytes 4325376
  695.2 7.8 collective-permute-start.2
  695.3 10.7 collective-permute-start.3
  695.4 11.5 collective-permute-start
  696.9 9.9 collective-permute-start.1
  708.8 9.2 collective-permute-start.2
  711.5 8.0 collective-permute-start.3
  714.1 6.3 collective-permute-start
  722.3 14.5 collective-permute-start.2
  728.1 8.8 collective-permute-start.3
  739.9 14.5 collective-permute-start.2
  747.1 7.8 collective-permute-start.3
  757.7 15.7 collective-permute-start.2
  763.9 9.5 collective-permute-start.3
  766.5 7.8 collective-permute-start
  776.5 13.7 collective-permute-start.2
  780.8 9.5 collective-permute-start.3
  783.3 7.7 collective-permute-start
  793.3 15.7 collective-permute-start.2
  799.0 10.0 collective-permute-start.3
  801.5 8.3 collective-permute-start
  812.0 15.9 collective-permute-start.2
  815.6 12.4 collective-permute-start.3
  818.2 10.6 collective-permute-start
  846.9 798.0 %reduce-scatter.35.cloned.1.call-start = ((), (), s32[]{:S(2)}) async-start(), calls=%async_computation.36 | async-start | bytes 4325376
  866.1 939.0 %reduce-scatter.25.cloned.1.call-start = ((), (), s32[]{:S(2)}) async-start(), calls=%async_computation.27 | async-start | bytes 11894784 | tf_op jit(solution)/shard_map/reduce_scatter | solution.py:502
  873.2 1093.0 %reduce-scatter.27.cloned.1.call-start = ((), (), s32[]{:S(2)}) async-start(), calls=%async_computation.28 | async-start | bytes 11894784 | tf_op jit(solution)/shard_map/reduce_scatter | solution.py:503
  880.2 1247.5 %reduce-scatter.29.cloned.1.call-start = ((), (), s32[]{:S(2)}) async-start(), calls=%async_computation.29 | async-start | bytes 11894784 | tf_op jit(solution)/shard_map/reduce_scatter | solution.py:504
  (71 other events, 2038.3 us)
Sparse Core Ops, SparseCore 0:
  11.0 59.1 all-gather.23
  73.2 55.3 all-gather.25
  131.5 55.4 all-gather.21
  188.5 28.5 all-gather.35
  219.2 30.8 all-gather.37
  252.1 28.6 all-gather.39
  283.8 57.2 all-gather.27
  344.0 55.3 all-gather.19
  402.3 66.1 all-gather.29
  471.1 66.2 all-gather.31
  540.3 66.2 all-gather.33
  635.8 27.8 all-gather.41
  666.0 135.1 reduce-scatter.38
  803.4 130.4 reduce-scatter.40
  936.6 139.3 reduce-scatter.22
  1078.6 139.2 reduce-scatter.36
  1220.6 140.0 reduce-scatter.30
  1363.4 139.1 reduce-scatter.32
  1505.5 139.4 reduce-scatter.34
  1647.7 157.3 reduce-scatter.24
  1808.0 158.1 reduce-scatter.26
  1969.1 158.5 reduce-scatter.28
where the time goes:
time: 2140 us
  waiting for transfers between devices  1550 us (72%)
  blocking collectives  259 us (12%)
  starting transfers between devices  115 us (5%)
  matrix products  106 us (5%)
  local copies, waits for them, and re-layouts  49.3 us (2%)
  other arithmetic  31.8 us (1%)
    unnamed x28, waiting for transfers between devices  575 us
    reduce_scatter x1, waiting for transfers between devices, local(): lax.psum_scatter(grad_down, ('head', 'seq'), scatter_dimension=0, tiled=T...  161 us
    reduce_scatter x1, waiting for transfers between devices, local(): lax.psum_scatter(grad_ffn_up, ('head', 'seq'), scatter_dimension=0, tiled...  161 us
    reduce_scatter x1, waiting for transfers between devices, local(): lax.psum_scatter(grad_ffn_gate, ('head', 'seq'), scatter_dimension=0, til...  160 us
    reduce_scatter x1, waiting for transfers between devices, local(): lax.psum_scatter(grad_out_weight, ('head', 'seq'), scatter_dimension=0, t...  127 us
    psum x2, blocking collectives, local(): lax.psum((jnp.sum(valid_rows * jnp.sum(error * error, axis=-1)), jnp.sum(...  86.1 us
    all_gather x1, waiting for transfers between devices, local(): lax.all_gather(ff_gate, ('head', 'seq'), axis=0, tiled=True)  66 us
    all_gather x1, waiting for transfers between devices, local(): lax.all_gather(ff_up, ('head', 'seq'), axis=0, tiled=True)  64.4 us
  transfers between devices with their start and end apart: 57, of which 26 were waited for; matrix products, arithmetic and copies ran while one was open for 7% of the time, Pallas kernels for 0%

commit v1 on v0

--- a/solution.py
+++ b/solution.py
@@ -1,6 +1,11 @@
+import functools
+import types
+
 import jax
 import jax.numpy as jnp
 from jax import lax
+from jax.experimental import pallas as pl
+from jax.experimental.pallas import tpu as pltpu
 from jax.sharding import PartitionSpec as P
 
 HEAD_COUNT = 8
@@ -11,6 +16,931 @@
 HIGHEST = lax.Precision.HIGHEST
 MASKED = -1e30
 EPSILON = 1e-06
+F32 = jnp.float32
+BF16 = jnp.bfloat16
+MESH_IDS = pl.DeviceIdType.MESH
+
+
+def nn(left, right):
+    return lax.dot_general(left, right, (((1,), (0,)), ((), ())), preferred_element_type=F32)
+
+
+def nt(left, right):
+    return lax.dot_general(left, right, (((1,), (1,)), ((), ())), preferred_element_type=F32)
+
+
+def tn(left, right):
+    return lax.dot_general(left, right, (((0,), (0,)), ((), ())), preferred_element_type=F32)
+
+
+def tn_exact(left, right):
+    return lax.dot_general(
+        left, right, (((0,), (0,)), ((), ())), precision=HIGHEST, preferred_element_type=F32
+    )
+
+
+def nt_exact(left, right):
+    return lax.dot_general(
+        left, right, (((1,), (1,)), ((), ())), precision=HIGHEST, preferred_element_type=F32
+    )
+
+
+def nn_exact(left, right):
+    return lax.dot_general(
+        left, right, (((1,), (0,)), ((), ())), precision=HIGHEST, preferred_element_type=F32
+    )
+
+
+def block_rows(index, size):
+    return pl.ds(pl.multiple_of(index * size, size), size)
+
+
+def each(first, last, body):
+    def step(index, carry):
+        body(index)
+        return carry
+
+    lax.fori_loop(first, last, step, 0)
+
+
+SEQ_FLAGS = dict(
+    w1=8, t2=8, p2=8, x=8, wo=8, fgu=8, fd=8, gp=8, mx=8, dm=8, dg=8, rgu=8, rgd=8, rgo=8, gt=8,
+    gwa=8, fin2=8,
+)
+XY_FLAGS = dict(t1=4, p1=4, w2=4, fx=4, wox=4, sc=4, y=4, df=4, ds=4, gwo=4, gw=4, gfx=4, fin1=4)
+FLAGS = SEQ_FLAGS | XY_FLAGS
+
+
+def scratch_table(width, tokens, hidden, hidden_pad, length):
+    seqs, blocks, block = 4, 8, 128
+    table = dict(
+        x_all=((length, width), BF16),
+        wcs=((blocks, 32, 512), BF16),
+        wqk=((width, 512), BF16),
+        t1=((4, 8, 128), F32),
+        p1=((4, 32, 128), BF16),
+        t2s=((16, 128), F32),
+        t2=((8, 16, 128), F32),
+        p2=((8, 32, 128), BF16),
+        fs=((4, 2, 32, hidden_pad), BF16),
+        fgu=((2, 4, 256, hidden_pad), BF16),
+        fdp=((8, 96, width), BF16),
+        ffd=((hidden_pad, width), BF16),
+        wo_all=((width, width), BF16),
+        q=((length, HD), BF16),
+        k=((length, HD), BF16),
+        v=((length, HD), BF16),
+        gps=((length, HD), BF16),
+        fkv=((32, HD), BF16),
+        gain=((1, width), F32),
+        rrow=((1, length), F32),
+        rcol=((block, 8), F32),
+        probs=((length, length), BF16),
+        decay=((length, length), BF16),
+        both=((length, length), BF16),
+        fprobs=((length, P_SIZE), BF16),
+        mxs=((length, HD), BF16),
+        mx=((block, width), BF16),
+        gp=((block, width), BF16),
+        hid=((block, width), F32),
+        br=((block, width), F32),
+        inv=((block, 128), F32),
+        own=((block, width), F32),
+        dout=((block, width), F32),
+        sc=((4 * block, width), BF16),
+        gact=((4 * block, hidden_pad), F32),
+        uact=((4 * block, hidden_pad), F32),
+        inner=((4 * block, hidden_pad), BF16),
+        ysend=((4, block, width), BF16),
+        yrecv=((4, block, width), BF16),
+        df=((4 * block, width), BF16),
+        dga=((4 * block, hidden_pad), BF16),
+        dua=((4 * block, hidden_pad), BF16),
+        dbr=((block, width), BF16),
+        dgt=((block, width), BF16),
+        dms=((block, width), BF16),
+        dm=((length, HD), BF16),
+        dq=((length, 512), BF16),
+        ggain=((1, width), F32),
+        gus=((4, 2, 2, 4, 32, hidden_pad), BF16),
+        gur=((4, 2, 4, 32, hidden_pad), BF16),
+        guz=((4, 2, 4, 32, hidden_pad), BF16),
+        gux=((4, 2, 32, hidden_pad), BF16),
+        guxr=((4, 2, 32, hidden_pad), BF16),
+        gds=((4, 2, 96, width), BF16),
+        gdr=((4, 96, width), BF16),
+        gdz=((4, 96, width), BF16),
+        gwos=((4, 256, width), BF16),
+        gwor=((4, 256, width), BF16),
+        gos=((4, 2, 32, width), BF16),
+        gor=((4, 32, width), BF16),
+        goz=((4, 32, width), BF16),
+        gws=((4, 256, 512), BF16),
+        gwr=((4, 256, 512), BF16),
+        gas=((8, 32, 512), BF16),
+        gar=((8, 32, 512), BF16),
+        gts=((4, 2, block, width), BF16),
+        gtr=((4, block, width), BF16),
+        pgrad=((32, HD), F32),
+        fin0=((48, 128), F32),
+        fin1=((4, 48, 128), F32),
+        fin2s=((48, 128), F32),
+        fin2=((8, 48, 128), F32),
+    )
+    return table
+
+
+def block_kernel(names, width, hidden, ndoc, *refs):
+    (
+        tok, wq, wk, wv, wo, wg, fgi, fui, fdi, tea, tile, pin, vcol, docs,
+        out_o, gtok_o, gq_o, gk_o, gv_o, gwo_o, gwg_o, fin_o, pers_o, fg_o, fu_o, fd_o,
+    ) = refs[:26]
+    m = types.SimpleNamespace(**dict(zip(names, refs[26 : 26 + len(names)])))
+    sems = refs[26 + len(names) :]
+    s = types.SimpleNamespace(**dict(zip(FLAGS, zip(sems[0::2], sems[1::2]))))
+    pad = m.ffd.shape[0]
+    length = m.x_all.shape[0]
+    scale = HD ** (-0.5)
+    mem_scale = 0.125 / HD
+
+    a = lax.axis_index("head")
+    b = lax.axis_index("seq")
+    z = lax.div(b, 2)
+    c = lax.rem(b, 2)
+    sib = 2 * z + 1 - c
+
+    def copy(src, dst, ssem, rsem, device):
+        return pltpu.make_async_remote_copy(
+            src_ref=src, dst_ref=dst, send_sem=ssem, recv_sem=rsem,
+            device_id=device, device_id_type=MESH_IDS,
+        )
+
+    def seq_peers(body):
+        each(1, 8, lambda step: body(lax.rem(b + step, 8)))
+
+    def xy_peers(body):
+        each(1, 4, lambda step: body(lax.rem(a + step, 4)))
+
+    def z_peers(body):
+        each(1, 4, lambda step: body(lax.rem(z + step, 4)))
+
+    def seq_copy(pair, src, dst, peer, slot=None):
+        slot = peer if slot is None else slot
+        return copy(src, dst, pair[0].at[peer], pair[1].at[slot], (a, peer))
+
+    def seq_start(pair, src, dst, peer):
+        seq_copy(pair, src, dst, peer, b).start()
+
+    def seq_wait(pair, dst, peer):
+        seq_copy(pair, dst, dst, peer).wait_recv()
+
+    def xy_copy(pair, src, dst, peer, slot=None):
+        slot = peer if slot is None else slot
+        return copy(src, dst, pair[0].at[peer], pair[1].at[slot], (peer, b))
+
+    def xy_start(pair, src, dst, peer):
+        xy_copy(pair, src, dst, peer, a).start()
+
+    def xy_wait(pair, dst, peer):
+        xy_copy(pair, dst, dst, peer).wait_recv()
+
+    finals = []
+
+    def seq_drain(pair, view):
+        finals.append(lambda: seq_peers(lambda p: seq_copy(pair, view, view, p).wait_send()))
+
+    def xy_drain(pair, view):
+        finals.append(lambda: xy_peers(lambda p: xy_copy(pair, view, view, p).wait_send()))
+
+    def line_copy(pair, src, dst, zt):
+        return copy(src, dst, pair[0].at[zt], pair[1].at[z], (a, 2 * zt + c))
+
+    def pass_copy(pair, src, dst, zs):
+        return copy(src, dst, pair[0].at[4 + zs], pair[1].at[4 + zs], (a, sib))
+
+    def gather_start(pair, src, view):
+        z_peers(lambda zt: line_copy(pair, src, view(b), zt).start())
+        pass_copy(pair, src, view(b), z).start()
+        finals.append(lambda: z_peers(lambda zt: line_copy(pair, src, src, zt).wait_send()))
+        finals.append(lambda: each(0, 4, lambda zs: pass_copy(pair, src, src, zs).wait_send()))
+
+    def gather_line(pair, view, zs):
+        block = view(2 * zs + c)
+        copy(block, block, pair[0].at[zs], pair[1].at[zs], (a, 2 * zs + c)).wait_recv()
+        pass_copy(pair, block, block, zs).start()
+
+    def gather_pass(pair, view, zs):
+        block = view(2 * zs + 1 - c)
+        pass_copy(pair, block, block, zs).wait_recv()
+
+    barrier = pltpu.get_barrier_semaphore()
+    seq_peers(lambda p: pl.semaphore_signal(barrier, 1, device_id=(a, p), device_id_type=MESH_IDS))
+    xy_peers(lambda p: pl.semaphore_signal(barrier, 1, device_id=(p, b), device_id_type=MESH_IDS))
+
+    for head in range(8):
+        for place, weight in enumerate((wq, wk, wv, wg)):
+            m.wcs[head, :, place * 128 : place * 128 + 128] = weight[
+                :, head * 128 : head * 128 + 128
+            ]
+    for part in range(4):
+        for place, weight in enumerate((fgi, fui)):
+            m.fs[part, place, :, 0:hidden] = weight[:, part * hidden : (part + 1) * hidden]
+            m.fs[part, place, :, hidden:pad] = jnp.zeros((32, pad - hidden), BF16)
+    own_rows = block_rows(b, 128)
+    piece = pl.ds(pl.multiple_of(a * 256 + b * 32, 32), 32)
+    m.x_all[own_rows, :] = tok[...]
+    m.wqk[piece, :] = m.wcs[b]
+    m.wo_all[piece, :] = wo[...]
+    m.fdp[b] = fdi[...]
+    slot32 = block_rows(b, 32)
+    m.fgu[:, a, slot32, :] = m.fs[a]
+    m.t1[a] = tile[a]
+    m.p1[a] = pin[...]
+    pl.semaphore_wait(barrier, 10)
+
+    xy_peers(lambda p: xy_start(s.t1, tile.at[p], m.t1.at[a], p))
+    xy_peers(lambda p: xy_start(s.p1, pin, m.p1.at[a], p))
+    seq_peers(lambda p: seq_start(s.w1, m.wcs.at[p], m.wqk.at[piece, :], p))
+    x_view = lambda i: m.x_all.at[block_rows(i, 128), :]
+    gather_start(s.x, tok, x_view)
+    xy_peers(lambda p: xy_start(s.fx, m.fs.at[p], m.fgu.at[:, a, slot32, :], p))
+    xy_drain(s.t1, tile.at[0])
+    xy_drain(s.p1, pin)
+    seq_drain(s.w1, m.wcs.at[0])
+    xy_drain(s.fx, m.fs.at[0])
+
+    xy_peers(lambda p: xy_wait(s.t1, m.t1.at[p], p))
+    xy_peers(lambda p: xy_wait(s.p1, m.p1.at[p], p))
+    for group in range(4):
+        m.t2s[2 * group : 2 * group + 2, :] = m.t1[group, 0:2, :]
+        m.t2s[8 + group : 9 + group, :] = m.t1[group, 3:4, :]
+    m.t2s[12:13, :] = (m.t1[0, 2:3, :] + m.t1[1, 2:3, :]) + (m.t1[2, 2:3, :] + m.t1[3, 2:3, :])
+    m.t2s[13:16, :] = jnp.zeros((3, 128), F32)
+    m.t2[b] = m.t2s[...]
+    m.p2[b] = m.p1[lax.div(b, 2)]
+    seq_peers(lambda p: seq_start(s.t2, m.t2s, m.t2.at[b], p))
+    seq_peers(lambda p: seq_start(s.p2, m.p1.at[lax.div(p, 2)], m.p2.at[b], p))
+    seq_drain(s.t2, m.t2s)
+    seq_drain(s.p2, m.p1.at[0])
+
+    seq_peers(lambda p: seq_wait(s.w1, m.wqk.at[pl.ds(pl.multiple_of(a * 256 + p * 32, 32), 32), :], p))
+    quarter = lambda i: m.wqk.at[block_rows(i, 256), :]
+    xy_peers(lambda p: xy_start(s.w2, quarter(a), quarter(a), p))
+    xy_drain(s.w2, quarter(a))
+
+    def project(i):
+        rows = block_rows(i, 128)
+        wide = nn(m.x_all[rows, :], m.wqk[...])
+        m.q[rows, :] = wide[:, 0:128].astype(BF16)
+        m.k[rows, :] = wide[:, 128:256].astype(BF16)
+        m.v[rows, :] = wide[:, 256:384].astype(BF16)
+        m.gps[rows, :] = wide[:, 384:512].astype(BF16)
+
+    head_cols = pl.ds(pl.multiple_of(b * 128, 128), 128)
+
+    def send_gate(i):
+        seq_start(s.gp, m.gps.at[block_rows(i, 128), :], m.gp.at[:, head_cols], i)
+
+    xy_peers(lambda p: xy_wait(s.w2, quarter(p), p))
+    project(b)
+    m.gp[:, head_cols] = m.gps[own_rows, :]
+    gather_pass(s.x, x_view, z)
+    project(sib)
+    send_gate(sib)
+
+    def arrived_line(step):
+        zs = lax.rem(z + step, 4)
+        gather_line(s.x, x_view, zs)
+        project(2 * zs + c)
+        send_gate(2 * zs + c)
+
+    each(1, 4, arrived_line)
+
+    def arrived_pass(step):
+        zs = lax.rem(z + step, 4)
+        gather_pass(s.x, x_view, zs)
+        project(2 * zs + 1 - c)
+        send_gate(2 * zs + 1 - c)
+
+    wo_view = lambda i: m.wo_all.at[pl.ds(pl.multiple_of(a * 256 + i * 32, 32), 32), :]
+    gather_start(s.wo, wo, wo_view)
+    xy_peers(lambda p: xy_wait(s.fx, m.fgu.at[:, p, slot32, :], p))
+    fgu_view = lambda i: m.fgu.at[:, :, block_rows(i, 32), :]
+    fd_view = lambda i: m.fdp.at[i]
+    gather_start(s.fgu, fgu_view(b), fgu_view)
+    gather_start(s.fd, fdi, fd_view)
+    each(1, 4, arrived_pass)
+    seq_drain(s.gp, m.gps.at[own_rows, :])
+
+    seq_peers(lambda p: seq_wait(s.t2, m.t2.at[p], p))
+    seq_peers(lambda p: seq_wait(s.p2, m.p2.at[p], p))
+    small = m.t2[...]
+    place16 = lax.broadcasted_iota(jnp.int32, (8, 16, 128), 1)
+    rates = jnp.sum(jnp.where(place16 == b, small, 0.0), axis=1)
+    valid_total = jnp.sum(jnp.where(place16 == 12, small, 0.0))
+    for group in range(8):
+        line = 8 + group // 2
+        first = 4 * (group % 2)
+        m.gain[:, group * 128 : group * 128 + 128] = (
+            m.t2[first, line : line + 1, :] + m.t2[first + 1, line : line + 1, :]
+        ) + (m.t2[first + 2, line : line + 1, :] + m.t2[first + 3, line : line + 1, :])
+    half = 4 * lax.rem(b, 2)
+    m.fkv[...] = (
+        (m.p2[half].astype(F32) + m.p2[half + 1].astype(F32))
+        + (m.p2[half + 2].astype(F32) + m.p2[half + 3].astype(F32))
+    ).astype(BF16)
+    row_id = lax.broadcasted_iota(jnp.int32, (128, 128), 0)
+    col_id = lax.broadcasted_iota(jnp.int32, (128, 128), 1)
+    lower = (col_id <= row_id).astype(F32)
+    within = nt_exact(rates, lower)
+    earlier = (
+        lax.broadcasted_iota(jnp.int32, (8, 8), 1) < lax.broadcasted_iota(jnp.int32, (8, 8), 0)
+    ).astype(F32)
+    base = nn_exact(earlier, jnp.broadcast_to(jnp.sum(rates, axis=1, keepdims=True), (8, 128)))
+    running = within + base
+    for i in range(8):
+        m.rrow[:, i * 128 : i * 128 + 128] = running[i : i + 1, :]
+    eye = (col_id == row_id).astype(F32)
+    m.rcol[...] = nt_exact(eye, running)
+
+    key_pos = lax.broadcasted_iota(jnp.int32, (128, length), 1)
+    local_pos = lax.broadcasted_iota(jnp.int32, (128, 1), 0)
+    lane8 = lax.broadcasted_iota(jnp.int32, (128, 8), 1)
+
+    def attend(i):
+        rows = block_rows(i, 128)
+        query = m.q[rows, :]
+        raw = nt(query, m.k[...])
+        pos = i * 128 + local_pos
+        begin = jnp.zeros_like(pos)
+        for j in range(ndoc):
+            start = docs[a, j]
+            begin = jnp.where(start <= pos, jnp.maximum(begin, start), begin)
+        allowed = (key_pos <= pos) & (key_pos >= begin)
+        scores = jnp.where(allowed, raw * scale, MASKED)
+        fixed = nt(query, m.fkv[0:16, :]) * scale
+        top = jnp.maximum(
+            jnp.max(scores, axis=1, keepdims=True), jnp.max(fixed, axis=1, keepdims=True)
+        )
+        weight = jnp.exp(scores - top)
+        fixed_weight = jnp.exp(fixed - top)
+        share = 1.0 / (
+            jnp.sum(weight, axis=1, keepdims=True) + jnp.sum(fixed_weight, axis=1, keepdims=True)
+        )
+        prob = weight * share
+        fixed_prob = (fixed_weight * share).astype(BF16)
+        reach = jnp.sum(jnp.where(lane8 == i, m.rcol[...], 0.0), axis=1, keepdims=True)
+        kept = jnp.where(
+            allowed, jnp.exp(jnp.minimum(reach - m.rrow[...], 0.0)) * mem_scale, 0.0
+        )
+        joint = (prob + kept * raw).astype(BF16)
+        m.probs[rows, :] = prob.astype(BF16)
+        m.decay[rows, :] = kept.astype(BF16)
+        m.both[rows, :] = joint
+        m.fprobs[rows, :] = fixed_prob
+        mixed = nn(joint, m.v[...]) + nn(fixed_prob, m.fkv[16:32, :])
+        m.mxs[rows, :] = mixed.astype(BF16)
+
+    def attend_send(step):
+        i = lax.rem(b + step, 8)
+        attend(i)
+        seq_start(s.mx, m.mxs.at[block_rows(i, 128), :], m.mx.at[:, head_cols], i)
+
+    each(1, 4, attend_send)
+    z_peers(lambda zs: gather_line(s.wo, wo_view, zs))
+    each(4, 6, attend_send)
+    each(0, 4, lambda zs: gather_pass(s.wo, wo_view, zs))
+    wo_quarter = lambda i: m.wo_all.at[block_rows(i, 256), :]
+    xy_peers(lambda p: xy_start(s.wox, wo_quarter(a), wo_quarter(a), p))
+    xy_drain(s.wox, wo_quarter(a))
+    each(6, 8, attend_send)
+    seq_drain(s.mx, m.mxs.at[own_rows, :])
+    attend(b)
+    m.mx[:, head_cols] = m.mxs[own_rows, :]
+
+    seq_peers(lambda p: seq_wait(s.gp, m.gp.at[:, pl.ds(pl.multiple_of(p * 128, 128), 128)], p))
+    xy_peers(lambda p: xy_wait(s.wox, wo_quarter(p), p))
+    seq_peers(lambda p: seq_wait(s.mx, m.mx.at[:, pl.ds(pl.multiple_of(p * 128, 128), 128)], p))
+
+    m.br[...] = nn(m.mx[...], m.wo_all[...])
+
+    def normalise(i):
+        rows = block_rows(i, 32)
+        opened = jax.nn.sigmoid(m.gp[rows, :].astype(F32))
+        hidden_rows = tok[rows, :].astype(F32) + opened * m.br[rows, :]
+        inv = lax.rsqrt(jnp.mean(hidden_rows * hidden_rows, axis=1, keepdims=True) + EPSILON)
+        m.hid[rows, :] = hidden_rows
+        m.inv[rows, :] = jnp.broadcast_to(inv, (32, 128))
+        m.sc[pl.ds(pl.multiple_of(a * 128 + i * 32, 32), 32), :] = (
+            hidden_rows * inv * m.gain[...]
+        ).astype(BF16)
+
+    each(0, 4, normalise)
+    quad = lambda ref, i: ref.at[block_rows(i, 128), :]
+    xy_peers(lambda p: xy_start(s.sc, quad(m.sc, a), quad(m.sc, a), p))
+    xy_drain(s.sc, quad(m.sc, a))
+
+    z_peers(lambda zs: gather_line(s.fgu, fgu_view, zs))
+    z_peers(lambda zs: gather_line(s.fd, fd_view, zs))
+    each(0, 4, lambda zs: gather_pass(s.fgu, fgu_view, zs))
+    xy_peers(lambda p: xy_wait(s.sc, quad(m.sc, p), p))
+
+    gate_w = lambda: m.fgu[0].reshape(width, pad)
+    up_w = lambda: m.fgu[1].reshape(width, pad)
+
+    def feed(i):
+        rows = block_rows(i, 256)
+        scaled = m.sc[rows, :]
+        gate_act = nn(scaled, gate_w())
+        up_act = nn(scaled, up_w())
+        m.gact[rows, :] = gate_act
+        m.uact[rows, :] = up_act
+        m.inner[rows, :] = (gate_act * jax.nn.sigmoid(gate_act) * up_act).astype(BF16)
+
+    each(0, 2, feed)
+    each(0, 4, lambda zs: gather_pass(s.fd, fd_view, zs))
+    share_rows = m.fdp.shape[1] - 8
+    for i in range(4):
+        m.ffd[2 * i * share_rows : 2 * (i + 1) * share_rows, :] = jnp.concatenate(
+            [m.fdp[2 * i + j, 0:share_rows, :].astype(F32) for j in range(2)], axis=0
+        ).astype(BF16)
+    m.ffd[hidden:pad, :] = jnp.zeros((pad - hidden, width), BF16)
+
+    def feed_out(step):
+        i = lax.rem(a + step, 4)
+        m.ysend[i] = nn(m.inner[block_rows(i, 128), :], m.ffd[...]).astype(BF16)
+        xy_start(s.y, m.ysend.at[i], m.yrecv.at[a], i)
+
+    each(1, 4, feed_out)
+    m.own[...] = nn(m.inner[block_rows(a, 128), :], m.ffd[...])
+    xy_peers(lambda p: xy_wait(s.y, m.yrecv.at[p], p))
+
+    token_total = float(4 * length)
+    m.fin0[...] = jnp.zeros_like(m.fin0)
+
+    def finish(i):
+        rows = block_rows(i, 32)
+        final = m.hid[rows, :] + m.own[rows, :]
+        a1, a2, a3 = lax.rem(a + 1, 4), lax.rem(a + 2, 4), lax.rem(a + 3, 4)
+        final = final + m.yrecv[a1, rows, :].astype(F32)
+        final = final + m.yrecv[a2, rows, :].astype(F32)
+        final = final + m.yrecv[a3, rows, :].astype(F32)
+        out_o[rows, :] = final.astype(BF16)
+        error = final - tea[rows, :].astype(F32)
+        counted = vcol[rows, :] * error
+        grad = counted * (token_total / valid_total)
+        m.dout[rows, :] = grad
+        m.df[pl.ds(pl.multiple_of(a * 128 + i * 32, 32), 32), :] = grad.astype(BF16)
+        squares = jnp.sum(counted * error, axis=0, keepdims=True)
+        lanes = squares[:, 0:128]
+        for j in range(1, width // 128):
+            lanes = lanes + squares[:, j * 128 : j * 128 + 128]
+        m.fin0[40:41, :] += lanes
+
+    each(0, 4, finish)
+    xy_peers(lambda p: xy_start(s.df, quad(m.df, a), quad(m.df, a), p))
+    xy_drain(s.df, quad(m.df, a))
+    xy_peers(lambda p: xy_wait(s.df, quad(m.df, p), p))
+
+    def feed_back(i):
+        rows = block_rows(i, 256)
+        d_inner = nt(m.df[rows, :], m.ffd[...])
+        gate_act = m.gact[rows, :]
+        opened = jax.nn.sigmoid(gate_act)
+        m.dga[rows, :] = (
+            d_inner * m.uact[rows, :] * opened * (1.0 + gate_act * (1.0 - opened))
+        ).astype(BF16)
+        m.dua[rows, :] = (d_inner * gate_act * opened).astype(BF16)
+
+    each(0, 2, feed_back)
+
+    def scaled_grad(i):
+        rows = block_rows(i, 128)
+        return nt(m.dga[rows, :], gate_w()) + nt(m.dua[rows, :], up_w())
+
+    def feed_in(step):
+        i = lax.rem(a + step, 4)
+        m.ysend[i] = scaled_grad(i).astype(BF16)
+        xy_start(s.ds, m.ysend.at[i], m.yrecv.at[a], i)
+
+    xy_peers(lambda p: xy_copy(s.y, m.ysend.at[0], m.ysend.at[0], p).wait_send())
+    each(1, 4, feed_in)
+    xy_drain(s.ds, m.ysend.at[0])
+    m.own[...] = scaled_grad(a)
+
+    def down_grad(i):
+        cols = pl.ds(pl.multiple_of(i * 256, 256), 256)
+        m.ffd[block_rows(i, 256), :] = tn(m.inner[:, cols], m.df[...]).astype(BF16)
+
+    each(0, pad // 256, down_grad)
+    for i in range(4):
+        pair = m.ffd[2 * i * share_rows : 2 * (i + 1) * share_rows, :].astype(F32)
+        for j in range(2):
+            m.gds[i, j] = jnp.concatenate(
+                [pair[j * share_rows : (j + 1) * share_rows, :], jnp.zeros((8, width), F32)], axis=0
+            ).astype(BF16)
+    rgd_copy = copy(m.gds.at[:, 1 - c], m.gdr, s.rgd[0].at[4], s.rgd[1].at[4], (a, sib))
+    rgd_copy.start()
+
+    xy_peers(lambda p: xy_wait(s.ds, m.yrecv.at[p], p))
+    m.ggain[...] = jnp.zeros_like(m.ggain)
+
+    def norm_back(i):
+        rows = block_rows(i, 32)
+        a1, a2, a3 = lax.rem(a + 1, 4), lax.rem(a + 2, 4), lax.rem(a + 3, 4)
+        d_scaled = m.own[rows, :] + m.yrecv[a1, rows, :].astype(F32)
+        d_scaled = d_scaled + m.yrecv[a2, rows, :].astype(F32)
+        d_scaled = d_scaled + m.yrecv[a3, rows, :].astype(F32)
+        inv = m.inv[rows, 0:1]
+        normed = m.hid[rows, :] * inv
+        m.ggain[...] += jnp.sum(d_scaled * normed, axis=0, keepdims=True)
+        d_normed = d_scaled * m.gain[...]
+        lean = jnp.mean(d_normed * normed, axis=1, keepdims=True)
+        d_hidden = m.dout[rows, :] + inv * (d_normed - normed * lean)
+        m.dout[rows, :] = d_hidden
+        opened = jax.nn.sigmoid(m.gp[rows, :].astype(F32))
+        m.dbr[rows, :] = (d_hidden * opened).astype(BF16)
+        m.dgt[rows, :] = (d_hidden * m.br[rows, :] * opened * (1.0 - opened)).astype(BF16)
+
+    each(0, 4, norm_back)
+    gate_cols = pl.ds(384, 128)
+    cols_of = lambda i: pl.ds(pl.multiple_of(i * 128, 128), 128)
+    m.dms[...] = nt(m.dbr[...], m.wo_all[...]).astype(BF16)
+    seq_peers(lambda p: seq_start(s.dm, m.dms.at[:, cols_of(p)], m.dm.at[own_rows, :], p))
+    seq_peers(
+        lambda p: seq_start(s.dg, m.dgt.at[:, cols_of(p)], m.dq.at[own_rows, gate_cols], p)
+    )
+    seq_drain(s.dm, m.dms.at[:, 0:128])
+    seq_drain(s.dg, m.dgt.at[:, 0:128])
+    m.dm[own_rows, :] = m.dms[:, head_cols]
+    m.dq[own_rows, gate_cols] = m.dgt[:, head_cols]
+
+    def out_grad(i):
+        cols = pl.ds(pl.multiple_of(i * 256, 256), 256)
+        m.gwos[i] = tn(m.mx[:, cols], m.dbr[...]).astype(BF16)
+
+    def out_grad_send(step):
+        i = lax.rem(a + step, 4)
+        out_grad(i)
+        xy_start(s.gwo, m.gwos.at[i], m.gwor.at[a], i)
+
+    each(1, 4, out_grad_send)
+    xy_drain(s.gwo, m.gwos.at[0])
+    out_grad(a)
+
+    def up_gate_grad(i):
+        cols = pl.ds(pl.multiple_of(i * 256, 256), 256)
+        scaled = m.sc[:, cols]
+        m.gus[:, :, 0, i] = tn(scaled, m.dga[...]).astype(BF16).reshape(4, 2, 32, pad)
+        m.gus[:, :, 1, i] = tn(scaled, m.dua[...]).astype(BF16).reshape(4, 2, 32, pad)
+
+    each(0, 4, up_gate_grad)
+    rgu_copy = copy(m.gus.at[:, 1 - c], m.gur, s.rgu[0].at[4], s.rgu[1].at[4], (a, sib))
+    rgu_copy.start()
+
+    def sum_line_start(pair, combined, landing, zt):
+        copy(
+            combined.at[zt, c], landing.at[z], pair[0].at[zt], pair[1].at[z], (a, 2 * zt + c)
+        ).start()
+
+    def sum_line_wait(pair, landing, zs):
+        copy(
+            landing.at[zs], landing.at[zs], pair[0].at[zs], pair[1].at[zs], (a, 2 * zs + c)
+        ).wait_recv()
+
+    def sum_line_drain(pair, combined):
+        finals.append(
+            lambda: z_peers(
+                lambda zt: copy(
+                    combined.at[zt, c], combined.at[zt, c], pair[0].at[zt], pair[1].at[zt],
+                    (a, 2 * zt + c),
+                ).wait_send()
+            )
+        )
+
+    rgd_copy.wait_recv()
+
+    def add_down(zt):
+        m.gds[zt, c] = (m.gds[zt, c].astype(F32) + m.gdr[zt].astype(F32)).astype(BF16)
+
+    z_peers(lambda zt: (add_down(zt), sum_line_start(s.rgd, m.gds, m.gdz, zt))[0])
+    sum_line_drain(s.rgd, m.gds)
+    rgu_copy.wait_recv()
+
+    def add_up_gate(zt):
+        def one(i):
+            j = lax.div(i, 4)
+            g = lax.rem(i, 4)
+            m.gus[zt, c, j, g] = (
+                m.gus[zt, c, j, g].astype(F32) + m.gur[zt, j, g].astype(F32)
+            ).astype(BF16)
+
+        each(0, 8, one)
+
+    z_peers(lambda zt: (add_up_gate(zt), sum_line_start(s.rgu, m.gus, m.guz, zt))[0])
+    sum_line_drain(s.rgu, m.gus)
+
+    m.pgrad[...] = jnp.zeros_like(m.pgrad)
+
+    def attend_back(i):
+        rows = block_rows(i, 128)
+        d_mixed = m.dm[rows, :]
+        d_joint = nt(d_mixed, m.v[...])
+        prob = m.probs[rows, :].astype(F32)
+        turned = prob * d_joint
+        fixed_prob = m.fprobs[rows, :]
+        fixed_full = fixed_prob.astype(F32)
+        fixed_turned = fixed_full * nt(d_mixed, m.fkv[16:32, :])
+        delta = jnp.sum(turned, axis=1, keepdims=True) + jnp.sum(
+            fixed_turned, axis=1, keepdims=True
+        )
+        d_raw = (
+            scale * (turned - prob * delta) + m.decay[rows, :].astype(F32) * d_joint
+        ).astype(BF16)
+        m.probs[rows, :] = d_raw
+        d_fixed = (fixed_turned - fixed_full * delta).astype(BF16)
+        m.dq[rows, 0:128] = (
+            nn(d_raw, m.k[...]) + scale * nn(d_fixed, m.fkv[0:16, :])
+        ).astype(BF16)
+        m.pgrad[0:16, :] += scale * tn(d_fixed, m.q[rows, :])
+        m.pgrad[16:32, :] += tn(fixed_prob, d_mixed)
+
+    attend_back(b)
+
+    def attend_back_next(step):
+        i = lax.rem(b + step, 8)
+        seq_wait(s.dm, m.dm.at[block_rows(i, 128), :], i)
+        seq_wait(s.dg, m.dq.at[block_rows(i, 128), gate_cols], i)
+        attend_back(i)
+
+    each(1, 8, attend_back_next)
+
+    m.fin0[0:32, :] = m.pgrad[...]
+    for j in range(8):
+        m.fin0[32 + j : 33 + j, :] = m.ggain[:, j * 128 : j * 128 + 128]
+    m.fin1[a] = m.fin0[...]
+    xy_peers(lambda p: xy_start(s.fin1, m.fin0, m.fin1.at[a], p))
+    xy_drain(s.fin1, m.fin0)
+
+    query_turned = jnp.transpose(m.q[...].astype(F32)).astype(BF16)
+    mixed_turned = jnp.transpose(m.dm[...].astype(F32)).astype(BF16)
+
+    def key_value_grad(i):
+        cols = cols_of(i)
+        rows = block_rows(i, 128)
+        m.dq[rows, 128:256] = jnp.transpose(nn(query_turned, m.probs[:, cols])).astype(BF16)
+        m.dq[rows, 256:384] = jnp.transpose(nn(mixed_turned, m.both[:, cols])).astype(BF16)
+
+    each(0, 8, key_value_grad)
+
+    def head_weight_grad(i):
+        cols = pl.ds(pl.multiple_of(i * 256, 256), 256)
+        m.gws[i] = tn(m.x_all[:, cols], m.dq[...]).astype(BF16)
+
+    def head_weight_send(step):
+        i = lax.rem(a + step, 4)
+        head_weight_grad(i)
+        xy_start(s.gw, m.gws.at[i], m.gwr.at[a], i)
+
+    each(1, 4, head_weight_send)
+    xy_drain(s.gw, m.gws.at[0])
+    head_weight_grad(a)
+
+    def token_grad(i):
+        return nt(m.dq[block_rows(i, 128), :], m.wqk[...])
+
+    def token_sib(step):
+        zt = lax.rem(z + step, 4)
+        m.gts[zt, 1 - c] = token_grad(2 * zt + 1 - c).astype(BF16)
+        copy(
+            m.gts.at[zt, 1 - c], m.gtr.at[zt], s.gt[0].at[4 + zt], s.gt[1].at[4 + zt],
+            (a, sib),
+        ).start()
+
+    each(1, 5, token_sib)
+
+    def token_line(step):
+        zt = lax.rem(z + step, 4)
+        mine = token_grad(2 * zt + c)
+        copy(
+            m.gtr.at[zt], m.gtr.at[zt], s.gt[0].at[4 + zt], s.gt[1].at[4 + zt], (a, sib)
+        ).wait_recv()
+        m.gts[zt, c] = (mine + m.gtr[zt].astype(F32)).astype(BF16)
+        copy(
+            m.gts.at[zt, c], m.yrecv.at[z], s.gt[0].at[zt], s.gt[1].at[z], (a, 2 * zt + c)
+        ).start()
+
+    each(1, 4, token_line)
+    m.own[...] = token_grad(b)
+    finals.append(
+        lambda: each(
+            0, 4,
+            lambda zt: copy(
+                m.gtr.at[zt], m.gtr.at[zt], s.gt[0].at[4 + zt], s.gt[1].at[4 + zt], (a, sib)
+            ).wait_send(),
+        )
+    )
+    finals.append(
+        lambda: z_peers(
+            lambda zt: copy(
+                m.yrecv.at[zt], m.yrecv.at[zt], s.gt[0].at[zt], s.gt[1].at[zt], (a, 2 * zt + c)
+            ).wait_send()
+        )
+    )
+
+    xy_peers(lambda p: xy_wait(s.fin1, m.fin1.at[p], p))
+    m.fin2s[...] = (m.fin1[0] + m.fin1[1]) + (m.fin1[2] + m.fin1[3])
+    m.fin2[b] = m.fin2s[...]
+    seq_peers(lambda p: seq_start(s.fin2, m.fin2s, m.fin2.at[b], p))
+    seq_drain(s.fin2, m.fin2s)
+
+    xy_peers(lambda p: xy_wait(s.gw, m.gwr.at[p], p))
+    a1, a2, a3 = lax.rem(a + 1, 4), lax.rem(a + 2, 4), lax.rem(a + 3, 4)
+
+    def head_sum(p):
+        rows = block_rows(p, 32)
+        total = m.gws[a, rows, :].astype(F32) + m.gwr[a1, rows, :].astype(F32)
+        total = total + m.gwr[a2, rows, :].astype(F32)
+        total = total + m.gwr[a3, rows, :].astype(F32)
+        m.gas[p] = total.astype(BF16)
+
+    def head_sum_send(p):
+        head_sum(p)
+        seq_start(s.gwa, m.gas.at[p], m.gar.at[b], p)
+
+    seq_peers(head_sum_send)
+    seq_drain(s.gwa, m.gas.at[0])
+    head_sum(b)
+    m.gar[b] = m.gas[b]
+
+    xy_peers(lambda p: xy_wait(s.gwo, m.gwor.at[p], p))
+
+    def out_sum(i):
+        rows = block_rows(i, 32)
+        total = m.gwos[a, rows, :].astype(F32) + m.gwor[a1, rows, :].astype(F32)
+        total = total + m.gwor[a2, rows, :].astype(F32)
+        total = total + m.gwor[a3, rows, :].astype(F32)
+        m.gos[lax.div(i, 2), lax.rem(i, 2)] = total.astype(BF16)
+
+    each(0, 8, out_sum)
+    rgo_copy = copy(m.gos.at[:, 1 - c], m.gor, s.rgo[0].at[4], s.rgo[1].at[4], (a, sib))
+    rgo_copy.start()
+
+    z1, z2, z3 = lax.rem(z + 1, 4), lax.rem(z + 2, 4), lax.rem(z + 3, 4)
+    z_peers(lambda zs: sum_line_wait(s.rgu, m.guz, zs))
+
+    def up_gate_sum(i):
+        j = lax.div(i, 4)
+        g = lax.rem(i, 4)
+        total = m.gus[z, c, j, g].astype(F32) + m.gur[z, j, g].astype(F32)
+        total = total + m.guz[z1, j, g].astype(F32)
+        total = total + m.guz[z2, j, g].astype(F32)
+        total = total + m.guz[z3, j, g].astype(F32)
+        m.gux[g, j] = total.astype(BF16)
+
+    each(0, 8, up_gate_sum)
+    xy_peers(lambda p: xy_start(s.gfx, m.gux.at[p], m.guxr.at[a], p))
+    xy_drain(s.gfx, m.gux.at[0])
+    m.guxr[a] = m.gux[a]
+
+    rgo_copy.wait_recv()
+
+    def add_out(zt):
+        m.gos[zt, c] = (m.gos[zt, c].astype(F32) + m.gor[zt].astype(F32)).astype(BF16)
+
+    z_peers(lambda zt: (add_out(zt), sum_line_start(s.rgo, m.gos, m.goz, zt))[0])
+    sum_line_drain(s.rgo, m.gos)
+
+    z_peers(lambda zs: sum_line_wait(s.rgd, m.gdz, zs))
+    fd_o[...] = (
+        (m.gds[z, c, 0:share_rows, :].astype(F32) + m.gdr[z, 0:share_rows, :].astype(F32))
+        + (m.gdz[z1, 0:share_rows, :].astype(F32) + m.gdz[z2, 0:share_rows, :].astype(F32))
+    ) + m.gdz[z3, 0:share_rows, :].astype(F32)
+
+    z_peers(
+        lambda zs: copy(
+            m.yrecv.at[zs], m.yrecv.at[zs], s.gt[0].at[zs], s.gt[1].at[zs], (a, 2 * zs + c)
+        ).wait_recv()
+    )
+    copy(
+        m.gtr.at[z], m.gtr.at[z], s.gt[0].at[4 + z], s.gt[1].at[4 + z], (a, sib)
+    ).wait_recv()
+
+    def token_sum(i):
+        rows = block_rows(i, 32)
+        total = m.dout[rows, :] + m.own[rows, :]
+        total = total + m.gtr[z, rows, :].astype(F32)
+        total = total + m.yrecv[z1, rows, :].astype(F32)
+        total = total + m.yrecv[z2, rows, :].astype(F32)
+        gtok_o[rows, :] = total + m.yrecv[z3, rows, :].astype(F32)
+
+    each(0, 4, token_sum)
+
+    seq_peers(lambda p: seq_wait(s.gwa, m.gar.at[p], p))
+    for head in range(8):
+        cols = slice(head * 128, head * 128 + 128)
+        gq_o[:, cols] = m.gar[head, :, 0:128].astype(F32)
+        gk_o[:, cols] = m.gar[head, :, 128:256].astype(F32)
+        gv_o[:, cols] = m.gar[head, :, 256:384].astype(F32)
+        gwg_o[:, cols] = m.gar[head, :, 384:512].astype(F32)
+
+    xy_peers(lambda p: xy_wait(s.gfx, m.guxr.at[p], p))
+    for part in range(4):
+        fg_o[:, part * hidden : (part + 1) * hidden] = m.guxr[part, 0, :, 0:hidden].astype(F32)
+        fu_o[:, part * hidden : (part + 1) * hidden] = m.guxr[part, 1, :, 0:hidden].astype(F32)
+
+    z_peers(lambda zs: sum_line_wait(s.rgo, m.goz, zs))
+    gwo_o[...] = (
+        (m.gos[z, c].astype(F32) + m.gor[z].astype(F32))
+        + (m.goz[z1].astype(F32) + m.goz[z2].astype(F32))
+    ) + m.goz[z3].astype(F32)
+
+    seq_peers(lambda p: seq_wait(s.fin2, m.fin2.at[p], p))
+    everything = jnp.sum(m.fin2[:, 32:48, :], axis=0)
+    fin_o[0:8, :] = everything[0:8, :]
+    loss = jnp.sum(everything[8:9, :]) / (2.0 * width * valid_total)
+    fin_o[8:16, :] = jnp.full((8, 128), loss, F32)
+    pers_o[...] = m.fin2[2 * a + lax.div(b, 4), 0:32, :]
+
+    rgd_copy.wait_send()
+    rgu_copy.wait_send()
+    rgo_copy.wait_send()
+    for last in finals:
+        last()
+
+
+def local_block(
+    tokens, w_query, w_key, w_value, w_out, w_gate, persist_keys, persist_values, norm_gain,
+    ff_gate, ff_up, ff_down, retention, doc_starts, valid, teacher,
+):
+    _, block, width = tokens.shape
+    length = block * lax.axis_size("seq")
+    hidden = ff_gate.shape[1] // 4
+    pad = -(-hidden // 256) * 256
+    share = ff_down.shape[0]
+    a = lax.axis_index("head")
+    b = lax.axis_index("seq")
+    place = a * 8 + b
+    lanes = (jnp.arange(128) // 32) == lax.rem(b, 4)
+    spread = lambda v: jnp.where(lanes, jnp.tile(v, (1, 4)), jnp.zeros((), v.dtype))
+    rates = jnp.transpose(jnp.log(retention), (0, 2, 1))
+    line = lambda v: jnp.broadcast_to(v[None], (4, 1, 128))
+    tile = jnp.concatenate(
+        [
+            rates,
+            line(valid.astype(F32)),
+            line(spread(norm_gain.astype(F32)[None])),
+            jnp.zeros((4, 4, 128), F32),
+        ],
+        axis=1,
+    )
+    persist = spread(jnp.concatenate([persist_keys, persist_values], axis=0))
+    table = scratch_table(width, block, hidden, pad, length)
+    names = tuple(table)
+    vmem = pl.BlockSpec(memory_space=pltpu.VMEM)
+    shape = jax.ShapeDtypeStruct
+    outs = (
+        shape((block, width), BF16),
+        shape((block, width), F32),
+        shape((32, width), F32),
+        shape((32, width), F32),
+        shape((32, width), F32),
+        shape((32, width), F32),
+        shape((32, width), F32),
+        shape((16, 128), F32),
+        shape((32, 128), F32),
+        shape((32, 4 * hidden), F32),
+        shape((32, 4 * hidden), F32),
+        shape((share, width), F32),
+    )
+    scratch = [pltpu.VMEM(*table[name]) for name in names]
+    for count in FLAGS.values():
+        scratch += [pltpu.SemaphoreType.DMA((count,))] * 2
+    result = pl.pallas_call(
+        functools.partial(block_kernel, names, width, hidden, doc_starts.shape[1]),
+        out_shape=outs,
+        in_specs=[vmem] * 13 + [pl.BlockSpec(memory_space=pltpu.SMEM)],
+        out_specs=[vmem] * len(outs),
+        scratch_shapes=scratch,
+        compiler_params=pltpu.CompilerParams(
+            collective_id=0, has_side_effects=True, vmem_limit_bytes=VMEM_LIMIT
+        ),
+        name="block",
+    )(
+        tokens[0], w_query, w_key, w_value, w_out, w_gate, ff_gate, ff_up,
+        jnp.pad(ff_down, ((0, 96 - share), (0, 0))), teacher[0], tile, persist,
+        valid.astype(F32).reshape(block, 1), doc_starts,
+    )
+    (out, gtok, gq, gk, gv, gwo, gwg, fin, pers, fg, fu, fd) = result
+    own = lax.dynamic_slice_in_dim(pers, lax.rem(b, 4) * 32, 32, 1)
+    gain = lax.dynamic_slice_in_dim(fin[0:8].reshape(width), place * 32, 32, 0)
+    return (
+        out[None], fin[8, 0], gtok[None], gq, gk, gv, gwo, gwg, own[:P_SIZE], own[P_SIZE:],
+        gain, fg, fu, fd,
+    )
+
+
+VMEM_LIMIT = 62 << 20
 
 
 def entering(value, axis, join, neutral, backward):
@@ -556,4 +1486,6 @@
         P(("head", "seq"), None),
         P(("head", "seq"), None),
     )
-    return jax.shard_map(local, mesh=mesh, in_specs=in_specs, out_specs=out_specs, check_vma=False)
+    fits = mesh.shape["head"] == 4 and mesh.shape["seq"] == HEAD_COUNT
+    body = local_block if fits else local
+    return jax.shard_map(body, mesh=mesh, in_specs=in_specs, out_specs=out_specs, check_vma=False)

time: 2140 us -> 296 us (0.14)
  waiting for transfers between devices: 1550 us -> 0 us
  Pallas kernels: 0 us -> 275 us
  blocking collectives: 259 us -> 0 us
  starting transfers between devices: 115 us -> 0 us
  matrix products: 106 us -> 0 us
  local copies, waits for them, and re-layouts: 49.3 us -> 16.8 us
  other arithmetic: 31.8 us -> 2.67 us
    reduce_scatter x4 -> x0, waiting for transfers between devices: 609 us -> none  [the longest x1 161 us: local(): lax.psum_scatter(grad_down, ('head', 'seq'), scatter_dimension=0, tiled=T...]
    unnamed x28 -> x0, waiting for transfers between devices: 575 us -> none
    all_gather x12 -> x0, waiting for transfers between devices: 342 us -> none  [the longest x1 66 us: local(): lax.all_gather(ff_gate, ('head', 'seq'), axis=0, tiled=True)]
    pallas_call x0 -> x1, Pallas kernels: none -> 275 us  [local_block(): pl.pallas_call(functools.partial(block_kernel, names, width, hidden, doc_...]
    dot_general x49 -> x0, matrix products: 106 us -> none  [the longest x8 31 us: rows_outer(): jnp.einsum('nd,ne->de', left, right, preferred_element_type=jnp.float32)]
    ppermute x32 -> x0, starting transfers between devices: 102 us -> none  [the longest x16 55.5 us: from_behind(): return lax.ppermute(block, axis, route)]
    all_gather x3 -> x0, blocking collectives: 90.7 us -> none  [the longest x1 40.2 us: local(): lax.all_gather(jnp.transpose(persist_values), ('head', 'seq'), axis=0, ti...]
    psum x2 -> x0, blocking collectives: 86.1 us -> none  [local(): lax.psum((jnp.sum(valid_rows * jnp.sum(error * error, axis=-1)), jnp.sum(...]
  transfers between devices with their start and end apart: 57 -> 0, of which waited for: 26 -> 0; matrix products, arithmetic and copies ran while one was open for 7% -> 0% of each run, Pallas kernels for 0% -> 0%
where the time goes in v1:
time: 296 us
  Pallas kernels  275 us (93%)
  local copies, waits for them, and re-layouts  16.8 us (6%)
    pallas_call x1, Pallas kernels, local_block(): pl.pallas_call(functools.partial(block_kernel, names, width, hidden, doc_...  275 us
    unnamed x30, local copies, waits for them, and re-layouts  9.83 us

profile of v1, /device:TPU:0, one launch (start us, length us, event | category | flops | bytes accessed | tf_op | source)
XLA Modules:
  0.0 295.7 jit_solution(11307849767594266292)
XLA Ops:
  0.6 0.0 copy-start.4
  0.7 0.7 tile.8
  1.4 0.1 tile.18
  1.5 0.7 convert_bitcast_fusion
  2.1 0.7 log_bitcast_fusion
  2.8 0.1 pad.10.clone
  2.9 0.7 maximum_maximum_fusion.refs_10_
  3.6 0.7 pad_maximum_fusion
  4.3 0.1 tile.20
  4.4 0.6 broadcast_select_fusion.refs_11_
  5.0 0.7 copy.30.refs_12_
  5.8 0.0 copy-done.4
  5.8 0.7 pad.4.refs_8_
  6.4 275.5 %block.1 = (bf16[128,1024]{1,0:T(8,128)(2,1)}, f32[128,1024]{1,0:T(8,128)}, f32[32,1024]{1,0:T(8,128)}, f32[32,1024]{1,0:T(8,128)}, f32[32,1024]{1,0:T(8,128)}, ...) custom-call(bf16[128,1024]{1,0:T(8,128)(2,1)} %bitcast.15, ...), custom_call_target="tpu_custom_call" | custom-call | tf_op jit(solution)/shard_map/block/pallas_call | solution.py:919
  281.9 0.0 copy-start
  281.9 1.5 fusion.1
  283.4 0.7 slice_bitcast_fusion
  284.1 0.6 dynamic_slice.7
  284.6 1.2 slice.12
  285.8 1.7 copy.41
  287.5 0.0 copy-done
  287.5 0.0 copy-start.9
  287.5 0.8 copy.42
  288.3 0.2 copy-done.9
  288.5 0.0 copy-start.8
  288.5 0.7 copy.43
  289.2 0.3 copy-done.8
  289.5 0.0 copy-start.7
  289.5 0.0 copy-start.6
  289.5 0.7 copy.44
  290.1 0.3 copy-done.7
  290.4 0.0 copy-start.3
  290.4 0.7 copy.45
  291.1 0.0 copy-done.6
  291.1 0.0 copy-start.5
  291.1 0.7 copy.46
  291.7 0.3 copy-done.5
  292.0 0.7 copy.47
  292.7 0.0 copy-done.3
  292.7 0.0 copy-start.2
  292.7 0.7 copy.48
  293.4 0.4 copy-done.2
  293.8 0.0 copy-start.1
  293.8 0.7 copy.49
  294.6 0.4 copy-done.1
  294.9 0.7 copy.50
  (6 shorter events, 0.0 us)
Async XLA Ops:
  0.6 5.1 %copy-start.4 = (bf16[88,1024]{1,0:T(8,128)(2,1)S(1)}, bf16[88,1024]{1,0:T(8,128)(2,1)}, u32[]{:S(2)}) copy-start(bf16[88,1024]{1,0:T(8,128)(2,1)} %param.27) | copy-start | bytes 540676
  281.9 5.6 %copy-start = (f32[128,1024]{1,0:T(8,128)S(1)}, f32[128,1024]{1,0:T(8,128)}, u32[]{:S(2)}) copy-start(f32[128,1024]{1,0:T(8,128)} %get-tuple-element.28) | copy-start | bytes 1572868
  287.5 1.0 copy-start.9
  288.5 1.0 copy-start.8
  289.5 1.0 copy-start.7
  289.5 1.6 copy-start.6
  290.4 2.3 copy-start.3
  291.1 1.0 copy-start.5
  292.7 1.1 copy-start.2
  293.8 1.1 copy-start.1

commit v2 on v1

--- a/solution.py
+++ b/solution.py
@@ -64,8 +64,8 @@
 
 
 SEQ_FLAGS = dict(
-    w1=8, t2=8, p2=8, x=8, wo=8, fgu=8, fd=8, gp=8, mx=8, dm=8, dg=8, rgu=8, rgd=8, rgo=8, gt=8,
-    gwa=8, fin2=8,
+    w1=8, t2=8, p2=8, x=8, wo=8, fg=8, fd=8, fu=8, gp=8, mx=8, dm=8, dg=8, rgu=8, rgd=8, rgo=8,
+    gt=8, gwa=8, fin2=8, pers=8,
 )
 XY_FLAGS = dict(t1=4, p1=4, w2=4, fx=4, wox=4, sc=4, y=4, df=4, ds=4, gwo=4, gw=4, gfx=4, fin1=4)
 FLAGS = SEQ_FLAGS | XY_FLAGS
@@ -77,6 +77,9 @@
         x_all=((length, width), BF16),
         wcs=((blocks, 32, 512), BF16),
         wqk=((width, 512), BF16),
+        tile=((4, 8, 128), F32),
+        pin=((32, 128), BF16),
+        vcol=((block, 1), F32),
         t1=((4, 8, 128), F32),
         p1=((4, 32, 128), BF16),
         t2s=((16, 128), F32),
@@ -145,18 +148,19 @@
         fin0=((48, 128), F32),
         fin1=((4, 48, 128), F32),
         fin2s=((48, 128), F32),
-        fin2=((8, 48, 128), F32),
+        fin2=((8, 16, 128), F32),
+        pers=((32, 128), F32),
     )
     return table
 
 
 def block_kernel(names, width, hidden, ndoc, *refs):
     (
-        tok, wq, wk, wv, wo, wg, fgi, fui, fdi, tea, tile, pin, vcol, docs,
-        out_o, gtok_o, gq_o, gk_o, gv_o, gwo_o, gwg_o, fin_o, pers_o, fg_o, fu_o, fd_o,
-    ) = refs[:26]
-    m = types.SimpleNamespace(**dict(zip(names, refs[26 : 26 + len(names)])))
-    sems = refs[26 + len(names) :]
+        tok, wq, wk, wv, wo, wg, fgi, fui, fdi, tea, ret, pk, pv, gin, val, docs,
+        out_o, gtok_o, gar_o, gwo_o, fin_o, pers_o, gux_o, fd_o,
+    ) = refs[:24]
+    m = types.SimpleNamespace(**dict(zip(names, refs[24 : 24 + len(names)])))
+    sems = refs[24 + len(names) :]
     s = types.SimpleNamespace(**dict(zip(FLAGS, zip(sems[0::2], sems[1::2]))))
     pad = m.ffd.shape[0]
     length = m.x_all.shape[0]
@@ -168,6 +172,10 @@
     z = lax.div(b, 2)
     c = lax.rem(b, 2)
     sib = 2 * z + 1 - c
+    near = z + 1 - 2 * lax.rem(z, 2)
+    mirror = 3 - z
+    across = 3 - near
+    inner_chip = (z == 1) | (z == 2)
 
     def copy(src, dst, ssem, rsem, device):
         return pltpu.make_async_remote_copy(
@@ -219,7 +227,13 @@
         return copy(src, dst, pair[0].at[4 + zs], pair[1].at[4 + zs], (a, sib))
 
     def gather_start(pair, src, view):
-        z_peers(lambda zt: line_copy(pair, src, view(b), zt).start())
+        line_copy(pair, src, view(b), mirror).start()
+        line_copy(pair, src, view(b), near).start()
+
+        @pl.when(jnp.logical_not(inner_chip))
+        def _():
+            line_copy(pair, src, view(b), across).start()
+
         pass_copy(pair, src, view(b), z).start()
         finals.append(lambda: z_peers(lambda zt: line_copy(pair, src, src, zt).wait_send()))
         finals.append(lambda: each(0, 4, lambda zs: pass_copy(pair, src, src, zs).wait_send()))
@@ -228,6 +242,16 @@
         block = view(2 * zs + c)
         copy(block, block, pair[0].at[zs], pair[1].at[zs], (a, 2 * zs + c)).wait_recv()
         pass_copy(pair, block, block, zs).start()
+
+    def gather_mirror(pair, view):
+        gather_line(pair, view, mirror)
+        block = view(2 * mirror + c)
+
+        @pl.when(inner_chip)
+        def _():
+            copy(
+                block, block, pair[0].at[across], pair[1].at[mirror], (a, 2 * near + c)
+            ).start()
 
     def gather_pass(pair, view, zs):
         block = view(2 * zs + 1 - c)
@@ -251,21 +275,40 @@
     m.x_all[own_rows, :] = tok[...]
     m.wqk[piece, :] = m.wcs[b]
     m.wo_all[piece, :] = wo[...]
-    m.fdp[b] = fdi[...]
+    down = fdi[...].astype(F32)
+    m.fdp[b] = jnp.concatenate(
+        [down, jnp.zeros((96 - down.shape[0], width), F32)], axis=0
+    ).astype(BF16)
     slot32 = block_rows(b, 32)
     m.fgu[:, a, slot32, :] = m.fs[a]
-    m.t1[a] = tile[a]
-    m.p1[a] = pin[...]
+    row_id = lax.broadcasted_iota(jnp.int32, (128, 128), 0)
+    col_id = lax.broadcasted_iota(jnp.int32, (128, 128), 1)
+    place = (
+        lax.broadcasted_iota(jnp.int32, (32, 128), 1)
+        == lax.broadcasted_iota(jnp.int32, (32, 128), 0) + 32 * lax.rem(b, 4)
+    ).astype(BF16)
+    m.pin[0:16, :] = nn(pk[...], place).astype(BF16)
+    m.pin[16:32, :] = nn(pv[...], place).astype(BF16)
+    counted_row = val[...].astype(F32)
+    m.vcol[...] = jnp.sum(jnp.where(row_id == col_id, counted_row, 0.0), axis=1, keepdims=True)
+    gain_row = nn(gin[...], place)
+    m.tile[...] = jnp.zeros_like(m.tile)
+    for group in range(4):
+        m.tile[group, 0:2, :] = jnp.log(ret[group])
+        m.tile[group, 2:3, :] = counted_row
+        m.tile[group, 3:4, :] = gain_row
+    m.t1[a] = m.tile[a]
+    m.p1[a] = m.pin[...]
     pl.semaphore_wait(barrier, 10)
 
-    xy_peers(lambda p: xy_start(s.t1, tile.at[p], m.t1.at[a], p))
-    xy_peers(lambda p: xy_start(s.p1, pin, m.p1.at[a], p))
+    xy_peers(lambda p: xy_start(s.t1, m.tile.at[p], m.t1.at[a], p))
+    xy_peers(lambda p: xy_start(s.p1, m.pin, m.p1.at[a], p))
     seq_peers(lambda p: seq_start(s.w1, m.wcs.at[p], m.wqk.at[piece, :], p))
     x_view = lambda i: m.x_all.at[block_rows(i, 128), :]
     gather_start(s.x, tok, x_view)
     xy_peers(lambda p: xy_start(s.fx, m.fs.at[p], m.fgu.at[:, a, slot32, :], p))
-    xy_drain(s.t1, tile.at[0])
-    xy_drain(s.p1, pin)
+    xy_drain(s.t1, m.tile.at[0])
+    xy_drain(s.p1, m.pin)
     seq_drain(s.w1, m.wcs.at[0])
     xy_drain(s.fx, m.fs.at[0])
 
@@ -279,9 +322,26 @@
     m.t2[b] = m.t2s[...]
     m.p2[b] = m.p1[lax.div(b, 2)]
     seq_peers(lambda p: seq_start(s.t2, m.t2s, m.t2.at[b], p))
-    seq_peers(lambda p: seq_start(s.p2, m.p1.at[lax.div(p, 2)], m.p2.at[b], p))
+    half = 4 * c
+
+    def persist_send(p):
+        @pl.when(lax.rem(p, 2) == lax.div(b, 4))
+        def _():
+            seq_start(s.p2, m.p1.at[lax.div(p, 2)], m.p2.at[b], p)
+
+    def persist_drain(p):
+        @pl.when(lax.rem(p, 2) == lax.div(b, 4))
+        def _():
+            seq_copy(s.p2, m.pin, m.pin, p).wait_send()
+
+    def persist_wait(p):
+        @pl.when(lax.div(p, 4) == c)
+        def _():
+            seq_wait(s.p2, m.p2.at[p], p)
+
+    seq_peers(persist_send)
+    finals.append(lambda: seq_peers(persist_drain))
     seq_drain(s.t2, m.t2s)
-    seq_drain(s.p2, m.p1.at[0])
 
     seq_peers(lambda p: seq_wait(s.w1, m.wqk.at[pl.ds(pl.multiple_of(a * 256 + p * 32, 32), 32), :], p))
     quarter = lambda i: m.wqk.at[block_rows(i, 256), :]
@@ -314,26 +374,34 @@
         project(2 * zs + c)
         send_gate(2 * zs + c)
 
-    each(1, 4, arrived_line)
+    def arrived(i):
+        project(i)
+        send_gate(i)
+
+    gather_mirror(s.x, x_view)
+    arrived(2 * mirror + c)
+    gather_line(s.x, x_view, near)
+    arrived(2 * near + c)
+    gather_line(s.x, x_view, across)
 
     def arrived_pass(step):
         zs = lax.rem(z + step, 4)
         gather_pass(s.x, x_view, zs)
-        project(2 * zs + 1 - c)
-        send_gate(2 * zs + 1 - c)
+        arrived(2 * zs + 1 - c)
 
     wo_view = lambda i: m.wo_all.at[pl.ds(pl.multiple_of(a * 256 + i * 32, 32), 32), :]
     gather_start(s.wo, wo, wo_view)
     xy_peers(lambda p: xy_wait(s.fx, m.fgu.at[:, p, slot32, :], p))
-    fgu_view = lambda i: m.fgu.at[:, :, block_rows(i, 32), :]
+    fg_view = lambda i: m.fgu.at[0, :, block_rows(i, 32), :]
+    fu_view = lambda i: m.fgu.at[1, :, block_rows(i, 32), :]
     fd_view = lambda i: m.fdp.at[i]
-    gather_start(s.fgu, fgu_view(b), fgu_view)
-    gather_start(s.fd, fdi, fd_view)
+    gather_start(s.fg, fg_view(b), fg_view)
+    arrived(2 * across + c)
     each(1, 4, arrived_pass)
     seq_drain(s.gp, m.gps.at[own_rows, :])
 
     seq_peers(lambda p: seq_wait(s.t2, m.t2.at[p], p))
-    seq_peers(lambda p: seq_wait(s.p2, m.p2.at[p], p))
+    seq_peers(persist_wait)
     small = m.t2[...]
     place16 = lax.broadcasted_iota(jnp.int32, (8, 16, 128), 1)
     rates = jnp.sum(jnp.where(place16 == b, small, 0.0), axis=1)
@@ -344,13 +412,10 @@
         m.gain[:, group * 128 : group * 128 + 128] = (
             m.t2[first, line : line + 1, :] + m.t2[first + 1, line : line + 1, :]
         ) + (m.t2[first + 2, line : line + 1, :] + m.t2[first + 3, line : line + 1, :])
-    half = 4 * lax.rem(b, 2)
     m.fkv[...] = (
         (m.p2[half].astype(F32) + m.p2[half + 1].astype(F32))
         + (m.p2[half + 2].astype(F32) + m.p2[half + 3].astype(F32))
     ).astype(BF16)
-    row_id = lax.broadcasted_iota(jnp.int32, (128, 128), 0)
-    col_id = lax.broadcasted_iota(jnp.int32, (128, 128), 1)
     lower = (col_id <= row_id).astype(F32)
     within = nt_exact(rates, lower)
     earlier = (
@@ -407,13 +472,18 @@
         seq_start(s.mx, m.mxs.at[block_rows(i, 128), :], m.mx.at[:, head_cols], i)
 
     each(1, 4, attend_send)
-    z_peers(lambda zs: gather_line(s.wo, wo_view, zs))
+    gather_mirror(s.wo, wo_view)
+    gather_line(s.wo, wo_view, near)
+    gather_line(s.wo, wo_view, across)
     each(4, 6, attend_send)
     each(0, 4, lambda zs: gather_pass(s.wo, wo_view, zs))
     wo_quarter = lambda i: m.wo_all.at[block_rows(i, 256), :]
     xy_peers(lambda p: xy_start(s.wox, wo_quarter(a), wo_quarter(a), p))
     xy_drain(s.wox, wo_quarter(a))
-    each(6, 8, attend_send)
+    each(6, 7, attend_send)
+    gather_mirror(s.fg, fg_view)
+    gather_start(s.fu, fu_view(b), fu_view)
+    each(7, 8, attend_send)
     seq_drain(s.mx, m.mxs.at[own_rows, :])
     attend(b)
     m.mx[:, head_cols] = m.mxs[own_rows, :]
@@ -440,9 +510,15 @@
     xy_peers(lambda p: xy_start(s.sc, quad(m.sc, a), quad(m.sc, a), p))
     xy_drain(s.sc, quad(m.sc, a))
 
-    z_peers(lambda zs: gather_line(s.fgu, fgu_view, zs))
-    z_peers(lambda zs: gather_line(s.fd, fd_view, zs))
-    each(0, 4, lambda zs: gather_pass(s.fgu, fgu_view, zs))
+    gather_mirror(s.fu, fu_view)
+    gather_start(s.fd, fd_view(b), fd_view)
+    gather_line(s.fg, fg_view, near)
+    gather_line(s.fg, fg_view, across)
+    each(0, 4, lambda zs: gather_pass(s.fg, fg_view, zs))
+    gather_mirror(s.fd, fd_view)
+    gather_line(s.fu, fu_view, near)
+    gather_line(s.fu, fu_view, across)
+    each(0, 4, lambda zs: gather_pass(s.fu, fu_view, zs))
     xy_peers(lambda p: xy_wait(s.sc, quad(m.sc, p), p))
 
     gate_w = lambda: m.fgu[0].reshape(width, pad)
@@ -458,6 +534,8 @@
         m.inner[rows, :] = (gate_act * jax.nn.sigmoid(gate_act) * up_act).astype(BF16)
 
     each(0, 2, feed)
+    gather_line(s.fd, fd_view, near)
+    gather_line(s.fd, fd_view, across)
     each(0, 4, lambda zs: gather_pass(s.fd, fd_view, zs))
     share_rows = m.fdp.shape[1] - 8
     for i in range(4):
@@ -487,7 +565,7 @@
         final = final + m.yrecv[a3, rows, :].astype(F32)
         out_o[rows, :] = final.astype(BF16)
         error = final - tea[rows, :].astype(F32)
-        counted = vcol[rows, :] * error
+        counted = m.vcol[rows, :] * error
         grad = counted * (token_total / valid_total)
         m.dout[rows, :] = grad
         m.df[pl.ds(pl.multiple_of(a * 128 + i * 32, 32), 32), :] = grad.astype(BF16)
@@ -528,6 +606,55 @@
     xy_drain(s.ds, m.ysend.at[0])
     m.own[...] = scaled_grad(a)
 
+    def share_copy(pair, share, landing, slot, zt):
+        return copy(share, landing.at[slot], pair[0].at[zt], pair[1].at[slot], (a, 2 * zt + c))
+
+    def sum_start(pair, share, landing):
+        share_copy(pair, share(near), landing, z, near).start()
+
+        @pl.when(inner_chip)
+        def _():
+            share_copy(pair, share(across), landing, z, across).start()
+
+        @pl.when(jnp.logical_not(inner_chip))
+        def _():
+            share_copy(pair, share(mirror), landing, z, mirror).start()
+            copy(
+                share(across), landing.at[mirror], pair[0].at[across], pair[1].at[mirror],
+                (a, 2 * near + c),
+            ).start()
+
+    def sum_wait(pair, landing, zs):
+        copy(
+            landing.at[zs], landing.at[zs], pair[0].at[zs], pair[1].at[zs], (a, 2 * zs + c)
+        ).wait_recv()
+
+    def sum_pass(pair, share, landing, add):
+        @pl.when(inner_chip)
+        def _():
+            sum_wait(pair, landing, across)
+            add(mirror, across)
+            share_copy(pair, share(mirror), landing, z, mirror).start()
+
+    def sum_finish(pair, share, landing):
+        sum_wait(pair, landing, near)
+        sum_wait(pair, landing, mirror)
+
+        @pl.when(jnp.logical_not(inner_chip))
+        def _():
+            sum_wait(pair, landing, across)
+
+        finals.append(
+            lambda: z_peers(
+                lambda zt: share_copy(pair, share(zt), landing, zt, zt).wait_send()
+            )
+        )
+
+    def landed(landing, where):
+        total = landing[(near,) + where].astype(F32) + landing[(mirror,) + where].astype(F32)
+        last = landing[(across,) + where].astype(F32)
+        return total + jnp.where(inner_chip, 0.0, last)
+
     def down_grad(i):
         cols = pl.ds(pl.multiple_of(i * 256, 256), 256)
         m.ffd[block_rows(i, 256), :] = tn(m.inner[:, cols], m.df[...]).astype(BF16)
@@ -541,6 +668,28 @@
             ).astype(BF16)
     rgd_copy = copy(m.gds.at[:, 1 - c], m.gdr, s.rgd[0].at[4], s.rgd[1].at[4], (a, sib))
     rgd_copy.start()
+
+    def up_gate_grad(i):
+        cols = pl.ds(pl.multiple_of(i * 256, 256), 256)
+        scaled = m.sc[:, cols]
+        m.gus[:, :, 0, i] = tn(scaled, m.dga[...]).astype(BF16).reshape(4, 2, 32, pad)
+        m.gus[:, :, 1, i] = tn(scaled, m.dua[...]).astype(BF16).reshape(4, 2, 32, pad)
+
+    each(0, 4, up_gate_grad)
+    rgu_copy = copy(m.gus.at[:, 1 - c], m.gur, s.rgu[0].at[4], s.rgu[1].at[4], (a, sib))
+    rgu_copy.start()
+
+    down_share = lambda zt: m.gds.at[zt, c]
+
+    def add_down(zt):
+        m.gds[zt, c] = (m.gds[zt, c].astype(F32) + m.gdr[zt].astype(F32)).astype(BF16)
+
+    def pass_down(zt, slot):
+        m.gds[zt, c] = (m.gds[zt, c].astype(F32) + m.gdz[slot].astype(F32)).astype(BF16)
+
+    rgd_copy.wait_recv()
+    z_peers(add_down)
+    sum_start(s.rgd, down_share, m.gdz)
 
     xy_peers(lambda p: xy_wait(s.ds, m.yrecv.at[p], p))
     m.ggain[...] = jnp.zeros_like(m.ggain)
@@ -588,44 +737,7 @@
     xy_drain(s.gwo, m.gwos.at[0])
     out_grad(a)
 
-    def up_gate_grad(i):
-        cols = pl.ds(pl.multiple_of(i * 256, 256), 256)
-        scaled = m.sc[:, cols]
-        m.gus[:, :, 0, i] = tn(scaled, m.dga[...]).astype(BF16).reshape(4, 2, 32, pad)
-        m.gus[:, :, 1, i] = tn(scaled, m.dua[...]).astype(BF16).reshape(4, 2, 32, pad)
-
-    each(0, 4, up_gate_grad)
-    rgu_copy = copy(m.gus.at[:, 1 - c], m.gur, s.rgu[0].at[4], s.rgu[1].at[4], (a, sib))
-    rgu_copy.start()
-
-    def sum_line_start(pair, combined, landing, zt):
-        copy(
-            combined.at[zt, c], landing.at[z], pair[0].at[zt], pair[1].at[z], (a, 2 * zt + c)
-        ).start()
-
-    def sum_line_wait(pair, landing, zs):
-        copy(
-            landing.at[zs], landing.at[zs], pair[0].at[zs], pair[1].at[zs], (a, 2 * zs + c)
-        ).wait_recv()
-
-    def sum_line_drain(pair, combined):
-        finals.append(
-            lambda: z_peers(
-                lambda zt: copy(
-                    combined.at[zt, c], combined.at[zt, c], pair[0].at[zt], pair[1].at[zt],
-                    (a, 2 * zt + c),
-                ).wait_send()
-            )
-        )
-
-    rgd_copy.wait_recv()
-
-    def add_down(zt):
-        m.gds[zt, c] = (m.gds[zt, c].astype(F32) + m.gdr[zt].astype(F32)).astype(BF16)
-
-    z_peers(lambda zt: (add_down(zt), sum_line_start(s.rgd, m.gds, m.gdz, zt))[0])
-    sum_line_drain(s.rgd, m.gds)
-    rgu_copy.wait_recv()
+    up_gate_share = lambda zt: m.gus.at[zt, c]
 
     def add_up_gate(zt):
         def one(i):
@@ -637,9 +749,19 @@
 
         each(0, 8, one)
 
-    z_peers(lambda zt: (add_up_gate(zt), sum_line_start(s.rgu, m.gus, m.guz, zt))[0])
-    sum_line_drain(s.rgu, m.gus)
-
+    def pass_up_gate(zt, slot):
+        def one(i):
+            j = lax.div(i, 4)
+            g = lax.rem(i, 4)
+            m.gus[zt, c, j, g] = (
+                m.gus[zt, c, j, g].astype(F32) + m.guz[slot, j, g].astype(F32)
+            ).astype(BF16)
+
+        each(0, 8, one)
+
+    rgu_copy.wait_recv()
+    z_peers(add_up_gate)
+    sum_start(s.rgu, up_gate_share, m.guz)
     m.pgrad[...] = jnp.zeros_like(m.pgrad)
 
     def attend_back(i):
@@ -673,7 +795,9 @@
         seq_wait(s.dg, m.dq.at[block_rows(i, 128), gate_cols], i)
         attend_back(i)
 
-    each(1, 8, attend_back_next)
+    each(1, 4, attend_back_next)
+    sum_pass(s.rgd, down_share, m.gdz, pass_down)
+    each(4, 8, attend_back_next)
 
     m.fin0[0:32, :] = m.pgrad[...]
     for j in range(8):
@@ -693,6 +817,7 @@
 
     each(0, 8, key_value_grad)
 
+    sum_pass(s.rgu, up_gate_share, m.guz, pass_up_gate)
     def head_weight_grad(i):
         cols = pl.ds(pl.multiple_of(i * 256, 256), 256)
         m.gws[i] = tn(m.x_all[:, cols], m.dq[...]).astype(BF16)
@@ -719,6 +844,8 @@
 
     each(1, 5, token_sib)
 
+    token_share = lambda zt: m.gts.at[zt, c]
+
     def token_line(step):
         zt = lax.rem(z + step, 4)
         mine = token_grad(2 * zt + c)
@@ -726,11 +853,12 @@
             m.gtr.at[zt], m.gtr.at[zt], s.gt[0].at[4 + zt], s.gt[1].at[4 + zt], (a, sib)
         ).wait_recv()
         m.gts[zt, c] = (mine + m.gtr[zt].astype(F32)).astype(BF16)
-        copy(
-            m.gts.at[zt, c], m.yrecv.at[z], s.gt[0].at[zt], s.gt[1].at[z], (a, 2 * zt + c)
-        ).start()
+
+    def pass_token(zt, slot):
+        m.gts[zt, c] = (m.gts[zt, c].astype(F32) + m.yrecv[slot].astype(F32)).astype(BF16)
 
     each(1, 4, token_line)
+    sum_start(s.gt, token_share, m.yrecv)
     m.own[...] = token_grad(b)
     finals.append(
         lambda: each(
@@ -740,20 +868,35 @@
             ).wait_send(),
         )
     )
-    finals.append(
-        lambda: z_peers(
-            lambda zt: copy(
-                m.yrecv.at[zt], m.yrecv.at[zt], s.gt[0].at[zt], s.gt[1].at[zt], (a, 2 * zt + c)
-            ).wait_send()
-        )
-    )
 
     xy_peers(lambda p: xy_wait(s.fin1, m.fin1.at[p], p))
     m.fin2s[...] = (m.fin1[0] + m.fin1[1]) + (m.fin1[2] + m.fin1[3])
-    m.fin2[b] = m.fin2s[...]
-    seq_peers(lambda p: seq_start(s.fin2, m.fin2s, m.fin2.at[b], p))
-    seq_drain(s.fin2, m.fin2s)
-
+    m.fin2[b] = m.fin2s[32:48, :]
+    seq_peers(lambda p: seq_start(s.fin2, m.fin2s.at[pl.ds(32, 16), :], m.fin2.at[b], p))
+    seq_drain(s.fin2, m.fin2.at[0])
+    holder = 2 * a + lax.div(b, 4)
+    keeps = lambda p: (lax.div(b, 2) == a) & (lax.div(p, 4) == c)
+
+    def pers_send(p):
+        @pl.when(keeps(p))
+        def _():
+            copy(
+                m.fin2s.at[pl.ds(0, 32), :], m.pers, s.pers[0].at[p], s.pers[1].at[0], (a, p)
+            ).start()
+
+    def pers_drain(p):
+        @pl.when(keeps(p))
+        def _():
+            copy(m.pers, m.pers, s.pers[0].at[p], s.pers[1].at[0], (a, p)).wait_send()
+
+    seq_peers(pers_send)
+    finals.append(lambda: seq_peers(pers_drain))
+
+    @pl.when(holder == b)
+    def _():
+        m.pers[...] = m.fin2s[0:32, :]
+
+    sum_pass(s.gt, token_share, m.yrecv, pass_token)
     xy_peers(lambda p: xy_wait(s.gw, m.gwr.at[p], p))
     a1, a2, a3 = lax.rem(a + 1, 4), lax.rem(a + 2, 4), lax.rem(a + 3, 4)
 
@@ -786,16 +929,13 @@
     rgo_copy = copy(m.gos.at[:, 1 - c], m.gor, s.rgo[0].at[4], s.rgo[1].at[4], (a, sib))
     rgo_copy.start()
 
-    z1, z2, z3 = lax.rem(z + 1, 4), lax.rem(z + 2, 4), lax.rem(z + 3, 4)
-    z_peers(lambda zs: sum_line_wait(s.rgu, m.guz, zs))
+    sum_finish(s.rgu, up_gate_share, m.guz)
 
     def up_gate_sum(i):
         j = lax.div(i, 4)
         g = lax.rem(i, 4)
         total = m.gus[z, c, j, g].astype(F32) + m.gur[z, j, g].astype(F32)
-        total = total + m.guz[z1, j, g].astype(F32)
-        total = total + m.guz[z2, j, g].astype(F32)
-        total = total + m.guz[z3, j, g].astype(F32)
+        total = total + landed(m.guz, (j, g))
         m.gux[g, j] = total.astype(BF16)
 
     each(0, 8, up_gate_sum)
@@ -804,24 +944,24 @@
     m.guxr[a] = m.gux[a]
 
     rgo_copy.wait_recv()
+    out_share = lambda zt: m.gos.at[zt, c]
 
     def add_out(zt):
         m.gos[zt, c] = (m.gos[zt, c].astype(F32) + m.gor[zt].astype(F32)).astype(BF16)
 
-    z_peers(lambda zt: (add_out(zt), sum_line_start(s.rgo, m.gos, m.goz, zt))[0])
-    sum_line_drain(s.rgo, m.gos)
-
-    z_peers(lambda zs: sum_line_wait(s.rgd, m.gdz, zs))
+    def pass_out(zt, slot):
+        m.gos[zt, c] = (m.gos[zt, c].astype(F32) + m.goz[slot].astype(F32)).astype(BF16)
+
+    z_peers(add_out)
+    sum_start(s.rgo, out_share, m.goz)
+    sum_finish(s.rgd, down_share, m.gdz)
+    some = slice(0, share_rows)
     fd_o[...] = (
-        (m.gds[z, c, 0:share_rows, :].astype(F32) + m.gdr[z, 0:share_rows, :].astype(F32))
-        + (m.gdz[z1, 0:share_rows, :].astype(F32) + m.gdz[z2, 0:share_rows, :].astype(F32))
-    ) + m.gdz[z3, 0:share_rows, :].astype(F32)
-
-    z_peers(
-        lambda zs: copy(
-            m.yrecv.at[zs], m.yrecv.at[zs], s.gt[0].at[zs], s.gt[1].at[zs], (a, 2 * zs + c)
-        ).wait_recv()
-    )
+        m.gds[z, c, some, :].astype(F32) + m.gdr[z, some, :].astype(F32)
+    ) + landed(m.gdz, (some, slice(None)))
+    sum_pass(s.rgo, out_share, m.goz, pass_out)
+
+    sum_finish(s.gt, token_share, m.yrecv)
     copy(
         m.gtr.at[z], m.gtr.at[z], s.gt[0].at[4 + z], s.gt[1].at[4 + z], (a, sib)
     ).wait_recv()
@@ -830,43 +970,69 @@
         rows = block_rows(i, 32)
         total = m.dout[rows, :] + m.own[rows, :]
         total = total + m.gtr[z, rows, :].astype(F32)
-        total = total + m.yrecv[z1, rows, :].astype(F32)
-        total = total + m.yrecv[z2, rows, :].astype(F32)
-        gtok_o[rows, :] = total + m.yrecv[z3, rows, :].astype(F32)
+        gtok_o[rows, :] = total + landed(m.yrecv, (rows, slice(None)))
 
     each(0, 4, token_sum)
 
     seq_peers(lambda p: seq_wait(s.gwa, m.gar.at[p], p))
-    for head in range(8):
-        cols = slice(head * 128, head * 128 + 128)
-        gq_o[:, cols] = m.gar[head, :, 0:128].astype(F32)
-        gk_o[:, cols] = m.gar[head, :, 128:256].astype(F32)
-        gv_o[:, cols] = m.gar[head, :, 256:384].astype(F32)
-        gwg_o[:, cols] = m.gar[head, :, 384:512].astype(F32)
+    gar_o[...] = m.gar[...]
 
     xy_peers(lambda p: xy_wait(s.gfx, m.guxr.at[p], p))
-    for part in range(4):
-        fg_o[:, part * hidden : (part + 1) * hidden] = m.guxr[part, 0, :, 0:hidden].astype(F32)
-        fu_o[:, part * hidden : (part + 1) * hidden] = m.guxr[part, 1, :, 0:hidden].astype(F32)
-
-    z_peers(lambda zs: sum_line_wait(s.rgo, m.goz, zs))
-    gwo_o[...] = (
-        (m.gos[z, c].astype(F32) + m.gor[z].astype(F32))
-        + (m.goz[z1].astype(F32) + m.goz[z2].astype(F32))
-    ) + m.goz[z3].astype(F32)
+    gux_o[...] = m.guxr[...]
+
+    sum_finish(s.rgo, out_share, m.goz)
+    gwo_o[...] = (m.gos[z, c].astype(F32) + m.gor[z].astype(F32)) + landed(m.goz, ())
 
     seq_peers(lambda p: seq_wait(s.fin2, m.fin2.at[p], p))
-    everything = jnp.sum(m.fin2[:, 32:48, :], axis=0)
+    everything = jnp.sum(m.fin2[...], axis=0)
     fin_o[0:8, :] = everything[0:8, :]
     loss = jnp.sum(everything[8:9, :]) / (2.0 * width * valid_total)
     fin_o[8:16, :] = jnp.full((8, 128), loss, F32)
-    pers_o[...] = m.fin2[2 * a + lax.div(b, 4), 0:32, :]
+
+    @pl.when(holder != b)
+    def _():
+        copy(m.pers, m.pers, s.pers[0].at[0], s.pers[1].at[0], (a, holder)).wait_recv()
+
+    pers_o[...] = m.pers[...]
 
     rgd_copy.wait_send()
     rgu_copy.wait_send()
     rgo_copy.wait_send()
     for last in finals:
         last()
+
+
+def finish_kernel(
+    width, hidden, out, gtok, gar, gwo, fin, pers, gux, fd,
+    out_o, loss_o, gtok_o, gq_o, gk_o, gv_o, gwo_o, gwg_o, pk_o, pv_o, gain_o, fg_o, fu_o, fd_o,
+):
+    a = lax.axis_index("head")
+    b = lax.axis_index("seq")
+    quarter = lax.rem(b, 4)
+
+    def lanes(value):
+        picked = value[:, 0:32]
+        for j in range(1, 4):
+            picked = jnp.where(quarter == j, value[:, 32 * j : 32 * j + 32], picked)
+        return picked
+
+    out_o[...] = out[...]
+    gtok_o[...] = gtok[...]
+    gwo_o[...] = gwo[...]
+    fd_o[...] = fd[...]
+    loss_o[...] = fin[8:9, 0:1]
+    pk_o[...] = lanes(pers[0:16, :])
+    pv_o[...] = lanes(pers[16:32, :])
+    gain_o[...] = lanes(fin[pl.ds(2 * a + lax.div(b, 4), 1), :])
+    for head in range(8):
+        cols = slice(head * 128, head * 128 + 128)
+        gq_o[:, cols] = gar[head, :, 0:128].astype(F32)
+        gk_o[:, cols] = gar[head, :, 128:256].astype(F32)
+        gv_o[:, cols] = gar[head, :, 256:384].astype(F32)
+        gwg_o[:, cols] = gar[head, :, 384:512].astype(F32)
+    for part in range(4):
+        fg_o[:, part * hidden : (part + 1) * hidden] = gux[part, 0, :, 0:hidden].astype(F32)
+        fu_o[:, part * hidden : (part + 1) * hidden] = gux[part, 1, :, 0:hidden].astype(F32)
 
 
 def local_block(
@@ -878,23 +1044,6 @@
     hidden = ff_gate.shape[1] // 4
     pad = -(-hidden // 256) * 256
     share = ff_down.shape[0]
-    a = lax.axis_index("head")
-    b = lax.axis_index("seq")
-    place = a * 8 + b
-    lanes = (jnp.arange(128) // 32) == lax.rem(b, 4)
-    spread = lambda v: jnp.where(lanes, jnp.tile(v, (1, 4)), jnp.zeros((), v.dtype))
-    rates = jnp.transpose(jnp.log(retention), (0, 2, 1))
-    line = lambda v: jnp.broadcast_to(v[None], (4, 1, 128))
-    tile = jnp.concatenate(
-        [
-            rates,
-            line(valid.astype(F32)),
-            line(spread(norm_gain.astype(F32)[None])),
-            jnp.zeros((4, 4, 128), F32),
-        ],
-        axis=1,
-    )
-    persist = spread(jnp.concatenate([persist_keys, persist_values], axis=0))
     table = scratch_table(width, block, hidden, pad, length)
     names = tuple(table)
     vmem = pl.BlockSpec(memory_space=pltpu.VMEM)
@@ -902,15 +1051,11 @@
     outs = (
         shape((block, width), BF16),
         shape((block, width), F32),
-        shape((32, width), F32),
-        shape((32, width), F32),
-        shape((32, width), F32),
-        shape((32, width), F32),
+        shape((8, 32, 512), BF16),
         shape((32, width), F32),
         shape((16, 128), F32),
         shape((32, 128), F32),
-        shape((32, 4 * hidden), F32),
-        shape((32, 4 * hidden), F32),
+        shape((4, 2, 32, pad), BF16),
         shape((share, width), F32),
     )
     scratch = [pltpu.VMEM(*table[name]) for name in names]
@@ -919,7 +1064,7 @@
     result = pl.pallas_call(
         functools.partial(block_kernel, names, width, hidden, doc_starts.shape[1]),
         out_shape=outs,
-        in_specs=[vmem] * 13 + [pl.BlockSpec(memory_space=pltpu.SMEM)],
+        in_specs=[vmem] * 15 + [pl.BlockSpec(memory_space=pltpu.SMEM)],
         out_specs=[vmem] * len(outs),
         scratch_shapes=scratch,
         compiler_params=pltpu.CompilerParams(
@@ -927,16 +1072,27 @@
         ),
         name="block",
     )(
-        tokens[0], w_query, w_key, w_value, w_out, w_gate, ff_gate, ff_up,
-        jnp.pad(ff_down, ((0, 96 - share), (0, 0))), teacher[0], tile, persist,
-        valid.astype(F32).reshape(block, 1), doc_starts,
-    )
-    (out, gtok, gq, gk, gv, gwo, gwg, fin, pers, fg, fu, fd) = result
-    own = lax.dynamic_slice_in_dim(pers, lax.rem(b, 4) * 32, 32, 1)
-    gain = lax.dynamic_slice_in_dim(fin[0:8].reshape(width), place * 32, 32, 0)
+        tokens[0], w_query, w_key, w_value, w_out, w_gate, ff_gate, ff_up, ff_down, teacher[0],
+        jnp.transpose(retention, (0, 2, 1)), persist_keys, persist_values, norm_gain[None],
+        valid, doc_starts,
+    )
+    square = shape((32, width), F32)
+    wide = shape((32, 4 * hidden), F32)
+    finals = (
+        outs[0], shape((1, 1), F32), outs[1], square, square, square, square, square,
+        shape((P_SIZE, 32), F32), shape((P_SIZE, 32), F32), shape((1, 32), F32), wide, wide,
+        outs[7],
+    )
+    done = pl.pallas_call(
+        functools.partial(finish_kernel, width, hidden),
+        out_shape=finals,
+        in_specs=[vmem] * len(outs),
+        out_specs=[vmem] * len(finals),
+        name="finish",
+    )(*result)
+    (out, loss, gtok, gq, gk, gv, gwo, gwg, gpk, gpv, gain, fg, fu, fd) = done
     return (
-        out[None], fin[8, 0], gtok[None], gq, gk, gv, gwo, gwg, own[:P_SIZE], own[P_SIZE:],
-        gain, fg, fu, fd,
+        out[None], loss[0, 0], gtok[None], gq, gk, gv, gwo, gwg, gpk, gpv, gain[0], fg, fu, fd,
     )
 
 

time: 296 us -> 236 us (0.80)
  Pallas kernels: 275 us -> 235 us
  local copies, waits for them, and re-layouts: 16.8 us -> 0 us
    pallas_call x1, Pallas kernels: 275 us -> 232 us  [local_block(): pl.pallas_call(functools.partial(block_kernel, names, width, hidden, doc_...]
    unnamed x30 -> x0, local copies, waits for them, and re-layouts: 9.83 us -> none
    pallas_call x0 -> x1, Pallas kernels: none -> 3.19 us  [local_block(): pl.pallas_call(functools.partial(finish_kernel, width, hidden), out_shape...]
where the time goes in v2:
time: 236 us
  Pallas kernels  235 us (100%)
    pallas_call x1, Pallas kernels, local_block(): pl.pallas_call(functools.partial(block_kernel, names, width, hidden, doc_...  232 us

profile of v2, /device:TPU:0, one launch (start us, length us, event | category | flops | bytes accessed | tf_op | source)
XLA Modules:
  0.0 235.6 jit_solution(4190956396244065364)
XLA Ops:
  0.7 231.8 %block.1 = (bf16[128,1024]{1,0:T(8,128)(2,1)}, f32[128,1024]{1,0:T(8,128)}, bf16[8,32,512]{2,1,0:T(8,128)(2,1)}, f32[32,1024]{1,0:T(8,128)}, f32[16,128]{1,0:T(8...) custom-call(bf16[128,1024]{1,0:T(8,128)(2,1)} %bitcast.8, ...), custom_call_target="tpu_custom_call" | custom-call | tf_op jit(solution)/shard_map/block/pallas_call | solution.py:1064
  232.4 3.2 %finish.1 = (bf16[128,1024]{1,0:T(8,128)(2,1)}, f32[1,1]{1,0:T(1,128)}, f32[128,1024]{1,0:T(8,128)}, f32[32,1024]{1,0:T(8,128)}, f32[32,1024]{1,0:T(8,128)}, /*i...) custom-call(bf16[128,1024]{1,0:T(8,128)(2,1)} %get-tuple-element.36., ...), custom_call_target="tpu_custom_call" | custom-call | tf_op jit(solution)/shard_map/finish/pallas_call | solution.py:1086

commit v3 on v2

--- a/solution.py
+++ b/solution.py
@@ -67,7 +67,7 @@
     w1=8, t2=8, p2=8, x=8, wo=8, fg=8, fd=8, fu=8, gp=8, mx=8, dm=8, dg=8, rgu=8, rgd=8, rgo=8,
     gt=8, gwa=8, fin2=8, pers=8,
 )
-XY_FLAGS = dict(t1=4, p1=4, w2=4, fx=4, wox=4, sc=4, y=4, df=4, ds=4, gwo=4, gw=4, gfx=4, fin1=4)
+XY_FLAGS = dict(t1=4, p1=4, w2=4, fx=4, wox=4, sc=8, y=8, df=8, ds=8, gwo=4, gw=4, gfx=4, fin1=4)
 FLAGS = SEQ_FLAGS | XY_FLAGS
 
 
@@ -89,7 +89,7 @@
         fgu=((2, 4, 256, hidden_pad), BF16),
         fdp=((8, 96, width), BF16),
         ffd=((hidden_pad, width), BF16),
-        wo_all=((width, width), BF16),
+        wo_all=((4, 4, 2, 32, width), BF16),
         q=((length, HD), BF16),
         k=((length, HD), BF16),
         v=((length, HD), BF16),
@@ -226,32 +226,42 @@
     def pass_copy(pair, src, dst, zs):
         return copy(src, dst, pair[0].at[4 + zs], pair[1].at[4 + zs], (a, sib))
 
-    def gather_start(pair, src, view):
-        line_copy(pair, src, view(b), mirror).start()
-        line_copy(pair, src, view(b), near).start()
+    def line_start(pair, src, place):
+        line_copy(pair, src, place(z), mirror).start()
+        line_copy(pair, src, place(z), near).start()
 
         @pl.when(jnp.logical_not(inner_chip))
         def _():
-            line_copy(pair, src, view(b), across).start()
-
-        pass_copy(pair, src, view(b), z).start()
+            line_copy(pair, src, place(z), across).start()
+
         finals.append(lambda: z_peers(lambda zt: line_copy(pair, src, src, zt).wait_send()))
-        finals.append(lambda: each(0, 4, lambda zs: pass_copy(pair, src, src, zs).wait_send()))
-
-    def gather_line(pair, view, zs):
-        block = view(2 * zs + c)
+
+    def line_wait(pair, place, zs):
+        block = place(zs)
         copy(block, block, pair[0].at[zs], pair[1].at[zs], (a, 2 * zs + c)).wait_recv()
-        pass_copy(pair, block, block, zs).start()
-
-    def gather_mirror(pair, view):
-        gather_line(pair, view, mirror)
-        block = view(2 * mirror + c)
+
+    def line_hand_on(pair, place):
+        block = place(mirror)
 
         @pl.when(inner_chip)
         def _():
             copy(
                 block, block, pair[0].at[across], pair[1].at[mirror], (a, 2 * near + c)
             ).start()
+
+    def gather_start(pair, src, view):
+        line_start(pair, src, lambda zs: view(2 * zs + c))
+        pass_copy(pair, src, view(b), z).start()
+        finals.append(lambda: each(0, 4, lambda zs: pass_copy(pair, src, src, zs).wait_send()))
+
+    def gather_line(pair, view, zs):
+        block = view(2 * zs + c)
+        line_wait(pair, lambda _: block, zs)
+        pass_copy(pair, block, block, zs).start()
+
+    def gather_mirror(pair, view):
+        gather_line(pair, view, mirror)
+        line_hand_on(pair, lambda zs: view(2 * zs + c))
 
     def gather_pass(pair, view, zs):
         block = view(2 * zs + 1 - c)
@@ -274,7 +284,7 @@
     piece = pl.ds(pl.multiple_of(a * 256 + b * 32, 32), 32)
     m.x_all[own_rows, :] = tok[...]
     m.wqk[piece, :] = m.wcs[b]
-    m.wo_all[piece, :] = wo[...]
+    m.wo_all[a, z, c] = wo[...]
     down = fdi[...].astype(F32)
     m.fdp[b] = jnp.concatenate(
         [down, jnp.zeros((96 - down.shape[0], width), F32)], axis=0
@@ -306,6 +316,8 @@
     seq_peers(lambda p: seq_start(s.w1, m.wcs.at[p], m.wqk.at[piece, :], p))
     x_view = lambda i: m.x_all.at[block_rows(i, 128), :]
     gather_start(s.x, tok, x_view)
+    wo_place = lambda zs: m.wo_all.at[a, zs, c]
+    line_start(s.wo, wo, wo_place)
     xy_peers(lambda p: xy_start(s.fx, m.fs.at[p], m.fgu.at[:, a, slot32, :], p))
     xy_drain(s.t1, m.tile.at[0])
     xy_drain(s.p1, m.pin)
@@ -358,15 +370,11 @@
 
     head_cols = pl.ds(pl.multiple_of(b * 128, 128), 128)
 
-    def send_gate(i):
-        seq_start(s.gp, m.gps.at[block_rows(i, 128), :], m.gp.at[:, head_cols], i)
-
     xy_peers(lambda p: xy_wait(s.w2, quarter(p), p))
     project(b)
     m.gp[:, head_cols] = m.gps[own_rows, :]
     gather_pass(s.x, x_view, z)
     project(sib)
-    send_gate(sib)
 
     def arrived_line(step):
         zs = lax.rem(z + step, 4)
@@ -374,31 +382,40 @@
         project(2 * zs + c)
         send_gate(2 * zs + c)
 
-    def arrived(i):
-        project(i)
-        send_gate(i)
-
     gather_mirror(s.x, x_view)
-    arrived(2 * mirror + c)
+    project(2 * mirror + c)
     gather_line(s.x, x_view, near)
-    arrived(2 * near + c)
+    project(2 * near + c)
     gather_line(s.x, x_view, across)
 
     def arrived_pass(step):
         zs = lax.rem(z + step, 4)
         gather_pass(s.x, x_view, zs)
-        arrived(2 * zs + 1 - c)
-
-    wo_view = lambda i: m.wo_all.at[pl.ds(pl.multiple_of(a * 256 + i * 32, 32), 32), :]
-    gather_start(s.wo, wo, wo_view)
+        project(2 * zs + 1 - c)
+
+    wo_half = lambda i: m.wo_all.at[i, :, c]
+    line_wait(s.wo, wo_place, mirror)
+    line_hand_on(s.wo, wo_place)
+    line_wait(s.wo, wo_place, near)
+    line_wait(s.wo, wo_place, across)
+    xy_peers(lambda p: xy_start(s.wox, wo_half(a), wo_half(a), p))
+    xy_drain(s.wox, wo_half(a))
+    wo_pass = lambda i, block: copy(
+        block, block, s.wo[0].at[4 + i], s.wo[1].at[4 + i], (a, sib)
+    )
+    wo_pass(a, wo_half(a)).start()
+    finals.append(lambda: each(0, 4, lambda i: wo_pass(i, wo_half(i)).wait_send()))
+    project(2 * across + c)
+    each(1, 4, arrived_pass)
+    seq_peers(
+        lambda p: seq_start(s.gp, m.gps.at[block_rows(p, 128), :], m.gp.at[:, head_cols], p)
+    )
+    seq_drain(s.gp, m.gps.at[own_rows, :])
     xy_peers(lambda p: xy_wait(s.fx, m.fgu.at[:, p, slot32, :], p))
     fg_view = lambda i: m.fgu.at[0, :, block_rows(i, 32), :]
     fu_view = lambda i: m.fgu.at[1, :, block_rows(i, 32), :]
     fd_view = lambda i: m.fdp.at[i]
     gather_start(s.fg, fg_view(b), fg_view)
-    arrived(2 * across + c)
-    each(1, 4, arrived_pass)
-    seq_drain(s.gp, m.gps.at[own_rows, :])
 
     seq_peers(lambda p: seq_wait(s.t2, m.t2.at[p], p))
     seq_peers(persist_wait)
@@ -428,19 +445,27 @@
     eye = (col_id == row_id).astype(F32)
     m.rcol[...] = nt_exact(eye, running)
 
-    key_pos = lax.broadcasted_iota(jnp.int32, (128, length), 1)
     local_pos = lax.broadcasted_iota(jnp.int32, (128, 1), 0)
     lane8 = lax.broadcasted_iota(jnp.int32, (128, 8), 1)
 
-    def attend(i):
+    m.probs[...] = jnp.zeros_like(m.probs)
+    m.both[...] = jnp.zeros_like(m.both)
+
+    def by_extent(i, body):
+        for j in range(4):
+            pl.when(lax.div(i, 2) == j)(lambda j=j: body(i, 256 * (j + 1)))
+
+    def attend_keys(i, extent):
         rows = block_rows(i, 128)
+        keys = slice(0, extent)
         query = m.q[rows, :]
-        raw = nt(query, m.k[...])
+        raw = nt(query, m.k[keys, :])
         pos = i * 128 + local_pos
         begin = jnp.zeros_like(pos)
         for j in range(ndoc):
             start = docs[a, j]
             begin = jnp.where(start <= pos, jnp.maximum(begin, start), begin)
+        key_pos = lax.broadcasted_iota(jnp.int32, (128, extent), 1)
         allowed = (key_pos <= pos) & (key_pos >= begin)
         scores = jnp.where(allowed, raw * scale, MASKED)
         fixed = nt(query, m.fkv[0:16, :]) * scale
@@ -456,30 +481,24 @@
         fixed_prob = (fixed_weight * share).astype(BF16)
         reach = jnp.sum(jnp.where(lane8 == i, m.rcol[...], 0.0), axis=1, keepdims=True)
         kept = jnp.where(
-            allowed, jnp.exp(jnp.minimum(reach - m.rrow[...], 0.0)) * mem_scale, 0.0
+            allowed, jnp.exp(jnp.minimum(reach - m.rrow[:, keys], 0.0)) * mem_scale, 0.0
         )
         joint = (prob + kept * raw).astype(BF16)
-        m.probs[rows, :] = prob.astype(BF16)
-        m.decay[rows, :] = kept.astype(BF16)
-        m.both[rows, :] = joint
+        m.probs[rows, keys] = prob.astype(BF16)
+        m.decay[rows, keys] = kept.astype(BF16)
+        m.both[rows, keys] = joint
         m.fprobs[rows, :] = fixed_prob
-        mixed = nn(joint, m.v[...]) + nn(fixed_prob, m.fkv[16:32, :])
+        mixed = nn(joint, m.v[keys, :]) + nn(fixed_prob, m.fkv[16:32, :])
         m.mxs[rows, :] = mixed.astype(BF16)
+
+    attend = lambda i: by_extent(i, attend_keys)
 
     def attend_send(step):
         i = lax.rem(b + step, 8)
         attend(i)
         seq_start(s.mx, m.mxs.at[block_rows(i, 128), :], m.mx.at[:, head_cols], i)
 
-    each(1, 4, attend_send)
-    gather_mirror(s.wo, wo_view)
-    gather_line(s.wo, wo_view, near)
-    gather_line(s.wo, wo_view, across)
-    each(4, 6, attend_send)
-    each(0, 4, lambda zs: gather_pass(s.wo, wo_view, zs))
-    wo_quarter = lambda i: m.wo_all.at[block_rows(i, 256), :]
-    xy_peers(lambda p: xy_start(s.wox, wo_quarter(a), wo_quarter(a), p))
-    xy_drain(s.wox, wo_quarter(a))
+    each(1, 6, attend_send)
     each(6, 7, attend_send)
     gather_mirror(s.fg, fg_view)
     gather_start(s.fu, fu_view(b), fu_view)
@@ -489,10 +508,55 @@
     m.mx[:, head_cols] = m.mxs[own_rows, :]
 
     seq_peers(lambda p: seq_wait(s.gp, m.gp.at[:, pl.ds(pl.multiple_of(p * 128, 128), 128)], p))
-    xy_peers(lambda p: xy_wait(s.wox, wo_quarter(p), p))
+    def wo_arrived(p):
+        xy_wait(s.wox, wo_half(p), p)
+        wo_pass(p, wo_half(p)).start()
+
+    xy_peers(wo_arrived)
+    each(0, 4, lambda i: wo_pass(i, m.wo_all.at[i, :, 1 - c]).wait_recv())
     seq_peers(lambda p: seq_wait(s.mx, m.mx.at[:, pl.ds(pl.multiple_of(p * 128, 128), 128)], p))
 
-    m.br[...] = nn(m.mx[...], m.wo_all[...])
+    out_w = lambda: m.wo_all[...].reshape(width, width)
+    m.br[...] = nn(m.mx[...], out_w())
+
+    half_row = lambda i: pl.ds(
+        pl.multiple_of((4 * lax.div(i, 2) + a) * 64 + lax.rem(i, 2) * 32, 32), 32
+    )
+    quad = lambda ref, h, i: ref.at[block_rows(4 * h + i, 64), :]
+
+    def half_copy(pair, src, dst, h, peer, slot):
+        return copy(src, dst, pair[0].at[4 * h + peer], pair[1].at[4 * h + slot], (peer, b))
+
+    def half_gather(pair, ref, h):
+        xy_peers(lambda p: half_copy(pair, quad(ref, h, a), quad(ref, h, a), h, p, a).start())
+        finals.append(
+            lambda: xy_peers(
+                lambda p: half_copy(pair, quad(ref, h, a), quad(ref, h, a), h, p, p).wait_send()
+            )
+        )
+
+    def half_wait(pair, ref, h):
+        xy_peers(lambda p: half_copy(pair, quad(ref, h, p), quad(ref, h, p), h, p, p).wait_recv())
+
+    def half_scatter(pair, value, h):
+        for i in range(4):
+            m.ysend[i, h * 64 : h * 64 + 64, :] = value[i * 64 : i * 64 + 64, :].astype(BF16)
+        rows = pl.ds(h * 64, 64)
+        xy_peers(
+            lambda p: half_copy(
+                pair, m.ysend.at[p, rows, :], m.yrecv.at[a, rows, :], h, p, a
+            ).start()
+        )
+
+    def half_sent(pair, h):
+        rows = pl.ds(h * 64, 64)
+        block = lambda p: m.ysend.at[p, rows, :]
+        xy_peers(lambda p: half_copy(pair, block(p), block(p), h, p, p).wait_send())
+
+    def half_land(pair, h):
+        rows = pl.ds(h * 64, 64)
+        block = lambda p: m.yrecv.at[p, rows, :]
+        xy_peers(lambda p: half_copy(pair, block(p), block(p), h, p, p).wait_recv())
 
     def normalise(i):
         rows = block_rows(i, 32)
@@ -501,14 +565,14 @@
         inv = lax.rsqrt(jnp.mean(hidden_rows * hidden_rows, axis=1, keepdims=True) + EPSILON)
         m.hid[rows, :] = hidden_rows
         m.inv[rows, :] = jnp.broadcast_to(inv, (32, 128))
-        m.sc[pl.ds(pl.multiple_of(a * 128 + i * 32, 32), 32), :] = (
+        m.sc[half_row(i), :] = (
             hidden_rows * inv * m.gain[...]
         ).astype(BF16)
 
-    each(0, 4, normalise)
-    quad = lambda ref, i: ref.at[block_rows(i, 128), :]
-    xy_peers(lambda p: xy_start(s.sc, quad(m.sc, a), quad(m.sc, a), p))
-    xy_drain(s.sc, quad(m.sc, a))
+    each(0, 2, normalise)
+    half_gather(s.sc, m.sc, 0)
+    each(2, 4, normalise)
+    half_gather(s.sc, m.sc, 1)
 
     gather_mirror(s.fu, fu_view)
     gather_start(s.fd, fd_view(b), fd_view)
@@ -519,7 +583,7 @@
     gather_line(s.fu, fu_view, near)
     gather_line(s.fu, fu_view, across)
     each(0, 4, lambda zs: gather_pass(s.fu, fu_view, zs))
-    xy_peers(lambda p: xy_wait(s.sc, quad(m.sc, p), p))
+    half_wait(s.sc, m.sc, 0)
 
     gate_w = lambda: m.fgu[0].reshape(width, pad)
     up_w = lambda: m.fgu[1].reshape(width, pad)
@@ -533,7 +597,7 @@
         m.uact[rows, :] = up_act
         m.inner[rows, :] = (gate_act * jax.nn.sigmoid(gate_act) * up_act).astype(BF16)
 
-    each(0, 2, feed)
+    feed(0)
     gather_line(s.fd, fd_view, near)
     gather_line(s.fd, fd_view, across)
     each(0, 4, lambda zs: gather_pass(s.fd, fd_view, zs))
@@ -544,14 +608,15 @@
         ).astype(BF16)
     m.ffd[hidden:pad, :] = jnp.zeros((pad - hidden, width), BF16)
 
-    def feed_out(step):
-        i = lax.rem(a + step, 4)
-        m.ysend[i] = nn(m.inner[block_rows(i, 128), :], m.ffd[...]).astype(BF16)
-        xy_start(s.y, m.ysend.at[i], m.yrecv.at[a], i)
-
-    each(1, 4, feed_out)
-    m.own[...] = nn(m.inner[block_rows(a, 128), :], m.ffd[...])
-    xy_peers(lambda p: xy_wait(s.y, m.yrecv.at[p], p))
+    def feed_out(h):
+        half_scatter(s.y, nn(m.inner[block_rows(h, 256), :], m.ffd[...]), h)
+        m.own[block_rows(h, 64), :] = nn(m.inner[block_rows(4 * h + a, 64), :], m.ffd[...])
+
+    feed_out(0)
+    half_wait(s.sc, m.sc, 1)
+    feed(1)
+    feed_out(1)
+    half_land(s.y, 0)
 
     token_total = float(4 * length)
     m.fin0[...] = jnp.zeros_like(m.fin0)
@@ -568,17 +633,19 @@
         counted = m.vcol[rows, :] * error
         grad = counted * (token_total / valid_total)
         m.dout[rows, :] = grad
-        m.df[pl.ds(pl.multiple_of(a * 128 + i * 32, 32), 32), :] = grad.astype(BF16)
+        m.df[half_row(i), :] = grad.astype(BF16)
         squares = jnp.sum(counted * error, axis=0, keepdims=True)
         lanes = squares[:, 0:128]
         for j in range(1, width // 128):
             lanes = lanes + squares[:, j * 128 : j * 128 + 128]
         m.fin0[40:41, :] += lanes
 
-    each(0, 4, finish)
-    xy_peers(lambda p: xy_start(s.df, quad(m.df, a), quad(m.df, a), p))
-    xy_drain(s.df, quad(m.df, a))
-    xy_peers(lambda p: xy_wait(s.df, quad(m.df, p), p))
+    each(0, 2, finish)
+    half_gather(s.df, m.df, 0)
+    half_land(s.y, 1)
+    each(2, 4, finish)
+    half_gather(s.df, m.df, 1)
+    half_wait(s.df, m.df, 0)
 
     def feed_back(i):
         rows = block_rows(i, 256)
@@ -590,21 +657,20 @@
         ).astype(BF16)
         m.dua[rows, :] = (d_inner * gate_act * opened).astype(BF16)
 
-    each(0, 2, feed_back)
-
-    def scaled_grad(i):
-        rows = block_rows(i, 128)
-        return nt(m.dga[rows, :], gate_w()) + nt(m.dua[rows, :], up_w())
-
-    def feed_in(step):
-        i = lax.rem(a + step, 4)
-        m.ysend[i] = scaled_grad(i).astype(BF16)
-        xy_start(s.ds, m.ysend.at[i], m.yrecv.at[a], i)
-
-    xy_peers(lambda p: xy_copy(s.y, m.ysend.at[0], m.ysend.at[0], p).wait_send())
-    each(1, 4, feed_in)
-    xy_drain(s.ds, m.ysend.at[0])
-    m.own[...] = scaled_grad(a)
+    feed_back(0)
+
+    def feed_in(h):
+        rows = block_rows(h, 256)
+        half_sent(s.y, h)
+        half_scatter(s.ds, nt(m.dga[rows, :], gate_w()) + nt(m.dua[rows, :], up_w()), h)
+        rows = block_rows(4 * h + a, 64)
+        m.own[block_rows(h, 64), :] = nt(m.dga[rows, :], gate_w()) + nt(m.dua[rows, :], up_w())
+
+    feed_in(0)
+    half_wait(s.df, m.df, 1)
+    feed_back(1)
+    feed_in(1)
+    finals.append(lambda: (half_sent(s.ds, 0), half_sent(s.ds, 1)))
 
     def share_copy(pair, share, landing, slot, zt):
         return copy(share, landing.at[slot], pair[0].at[zt], pair[1].at[slot], (a, 2 * zt + c))
@@ -691,7 +757,7 @@
     z_peers(add_down)
     sum_start(s.rgd, down_share, m.gdz)
 
-    xy_peers(lambda p: xy_wait(s.ds, m.yrecv.at[p], p))
+    half_land(s.ds, 0)
     m.ggain[...] = jnp.zeros_like(m.ggain)
 
     def norm_back(i):
@@ -711,10 +777,12 @@
         m.dbr[rows, :] = (d_hidden * opened).astype(BF16)
         m.dgt[rows, :] = (d_hidden * m.br[rows, :] * opened * (1.0 - opened)).astype(BF16)
 
-    each(0, 4, norm_back)
+    each(0, 2, norm_back)
+    half_land(s.ds, 1)
+    each(2, 4, norm_back)
     gate_cols = pl.ds(384, 128)
     cols_of = lambda i: pl.ds(pl.multiple_of(i * 128, 128), 128)
-    m.dms[...] = nt(m.dbr[...], m.wo_all[...]).astype(BF16)
+    m.dms[...] = nt(m.dbr[...], out_w()).astype(BF16)
     seq_peers(lambda p: seq_start(s.dm, m.dms.at[:, cols_of(p)], m.dm.at[own_rows, :], p))
     seq_peers(
         lambda p: seq_start(s.dg, m.dgt.at[:, cols_of(p)], m.dq.at[own_rows, gate_cols], p)
@@ -764,11 +832,12 @@
     sum_start(s.rgu, up_gate_share, m.guz)
     m.pgrad[...] = jnp.zeros_like(m.pgrad)
 
-    def attend_back(i):
+    def attend_back_keys(i, extent):
         rows = block_rows(i, 128)
+        keys = slice(0, extent)
         d_mixed = m.dm[rows, :]
-        d_joint = nt(d_mixed, m.v[...])
-        prob = m.probs[rows, :].astype(F32)
+        d_joint = nt(d_mixed, m.v[keys, :])
+        prob = m.probs[rows, keys].astype(F32)
         turned = prob * d_joint
         fixed_prob = m.fprobs[rows, :]
         fixed_full = fixed_prob.astype(F32)
@@ -777,15 +846,17 @@
             fixed_turned, axis=1, keepdims=True
         )
         d_raw = (
-            scale * (turned - prob * delta) + m.decay[rows, :].astype(F32) * d_joint
+            scale * (turned - prob * delta) + m.decay[rows, keys].astype(F32) * d_joint
         ).astype(BF16)
-        m.probs[rows, :] = d_raw
+        m.probs[rows, keys] = d_raw
         d_fixed = (fixed_turned - fixed_full * delta).astype(BF16)
         m.dq[rows, 0:128] = (
-            nn(d_raw, m.k[...]) + scale * nn(d_fixed, m.fkv[0:16, :])
+            nn(d_raw, m.k[keys, :]) + scale * nn(d_fixed, m.fkv[0:16, :])
         ).astype(BF16)
         m.pgrad[0:16, :] += scale * tn(d_fixed, m.q[rows, :])
         m.pgrad[16:32, :] += tn(fixed_prob, d_mixed)
+
+    attend_back = lambda i: by_extent(i, attend_back_keys)
 
     attend_back(b)
 

time: 236 us -> 226 us (0.958)
  Pallas kernels: 235 us -> 225 us
    pallas_call x1, Pallas kernels: 232 us -> 222 us  [local_block(): pl.pallas_call(functools.partial(block_kernel, names, width, hidden, doc_...]
where the time goes in v3:
time: 226 us
  Pallas kernels  225 us (100%)
    pallas_call x1, Pallas kernels, local_block(): pl.pallas_call(functools.partial(block_kernel, names, width, hidden, doc_...  222 us

profile of v3, /device:TPU:0, one launch (start us, length us, event | category | flops | bytes accessed | tf_op | source)
XLA Modules:
  0.0 226.1 jit_solution(8286425071909715101)
XLA Ops:
  0.7 222.2 %block.1 = (bf16[128,1024]{1,0:T(8,128)(2,1)}, f32[128,1024]{1,0:T(8,128)}, bf16[8,32,512]{2,1,0:T(8,128)(2,1)}, f32[32,1024]{1,0:T(8,128)}, f32[16,128]{1,0:T(8...) custom-call(bf16[128,1024]{1,0:T(8,128)(2,1)} %bitcast.8, ...), custom_call_target="tpu_custom_call" | custom-call | tf_op jit(solution)/shard_map/block/pallas_call | solution.py:1135
  222.9 3.2 %finish.1 = (bf16[128,1024]{1,0:T(8,128)(2,1)}, f32[1,1]{1,0:T(1,128)}, f32[128,1024]{1,0:T(8,128)}, f32[32,1024]{1,0:T(8,128)}, f32[32,1024]{1,0:T(8,128)}, /*i...) custom-call(bf16[128,1024]{1,0:T(8,128)(2,1)} %get-tuple-element.36., ...), custom_call_target="tpu_custom_call" | custom-call | tf_op jit(solution)/shard_map/finish/pallas_call | solution.py:1157

commit v4 on v3

--- a/solution.py
+++ b/solution.py
@@ -64,10 +64,13 @@
 
 
 SEQ_FLAGS = dict(
-    w1=8, t2=8, p2=8, x=8, wo=8, fg=8, fd=8, fu=8, gp=8, mx=8, dm=8, dg=8, rgu=8, rgd=8, rgo=8,
-    gt=8, gwa=8, fin2=8, pers=8,
+    w1=8, t2=8, p2=8, x=8, wo=8, fxg=8, fxu=8, mx=8, dm=8, gxg=8, gxu=8, rgo=8, gt=8, gwa=8,
+    fin2=8, pers=8, sc=8, y=8, df=8, ds=8, fd=1, gfd=1, gos=1,
 )
-XY_FLAGS = dict(t1=4, p1=4, w2=4, fx=4, wox=4, sc=8, y=8, df=8, ds=8, gwo=4, gw=4, gfx=4, fin1=4)
+XY_FLAGS = dict(
+    t1=4, p1=4, w2=4, wox=4, fgx=4, fux=4, fdx=4, fdy=4, rg=3, ru=3, rdx=3, rdy=3, rox=3, roy=3,
+    rwx=3, rwy=3, fin1=4,
+)
 FLAGS = SEQ_FLAGS | XY_FLAGS
 
 
@@ -93,7 +96,6 @@
         q=((length, HD), BF16),
         k=((length, HD), BF16),
         v=((length, HD), BF16),
-        gps=((length, HD), BF16),
         fkv=((32, HD), BF16),
         gain=((1, width), F32),
         rrow=((1, length), F32),
@@ -102,7 +104,8 @@
         decay=((length, length), BF16),
         both=((length, length), BF16),
         fprobs=((length, P_SIZE), BF16),
-        mxs=((length, HD), BF16),
+        mgs=((length, 2 * HD), BF16),
+        mg=((8, block, 2 * HD), BF16),
         mx=((block, width), BF16),
         gp=((block, width), BF16),
         hid=((block, width), F32),
@@ -123,23 +126,29 @@
         dgt=((block, width), BF16),
         dms=((block, width), BF16),
         dm=((length, HD), BF16),
+        dgs=((8, block, 2 * HD), BF16),
+        dmg=((8, block, 2 * HD), BF16),
         dq=((length, 512), BF16),
         ggain=((1, width), F32),
-        gus=((4, 2, 2, 4, 32, hidden_pad), BF16),
-        gur=((4, 2, 4, 32, hidden_pad), BF16),
-        guz=((4, 2, 4, 32, hidden_pad), BF16),
-        gux=((4, 2, 32, hidden_pad), BF16),
-        guxr=((4, 2, 32, hidden_pad), BF16),
-        gds=((4, 2, 96, width), BF16),
-        gdr=((4, 96, width), BF16),
-        gdz=((4, 96, width), BF16),
-        gwos=((4, 256, width), BF16),
-        gwor=((4, 256, width), BF16),
-        gos=((4, 2, 32, width), BF16),
-        gor=((4, 32, width), BF16),
+        gus=((2, 4, 256, hidden_pad), BF16),
+        gpre=((2, 256, hidden_pad), BF16),
+        gland=((2, 2, 256, hidden_pad), BF16),
+        gxs=((8, 2, 32, hidden_pad), BF16),
+        gxr=((8, 2, 32, hidden_pad), BF16),
+        gds=((8, 96, width), BF16),
+        dpre=((2, 96, width), BF16),
+        dland=((2, 2, 96, width), BF16),
+        dsum=((2, 96, width), BF16),
+        dfar=((96, width), BF16),
+        gwos=((4, 4, 2, 32, width), BF16),
+        gwor=((4, 4, 32, width), BF16),
+        opre=((2, 2, 32, width), BF16),
+        oland=((2, 4, 32, width), BF16),
+        gos=((4, 32, width), BF16),
         goz=((4, 32, width), BF16),
         gws=((4, 256, 512), BF16),
-        gwr=((4, 256, 512), BF16),
+        wpre=((2, 128, 512), BF16),
+        wland=((2, 256, 512), BF16),
         gas=((8, 32, 512), BF16),
         gar=((8, 32, 512), BF16),
         gts=((4, 2, block, width), BF16),
@@ -176,6 +185,20 @@
     mirror = 3 - z
     across = 3 - near
     inner_chip = (z == 1) | (z == 2)
+    inside = lax.div(lax.rem(z, 3) + 1, 2)
+    order = (
+        near + inside * (mirror - near),
+        across + inside * (near - across),
+        mirror + inside * (across - mirror),
+    )
+    part = lax.div(b, 4)
+    mine = lax.rem(b, 4)
+    partner = 2 * near + c
+    far = b + 4 - 8 * part
+    mate, pmate, cross = lax.rem(sib, 4), lax.rem(partner, 4), lax.rem(2 * near + 1 - c, 4)
+    nx = a + 1 - 2 * lax.rem(a, 2)
+    ny = lax.rem(a + 2, 4)
+    diagonal = 3 - a
 
     def copy(src, dst, ssem, rsem, device):
         return pltpu.make_async_remote_copy(
@@ -183,89 +206,113 @@
             device_id=device, device_id_type=MESH_IDS,
         )
 
+    def sent(flag, total):
+        copy(total, total, flag, flag, (a, sib)).wait_send()
+
+    def landed_all(flag, total):
+        copy(total, total, flag, flag, (a, sib)).wait_recv()
+
     def seq_peers(body):
         each(1, 8, lambda step: body(lax.rem(b + step, 8)))
 
     def xy_peers(body):
         each(1, 4, lambda step: body(lax.rem(a + step, 4)))
 
-    def z_peers(body):
-        each(1, 4, lambda step: body(lax.rem(z + step, 4)))
-
-    def seq_copy(pair, src, dst, peer, slot=None):
-        slot = peer if slot is None else slot
-        return copy(src, dst, pair[0].at[peer], pair[1].at[slot], (a, peer))
-
     def seq_start(pair, src, dst, peer):
-        seq_copy(pair, src, dst, peer, b).start()
+        copy(src, dst, pair[0].at[0], pair[1].at[b], (a, peer)).start()
 
     def seq_wait(pair, dst, peer):
-        seq_copy(pair, dst, dst, peer).wait_recv()
-
-    def xy_copy(pair, src, dst, peer, slot=None):
-        slot = peer if slot is None else slot
-        return copy(src, dst, pair[0].at[peer], pair[1].at[slot], (peer, b))
+        landed_all(pair[1].at[peer], dst)
+
+    def all_start(pair, src, dst, peer):
+        copy(src, dst, pair[0].at[0], pair[1].at[0], (a, peer)).start()
 
     def xy_start(pair, src, dst, peer):
-        xy_copy(pair, src, dst, peer, a).start()
+        copy(src, dst, pair[0].at[0], pair[1].at[a], (peer, b)).start()
 
     def xy_wait(pair, dst, peer):
-        xy_copy(pair, dst, dst, peer).wait_recv()
+        landed_all(pair[1].at[peer], dst)
+
+    def xy_all_start(pair, src, dst, peer):
+        copy(src, dst, pair[0].at[0], pair[1].at[0], (peer, b)).start()
+
+    def all_wait(pair, total):
+        landed_all(pair[1].at[0], total)
 
     finals = []
 
-    def seq_drain(pair, view):
-        finals.append(lambda: seq_peers(lambda p: seq_copy(pair, view, view, p).wait_send()))
-
-    def xy_drain(pair, view):
-        finals.append(lambda: xy_peers(lambda p: xy_copy(pair, view, view, p).wait_send()))
+    def drain(pair, total):
+        finals.append(lambda: sent(pair[0].at[0], total))
 
     def line_copy(pair, src, dst, zt):
-        return copy(src, dst, pair[0].at[zt], pair[1].at[z], (a, 2 * zt + c))
+        return copy(src, dst, pair[0].at[0], pair[1].at[z], (a, 2 * zt + c))
 
     def pass_copy(pair, src, dst, zs):
-        return copy(src, dst, pair[0].at[4 + zs], pair[1].at[4 + zs], (a, sib))
-
-    def line_start(pair, src, place):
-        line_copy(pair, src, place(z), mirror).start()
-        line_copy(pair, src, place(z), near).start()
+        return copy(src, dst, pair[0].at[1], pair[1].at[4 + zs], (a, sib))
+
+    def line_start_far(pair, src, place, four, two):
+        @pl.when(inner_chip)
+        def _():
+            line_copy(pair, src, place(z), mirror).start()
 
         @pl.when(jnp.logical_not(inner_chip))
         def _():
             line_copy(pair, src, place(z), across).start()
 
-        finals.append(lambda: z_peers(lambda zt: line_copy(pair, src, src, zt).wait_send()))
+        def line_sent():
+            @pl.when(inner_chip)
+            def _():
+                sent(pair[0].at[0], four)
+
+            @pl.when(jnp.logical_not(inner_chip))
+            def _():
+                sent(pair[0].at[0], two)
+
+        finals.append(line_sent)
+
+    def line_start_near(pair, src, place):
+        line_copy(pair, src, place(z), near).start()
 
     def line_wait(pair, place, zs):
+        landed_all(pair[1].at[zs], place(zs))
+
+    def line_hand_on(pair, place, zs):
         block = place(zs)
-        copy(block, block, pair[0].at[zs], pair[1].at[zs], (a, 2 * zs + c)).wait_recv()
-
-    def line_hand_on(pair, place):
-        block = place(mirror)
 
         @pl.when(inner_chip)
         def _():
-            copy(
-                block, block, pair[0].at[across], pair[1].at[mirror], (a, 2 * near + c)
-            ).start()
-
-    def gather_start(pair, src, view):
-        line_start(pair, src, lambda zs: view(2 * zs + c))
-        pass_copy(pair, src, view(b), z).start()
-        finals.append(lambda: each(0, 4, lambda zs: pass_copy(pair, src, src, zs).wait_send()))
+            copy(block, block, pair[0].at[0], pair[1].at[zs], (a, 2 * near + c)).start()
 
     def gather_line(pair, view, zs):
         block = view(2 * zs + c)
         line_wait(pair, lambda _: block, zs)
         pass_copy(pair, block, block, zs).start()
 
-    def gather_mirror(pair, view):
-        gather_line(pair, view, mirror)
-        line_hand_on(pair, lambda zs: view(2 * zs + c))
-
     def gather_pass(pair, view, zs):
-        block = view(2 * zs + 1 - c)
-        pass_copy(pair, block, block, zs).wait_recv()
+        landed_all(pair[1].at[4 + zs], view(2 * zs + 1 - c))
+
+    def quad_start(pair, view, first, second):
+        block = view(a)
+        copy(block, block, pair[0].at[0], pair[1].at[0], (first, b)).start()
+        copy(block, block, pair[0].at[0], pair[1].at[1], (second, b)).start()
+
+    def quad_pass(pair, view, first, second):
+        block = view(first)
+        landed_all(pair[1].at[0], block)
+        copy(block, block, pair[0].at[0], pair[1].at[1], (second, b)).start()
+
+    def fold_start(pair, view, pre, land, first):
+        copy(view(diagonal), pre, pair[0].at[0], pair[1].at[0], (first, b)).start()
+        copy(view(first), land.at[0], pair[0].at[0], pair[1].at[1], (first, b)).start()
+
+    def fold_pass(pair, view, pre, land, add, second):
+        landed_all(pair[1].at[0], pre)
+        add(second)
+        copy(view(second), land.at[1], pair[0].at[0], pair[1].at[1], (second, b)).start()
+
+    def fold_finish(pair, land, three):
+        landed_all(pair[1].at[1], land)
+        drain(pair, three)
 
     barrier = pltpu.get_barrier_semaphore()
     seq_peers(lambda p: pl.semaphore_signal(barrier, 1, device_id=(a, p), device_id_type=MESH_IDS))
@@ -276,21 +323,16 @@
             m.wcs[head, :, place * 128 : place * 128 + 128] = weight[
                 :, head * 128 : head * 128 + 128
             ]
-    for part in range(4):
-        for place, weight in enumerate((fgi, fui)):
-            m.fs[part, place, :, 0:hidden] = weight[:, part * hidden : (part + 1) * hidden]
-            m.fs[part, place, :, hidden:pad] = jnp.zeros((32, pad - hidden), BF16)
     own_rows = block_rows(b, 128)
     piece = pl.ds(pl.multiple_of(a * 256 + b * 32, 32), 32)
     m.x_all[own_rows, :] = tok[...]
     m.wqk[piece, :] = m.wcs[b]
     m.wo_all[a, z, c] = wo[...]
     down = fdi[...].astype(F32)
-    m.fdp[b] = jnp.concatenate(
+    m.fdp[2 * a + part] = jnp.concatenate(
         [down, jnp.zeros((96 - down.shape[0], width), F32)], axis=0
     ).astype(BF16)
     slot32 = block_rows(b, 32)
-    m.fgu[:, a, slot32, :] = m.fs[a]
     row_id = lax.broadcasted_iota(jnp.int32, (128, 128), 0)
     col_id = lax.broadcasted_iota(jnp.int32, (128, 128), 1)
     place = (
@@ -311,21 +353,11 @@
     m.p1[a] = m.pin[...]
     pl.semaphore_wait(barrier, 10)
 
-    xy_peers(lambda p: xy_start(s.t1, m.tile.at[p], m.t1.at[a], p))
-    xy_peers(lambda p: xy_start(s.p1, m.pin, m.p1.at[a], p))
-    seq_peers(lambda p: seq_start(s.w1, m.wcs.at[p], m.wqk.at[piece, :], p))
-    x_view = lambda i: m.x_all.at[block_rows(i, 128), :]
-    gather_start(s.x, tok, x_view)
-    wo_place = lambda zs: m.wo_all.at[a, zs, c]
-    line_start(s.wo, wo, wo_place)
-    xy_peers(lambda p: xy_start(s.fx, m.fs.at[p], m.fgu.at[:, a, slot32, :], p))
-    xy_drain(s.t1, m.tile.at[0])
-    xy_drain(s.p1, m.pin)
-    seq_drain(s.w1, m.wcs.at[0])
-    xy_drain(s.fx, m.fs.at[0])
-
-    xy_peers(lambda p: xy_wait(s.t1, m.t1.at[p], p))
-    xy_peers(lambda p: xy_wait(s.p1, m.p1.at[p], p))
+    xy_peers(lambda p: xy_all_start(s.t1, m.tile.at[p], m.t1.at[a], p))
+    xy_peers(lambda p: xy_all_start(s.p1, m.pin, m.p1.at[a], p))
+    seq_peers(lambda p: all_start(s.w1, m.wcs.at[p], m.wqk.at[piece, :], p))
+    all_wait(s.t1, m.t1.at[pl.ds(0, 3)])
+    all_wait(s.p1, m.p1.at[pl.ds(0, 3)])
     for group in range(4):
         m.t2s[2 * group : 2 * group + 2, :] = m.t1[group, 0:2, :]
         m.t2s[8 + group : 9 + group, :] = m.t1[group, 3:4, :]
@@ -333,32 +365,110 @@
     m.t2s[13:16, :] = jnp.zeros((3, 128), F32)
     m.t2[b] = m.t2s[...]
     m.p2[b] = m.p1[lax.div(b, 2)]
-    seq_peers(lambda p: seq_start(s.t2, m.t2s, m.t2.at[b], p))
+    seq_peers(lambda p: all_start(s.t2, m.t2s, m.t2.at[b], p))
     half = 4 * c
 
     def persist_send(p):
         @pl.when(lax.rem(p, 2) == lax.div(b, 4))
         def _():
-            seq_start(s.p2, m.p1.at[lax.div(p, 2)], m.p2.at[b], p)
-
-    def persist_drain(p):
-        @pl.when(lax.rem(p, 2) == lax.div(b, 4))
-        def _():
-            seq_copy(s.p2, m.pin, m.pin, p).wait_send()
-
-    def persist_wait(p):
-        @pl.when(lax.div(p, 4) == c)
-        def _():
-            seq_wait(s.p2, m.p2.at[p], p)
+            all_start(s.p2, m.p1.at[lax.div(p, 2)], m.p2.at[b], p)
+
+    def persist_wait():
+        pl.when(part == c)(lambda: all_wait(s.p2, m.p2.at[pl.ds(0, 3)]))
+        pl.when(part != c)(lambda: all_wait(s.p2, m.p2.at[pl.ds(0, 4)]))
+
+    def persist_drain():
+        pl.when(part == c)(lambda: sent(s.p2[0].at[0], m.p2.at[pl.ds(0, 3)]))
+        pl.when(part != c)(lambda: sent(s.p2[0].at[0], m.p2.at[pl.ds(0, 4)]))
 
     seq_peers(persist_send)
-    finals.append(lambda: seq_peers(persist_drain))
-    seq_drain(s.t2, m.t2s)
-
-    seq_peers(lambda p: seq_wait(s.w1, m.wqk.at[pl.ds(pl.multiple_of(a * 256 + p * 32, 32), 32), :], p))
+    finals.append(persist_drain)
+    drain(s.t2, m.t2.at[pl.ds(0, 7)])
+
+    drain(s.t1, m.t1.at[pl.ds(0, 3)])
+    drain(s.p1, m.p1.at[pl.ds(0, 3)])
+    drain(s.w1, m.wcs.at[pl.ds(0, 7)])
+    x_view = lambda i: m.x_all.at[block_rows(i, 128), :]
+    x_place = lambda zs: x_view(2 * zs + c)
+    wo_place = lambda zs: m.wo_all.at[a, zs, c]
+    line_start_near(s.wo, wo, wo_place)
+    line_start_far(s.wo, wo, wo_place, m.wo_all.at[0, :, 0], m.wo_all.at[0, pl.ds(0, 2), 0])
+    line_start_near(s.x, tok, x_place)
+    line_start_far(
+        s.x, tok, x_place, m.x_all.at[pl.ds(0, 512), :], m.x_all.at[pl.ds(0, 256), :]
+    )
+    pass_copy(s.x, tok, x_view(b), z).start()
+    finals.append(lambda: sent(s.x[0].at[1], m.x_all.at[pl.ds(0, 512), :]))
+    down_x = lambda i: m.fdp.at[2 * i]
+    down_y = lambda i: m.fdp.at[2 * i + 1]
+
+    run = hidden // 8
+    for place, weight in enumerate((fgi, fui)):
+        for group in range(4):
+            m.fs[group, place, :, hidden:pad] = jnp.zeros((32, pad - hidden), BF16)
+            for i in range(8):
+                start = run * (4 * i + group)
+                m.fs[group, place, :, run * i : run * i + run] = weight[:, start : start + run]
+    m.fgu[:, a, slot32, :] = m.fs[mine]
+
+    def column_start(pair, place, p):
+        seq_start(pair, m.fs.at[lax.rem(p, 4), place], m.fgu.at[place, a, slot32, :], p)
+
+    def columns(pair, place):
+        seq_peers(lambda p: column_start(pair, place, p))
+
+    def columns_far(pair, place):
+        def one(p):
+            @pl.when(lax.div(p, 2) != near)
+            def _():
+                column_start(pair, place, p)
+
+        seq_peers(one)
+
+    def columns_near(pair, place):
+        column_start(pair, place, 2 * near)
+        column_start(pair, place, 2 * near + 1)
+
+    drain(s.fxg, m.gxr.at[pl.ds(0, 7), 0])
+    drain(s.fxu, m.gxr.at[pl.ds(0, 7), 1])
+    own_down = m.fdp.at[2 * a + part]
+    far_down = m.fdp.at[2 * a + 1 - part]
+    down_copy = copy(own_down, own_down, s.fd[0].at[0], s.fd[1].at[0], (a, far))
+    finals.append(down_copy.wait_send)
+
+    @pl.when(jnp.logical_not(inner_chip))
+    def _():
+        columns(s.fxg, 0)
+        columns(s.fxu, 1)
+        down_copy.start()
+
+
+    all_wait(s.w1, m.wqk.at[pl.ds(0, 224), :])
     quarter = lambda i: m.wqk.at[block_rows(i, 256), :]
-    xy_peers(lambda p: xy_start(s.w2, quarter(a), quarter(a), p))
-    xy_drain(s.w2, quarter(a))
+    xy_peers(lambda p: xy_all_start(s.w2, quarter(a), quarter(a), p))
+    drain(s.w2, m.wqk.at[pl.ds(0, 768), :])
+
+    def piece_view(place, p):
+        return lambda i: m.fgu.at[place, i, block_rows(p, 32), :]
+
+    ways = ((nx, ny), (ny, nx))
+
+    def pieces_on(peers, pair, quad_pair, place):
+        for p in peers:
+            seq_wait(pair, piece_view(place, p)(a), p)
+            quad_start(quad_pair, piece_view(place, p), *ways[place])
+
+    quad_start(s.fgx, piece_view(0, b), nx, ny)
+    quad_start(s.fux, piece_view(1, b), ny, nx)
+
+    @pl.when(part == 0)
+    def _():
+        quad_start(s.fdx, down_x, nx, ny)
+
+    @pl.when(part == 1)
+    def _():
+        quad_start(s.fdy, down_y, ny, nx)
+
 
     def project(i):
         rows = block_rows(i, 128)
@@ -366,59 +476,67 @@
         m.q[rows, :] = wide[:, 0:128].astype(BF16)
         m.k[rows, :] = wide[:, 128:256].astype(BF16)
         m.v[rows, :] = wide[:, 256:384].astype(BF16)
-        m.gps[rows, :] = wide[:, 384:512].astype(BF16)
+        m.mgs[rows, 128:256] = wide[:, 384:512].astype(BF16)
 
     head_cols = pl.ds(pl.multiple_of(b * 128, 128), 128)
 
-    xy_peers(lambda p: xy_wait(s.w2, quarter(p), p))
+    @pl.when(inner_chip)
+    def _():
+        line_wait(s.wo, wo_place, mirror)
+        line_hand_on(s.wo, wo_place, mirror)
+        line_wait(s.wo, wo_place, across)
+        line_hand_on(s.wo, wo_place, across)
+
+    gather_line(s.x, x_view, order[0])
+    line_hand_on(s.x, x_place, mirror)
+    @pl.when(inner_chip)
+    def _():
+        columns_far(s.fxg, 0)
+
+    all_wait(s.w2, m.wqk.at[pl.ds(0, 768), :])
     project(b)
-    m.gp[:, head_cols] = m.gps[own_rows, :]
     gather_pass(s.x, x_view, z)
     project(sib)
-
-    def arrived_line(step):
-        zs = lax.rem(z + step, 4)
-        gather_line(s.x, x_view, zs)
-        project(2 * zs + c)
-        send_gate(2 * zs + c)
-
-    gather_mirror(s.x, x_view)
-    project(2 * mirror + c)
-    gather_line(s.x, x_view, near)
-    project(2 * near + c)
-    gather_line(s.x, x_view, across)
-
-    def arrived_pass(step):
-        zs = lax.rem(z + step, 4)
+    project(2 * order[0] + c)
+    line_wait(s.wo, wo_place, near)
+
+    @pl.when(jnp.logical_not(inner_chip))
+    def _():
+        line_wait(s.wo, wo_place, across)
+        line_wait(s.wo, wo_place, mirror)
+
+    wo_half = lambda i: m.wo_all.at[i, :, c]
+    xy_peers(lambda p: xy_start(s.wox, wo_half(a), wo_half(a), p))
+    drain(s.wox, m.wo_all.at[pl.ds(0, 3), :, 0])
+    wo_pass = lambda i, block: copy(
+        block, block, s.wo[0].at[1], s.wo[1].at[4], (a, sib)
+    )
+    wo_pass(a, wo_half(a)).start()
+    finals.append(lambda: sent(s.wo[0].at[1], m.wo_all.at[:, :, 0]))
+    chips = tuple(2 * zs + core for zs in order for core in range(2))
+    pieces_on((sib,) + chips[0:2], s.fxg, s.fgx, 0)
+
+    gather_line(s.x, x_view, order[1])
+    gather_line(s.x, x_view, order[2])
+    line_hand_on(s.x, x_place, across)
+
+    @pl.when(inner_chip)
+    def _():
+        columns_near(s.fxg, 0)
+        columns(s.fxu, 1)
+        down_copy.start()
+
+    project(2 * order[1] + c)
+    project(2 * order[2] + c)
+
+    def arrived_pass(zs):
         gather_pass(s.x, x_view, zs)
         project(2 * zs + 1 - c)
 
-    wo_half = lambda i: m.wo_all.at[i, :, c]
-    line_wait(s.wo, wo_place, mirror)
-    line_hand_on(s.wo, wo_place)
-    line_wait(s.wo, wo_place, near)
-    line_wait(s.wo, wo_place, across)
-    xy_peers(lambda p: xy_start(s.wox, wo_half(a), wo_half(a), p))
-    xy_drain(s.wox, wo_half(a))
-    wo_pass = lambda i, block: copy(
-        block, block, s.wo[0].at[4 + i], s.wo[1].at[4 + i], (a, sib)
-    )
-    wo_pass(a, wo_half(a)).start()
-    finals.append(lambda: each(0, 4, lambda i: wo_pass(i, wo_half(i)).wait_send()))
-    project(2 * across + c)
-    each(1, 4, arrived_pass)
-    seq_peers(
-        lambda p: seq_start(s.gp, m.gps.at[block_rows(p, 128), :], m.gp.at[:, head_cols], p)
-    )
-    seq_drain(s.gp, m.gps.at[own_rows, :])
-    xy_peers(lambda p: xy_wait(s.fx, m.fgu.at[:, p, slot32, :], p))
-    fg_view = lambda i: m.fgu.at[0, :, block_rows(i, 32), :]
-    fu_view = lambda i: m.fgu.at[1, :, block_rows(i, 32), :]
-    fd_view = lambda i: m.fdp.at[i]
-    gather_start(s.fg, fg_view(b), fg_view)
-
-    seq_peers(lambda p: seq_wait(s.t2, m.t2.at[p], p))
-    seq_peers(persist_wait)
+    for zs in order:
+        arrived_pass(zs)
+    all_wait(s.t2, m.t2.at[pl.ds(0, 7)])
+    persist_wait()
     small = m.t2[...]
     place16 = lax.broadcasted_iota(jnp.int32, (8, 16, 128), 1)
     rates = jnp.sum(jnp.where(place16 == b, small, 0.0), axis=1)
@@ -489,74 +607,92 @@
         m.both[rows, keys] = joint
         m.fprobs[rows, :] = fixed_prob
         mixed = nn(joint, m.v[keys, :]) + nn(fixed_prob, m.fkv[16:32, :])
-        m.mxs[rows, :] = mixed.astype(BF16)
+        m.mgs[rows, 0:128] = mixed.astype(BF16)
 
     attend = lambda i: by_extent(i, attend_keys)
 
     def attend_send(step):
         i = lax.rem(b + step, 8)
         attend(i)
-        seq_start(s.mx, m.mxs.at[block_rows(i, 128), :], m.mx.at[:, head_cols], i)
-
-    each(1, 6, attend_send)
-    each(6, 7, attend_send)
-    gather_mirror(s.fg, fg_view)
-    gather_start(s.fu, fu_view(b), fu_view)
-    each(7, 8, attend_send)
-    seq_drain(s.mx, m.mxs.at[own_rows, :])
+        all_start(s.mx, m.mgs.at[block_rows(i, 128), :], m.mg.at[b], i)
+
+    each(1, 4, attend_send)
+    pieces_on(chips[2:6], s.fxg, s.fgx, 0)
+    pieces_on((sib,) + chips[0:2], s.fxu, s.fux, 1)
+    each(4, 8, attend_send)
+    drain(s.mx, m.mgs.at[pl.ds(0, 896), :])
     attend(b)
-    m.mx[:, head_cols] = m.mxs[own_rows, :]
-
-    seq_peers(lambda p: seq_wait(s.gp, m.gp.at[:, pl.ds(pl.multiple_of(p * 128, 128), 128)], p))
+    m.mg[b] = m.mgs[own_rows, :]
+    quad_pass(s.fgx, lambda i: m.fgu.at[0, i], nx, ny)
+    pieces_on(chips[2:6], s.fxu, s.fux, 1)
+    copy(far_down, far_down, s.fd[0].at[0], s.fd[1].at[0], (a, far)).wait_recv()
+
+    @pl.when(part == 1)
+    def _():
+        quad_start(s.fdx, down_x, nx, ny)
+
+    @pl.when(part == 0)
+    def _():
+        quad_start(s.fdy, down_y, ny, nx)
+
+
     def wo_arrived(p):
         xy_wait(s.wox, wo_half(p), p)
         wo_pass(p, wo_half(p)).start()
 
     xy_peers(wo_arrived)
-    each(0, 4, lambda i: wo_pass(i, m.wo_all.at[i, :, 1 - c]).wait_recv())
-    seq_peers(lambda p: seq_wait(s.mx, m.mx.at[:, pl.ds(pl.multiple_of(p * 128, 128), 128)], p))
+    landed_all(s.wo[1].at[4], m.wo_all.at[:, :, 1 - c])
+    quad_pass(s.fux, lambda i: m.fgu.at[1, i], ny, nx)
+    all_wait(s.mx, m.mg.at[pl.ds(0, 7)])
+    for head in range(8):
+        m.mx[:, head * 128 : head * 128 + 128] = m.mg[head, :, 0:128]
+        m.gp[:, head * 128 : head * 128 + 128] = m.mg[head, :, 128:256]
 
     out_w = lambda: m.wo_all[...].reshape(width, width)
     m.br[...] = nn(m.mx[...], out_w())
 
     half_row = lambda i: pl.ds(
-        pl.multiple_of((4 * lax.div(i, 2) + a) * 64 + lax.rem(i, 2) * 32, 32), 32
+        pl.multiple_of((4 * lax.div(i, 2) + mine) * 64 + lax.rem(i, 2) * 32, 32), 32
     )
     quad = lambda ref, h, i: ref.at[block_rows(4 * h + i, 64), :]
 
-    def half_copy(pair, src, dst, h, peer, slot):
-        return copy(src, dst, pair[0].at[4 * h + peer], pair[1].at[4 * h + slot], (peer, b))
+    def half_copy(pair, src, dst, h, slot, peer):
+        return copy(src, dst, pair[0].at[h], pair[1].at[2 * h + slot], (a, peer))
 
     def half_gather(pair, ref, h):
-        xy_peers(lambda p: half_copy(pair, quad(ref, h, a), quad(ref, h, a), h, p, a).start())
-        finals.append(
-            lambda: xy_peers(
-                lambda p: half_copy(pair, quad(ref, h, a), quad(ref, h, a), h, p, p).wait_send()
-            )
-        )
+        block = quad(ref, h, mine)
+        half_copy(pair, block, block, h, 0, partner).start()
+        half_copy(pair, block, block, h, 1, sib).start()
 
     def half_wait(pair, ref, h):
-        xy_peers(lambda p: half_copy(pair, quad(ref, h, p), quad(ref, h, p), h, p, p).wait_recv())
+        block = quad(ref, h, pmate)
+        landed_all(pair[1].at[2 * h], block)
+        half_copy(pair, block, block, h, 1, sib).start()
+        landed_all(pair[1].at[2 * h + 1], ref.at[pl.ds(0, 128), :])
+        finals.append(lambda: sent(pair[0].at[h], ref.at[pl.ds(0, 192), :]))
 
     def half_scatter(pair, value, h):
         for i in range(4):
             m.ysend[i, h * 64 : h * 64 + 64, :] = value[i * 64 : i * 64 + 64, :].astype(BF16)
         rows = pl.ds(h * 64, 64)
-        xy_peers(
-            lambda p: half_copy(
-                pair, m.ysend.at[p, rows, :], m.yrecv.at[a, rows, :], h, p, a
-            ).start()
-        )
+        half_copy(pair, m.ysend.at[cross, rows, :], m.yrecv.at[1, rows, :], h, 1, sib).start()
+        half_copy(pair, m.ysend.at[mate, rows, :], m.yrecv.at[0, rows, :], h, 0, sib).start()
+
+    def half_on(pair, h):
+        rows = pl.ds(h * 64, 64)
+        landed_all(pair[1].at[2 * h + 1], m.yrecv.at[1, rows, :])
+        m.ysend[pmate, rows, :] = (
+            m.ysend[pmate, rows, :].astype(F32) + m.yrecv[1, rows, :].astype(F32)
+        ).astype(BF16)
+        half_copy(
+            pair, m.ysend.at[pmate, rows, :], m.yrecv.at[2, rows, :], h, 0, partner
+        ).start()
 
     def half_sent(pair, h):
-        rows = pl.ds(h * 64, 64)
-        block = lambda p: m.ysend.at[p, rows, :]
-        xy_peers(lambda p: half_copy(pair, block(p), block(p), h, p, p).wait_send())
+        sent(pair[0].at[h], m.ysend.at[pl.ds(0, 3), pl.ds(h * 64, 64), :])
 
     def half_land(pair, h):
-        rows = pl.ds(h * 64, 64)
-        block = lambda p: m.yrecv.at[p, rows, :]
-        xy_peers(lambda p: half_copy(pair, block(p), block(p), h, p, p).wait_recv())
+        landed_all(pair[1].at[2 * h], m.yrecv.at[pl.ds(0, 2), pl.ds(h * 64, 64), :])
 
     def normalise(i):
         rows = block_rows(i, 32)
@@ -574,15 +710,14 @@
     each(2, 4, normalise)
     half_gather(s.sc, m.sc, 1)
 
-    gather_mirror(s.fu, fu_view)
-    gather_start(s.fd, fd_view(b), fd_view)
-    gather_line(s.fg, fg_view, near)
-    gather_line(s.fg, fg_view, across)
-    each(0, 4, lambda zs: gather_pass(s.fg, fg_view, zs))
-    gather_mirror(s.fd, fd_view)
-    gather_line(s.fu, fu_view, near)
-    gather_line(s.fu, fu_view, across)
-    each(0, 4, lambda zs: gather_pass(s.fu, fu_view, zs))
+    quad_pass(s.fdx, down_x, nx, ny)
+    quad_pass(s.fdy, down_y, ny, nx)
+    landed_all(s.fgx[1].at[1], m.fgu.at[0, pl.ds(0, 2)])
+    landed_all(s.fux[1].at[1], m.fgu.at[1, pl.ds(0, 2)])
+    drain(s.fgx, m.fgu.at[0, pl.ds(0, 3)])
+    drain(s.fux, m.fgu.at[1, pl.ds(0, 3)])
+    drain(s.fdx, m.fdp.at[pl.ds(0, 3)])
+    drain(s.fdy, m.fdp.at[pl.ds(0, 3)])
     half_wait(s.sc, m.sc, 0)
 
     gate_w = lambda: m.fgu[0].reshape(width, pad)
@@ -598,9 +733,8 @@
         m.inner[rows, :] = (gate_act * jax.nn.sigmoid(gate_act) * up_act).astype(BF16)
 
     feed(0)
-    gather_line(s.fd, fd_view, near)
-    gather_line(s.fd, fd_view, across)
-    each(0, 4, lambda zs: gather_pass(s.fd, fd_view, zs))
+    landed_all(s.fdx[1].at[1], m.fdp.at[pl.ds(0, 2)])
+    landed_all(s.fdy[1].at[1], m.fdp.at[pl.ds(0, 2)])
     share_rows = m.fdp.shape[1] - 8
     for i in range(4):
         m.ffd[2 * i * share_rows : 2 * (i + 1) * share_rows, :] = jnp.concatenate(
@@ -610,7 +744,8 @@
 
     def feed_out(h):
         half_scatter(s.y, nn(m.inner[block_rows(h, 256), :], m.ffd[...]), h)
-        m.own[block_rows(h, 64), :] = nn(m.inner[block_rows(4 * h + a, 64), :], m.ffd[...])
+        m.own[block_rows(h, 64), :] = nn(m.inner[block_rows(4 * h + mine, 64), :], m.ffd[...])
+        half_on(s.y, h)
 
     feed_out(0)
     half_wait(s.sc, m.sc, 1)
@@ -624,10 +759,7 @@
     def finish(i):
         rows = block_rows(i, 32)
         final = m.hid[rows, :] + m.own[rows, :]
-        a1, a2, a3 = lax.rem(a + 1, 4), lax.rem(a + 2, 4), lax.rem(a + 3, 4)
-        final = final + m.yrecv[a1, rows, :].astype(F32)
-        final = final + m.yrecv[a2, rows, :].astype(F32)
-        final = final + m.yrecv[a3, rows, :].astype(F32)
+        final = final + m.yrecv[0, rows, :].astype(F32) + m.yrecv[2, rows, :].astype(F32)
         out_o[rows, :] = final.astype(BF16)
         error = final - tea[rows, :].astype(F32)
         counted = m.vcol[rows, :] * error
@@ -663,8 +795,9 @@
         rows = block_rows(h, 256)
         half_sent(s.y, h)
         half_scatter(s.ds, nt(m.dga[rows, :], gate_w()) + nt(m.dua[rows, :], up_w()), h)
-        rows = block_rows(4 * h + a, 64)
+        rows = block_rows(4 * h + mine, 64)
         m.own[block_rows(h, 64), :] = nt(m.dga[rows, :], gate_w()) + nt(m.dua[rows, :], up_w())
+        half_on(s.ds, h)
 
     feed_in(0)
     half_wait(s.df, m.df, 1)
@@ -672,100 +805,78 @@
     feed_in(1)
     finals.append(lambda: (half_sent(s.ds, 0), half_sent(s.ds, 1)))
 
-    def share_copy(pair, share, landing, slot, zt):
-        return copy(share, landing.at[slot], pair[0].at[zt], pair[1].at[slot], (a, 2 * zt + c))
+    def share_copy(pair, share, landing, zt):
+        return copy(share, landing.at[z], pair[0].at[0], pair[1].at[0], (a, 2 * zt + c))
+
+    def sum_near(pair, share, landing):
+        share_copy(pair, share(near), landing, near).start()
+
+    def sum_far(pair, share, landing, zt, slot, flag):
+        copy(
+            share(zt), landing.at[slot], pair[0].at[0], pair[1].at[flag], (a, 2 * near + c)
+        ).start()
 
     def sum_start(pair, share, landing):
-        share_copy(pair, share(near), landing, z, near).start()
-
-        @pl.when(inner_chip)
-        def _():
-            share_copy(pair, share(across), landing, z, across).start()
-
         @pl.when(jnp.logical_not(inner_chip))
         def _():
-            share_copy(pair, share(mirror), landing, z, mirror).start()
-            copy(
-                share(across), landing.at[mirror], pair[0].at[across], pair[1].at[mirror],
-                (a, 2 * near + c),
-            ).start()
-
-    def sum_wait(pair, landing, zs):
-        copy(
-            landing.at[zs], landing.at[zs], pair[0].at[zs], pair[1].at[zs], (a, 2 * zs + c)
-        ).wait_recv()
+            sum_far(pair, share, landing, across, mirror, 1)
+            sum_far(pair, share, landing, mirror, near, 2)
+
+        sum_near(pair, share, landing)
 
     def sum_pass(pair, share, landing, add):
         @pl.when(inner_chip)
         def _():
-            sum_wait(pair, landing, across)
-            add(mirror, across)
-            share_copy(pair, share(mirror), landing, z, mirror).start()
-
-    def sum_finish(pair, share, landing):
-        sum_wait(pair, landing, near)
-        sum_wait(pair, landing, mirror)
-
-        @pl.when(jnp.logical_not(inner_chip))
-        def _():
-            sum_wait(pair, landing, across)
-
-        finals.append(
-            lambda: z_peers(
-                lambda zt: share_copy(pair, share(zt), landing, zt, zt).wait_send()
-            )
-        )
+            for zt, slot, flag in ((mirror, across, 1), (across, z, 2)):
+                landed_all(pair[1].at[flag], landing.at[slot])
+                add(zt, slot)
+                share_copy(pair, share(zt), landing, zt).start()
+
+    second = across + inside * (mirror - across)
+
+    def sum_finish(pair, landing, three):
+        landed_all(pair[1].at[0], landing.at[pl.ds(0, 2)])
+        drain(pair, three)
 
     def landed(landing, where):
-        total = landing[(near,) + where].astype(F32) + landing[(mirror,) + where].astype(F32)
-        last = landing[(across,) + where].astype(F32)
-        return total + jnp.where(inner_chip, 0.0, last)
-
-    def down_grad(i):
+        return landing[(near,) + where].astype(F32) + landing[(second,) + where].astype(F32)
+
+    def fold_add(view, pre, chunk):
+        def add(second):
+            rows = view(second).shape[0]
+
+            def one(i):
+                part_rows = pl.ds(pl.multiple_of(i * chunk, chunk), chunk)
+                target = view(second)
+                target[part_rows] = (
+                    target[part_rows].astype(F32) + pre[part_rows].astype(F32)
+                ).astype(BF16)
+
+            each(0, rows // chunk, one)
+
+        return add
+
+    gate_share = lambda i: m.gus.at[0, i]
+    up_share = lambda i: m.gus.at[1, i]
+
+    def one_grad(i, place, grads):
         cols = pl.ds(pl.multiple_of(i * 256, 256), 256)
-        m.ffd[block_rows(i, 256), :] = tn(m.inner[:, cols], m.df[...]).astype(BF16)
-
-    each(0, pad // 256, down_grad)
-    for i in range(4):
-        pair = m.ffd[2 * i * share_rows : 2 * (i + 1) * share_rows, :].astype(F32)
-        for j in range(2):
-            m.gds[i, j] = jnp.concatenate(
-                [pair[j * share_rows : (j + 1) * share_rows, :], jnp.zeros((8, width), F32)], axis=0
-            ).astype(BF16)
-    rgd_copy = copy(m.gds.at[:, 1 - c], m.gdr, s.rgd[0].at[4], s.rgd[1].at[4], (a, sib))
-    rgd_copy.start()
-
-    def up_gate_grad(i):
-        cols = pl.ds(pl.multiple_of(i * 256, 256), 256)
-        scaled = m.sc[:, cols]
-        m.gus[:, :, 0, i] = tn(scaled, m.dga[...]).astype(BF16).reshape(4, 2, 32, pad)
-        m.gus[:, :, 1, i] = tn(scaled, m.dua[...]).astype(BF16).reshape(4, 2, 32, pad)
-
-    each(0, 4, up_gate_grad)
-    rgu_copy = copy(m.gus.at[:, 1 - c], m.gur, s.rgu[0].at[4], s.rgu[1].at[4], (a, sib))
-    rgu_copy.start()
-
-    down_share = lambda zt: m.gds.at[zt, c]
-
-    def add_down(zt):
-        m.gds[zt, c] = (m.gds[zt, c].astype(F32) + m.gdr[zt].astype(F32)).astype(BF16)
-
-    def pass_down(zt, slot):
-        m.gds[zt, c] = (m.gds[zt, c].astype(F32) + m.gdz[slot].astype(F32)).astype(BF16)
-
-    rgd_copy.wait_recv()
-    z_peers(add_down)
-    sum_start(s.rgd, down_share, m.gdz)
+        m.gus[place, i] = tn(m.sc[:, cols], grads[...]).astype(BF16)
+
+    one_grad(diagonal, 0, m.dga)
+    one_grad(ny, 0, m.dga)
+    fold_start(s.rg, gate_share, m.gpre.at[0], m.gland.at[0], ny)
+    one_grad(diagonal, 1, m.dua)
+    one_grad(nx, 1, m.dua)
+    fold_start(s.ru, up_share, m.gpre.at[1], m.gland.at[1], nx)
 
     half_land(s.ds, 0)
     m.ggain[...] = jnp.zeros_like(m.ggain)
 
     def norm_back(i):
         rows = block_rows(i, 32)
-        a1, a2, a3 = lax.rem(a + 1, 4), lax.rem(a + 2, 4), lax.rem(a + 3, 4)
-        d_scaled = m.own[rows, :] + m.yrecv[a1, rows, :].astype(F32)
-        d_scaled = d_scaled + m.yrecv[a2, rows, :].astype(F32)
-        d_scaled = d_scaled + m.yrecv[a3, rows, :].astype(F32)
+        d_scaled = m.own[rows, :] + m.yrecv[0, rows, :].astype(F32)
+        d_scaled = d_scaled + m.yrecv[2, rows, :].astype(F32)
         inv = m.inv[rows, 0:1]
         normed = m.hid[rows, :] * inv
         m.ggain[...] += jnp.sum(d_scaled * normed, axis=0, keepdims=True)
@@ -783,59 +894,58 @@
     gate_cols = pl.ds(384, 128)
     cols_of = lambda i: pl.ds(pl.multiple_of(i * 128, 128), 128)
     m.dms[...] = nt(m.dbr[...], out_w()).astype(BF16)
-    seq_peers(lambda p: seq_start(s.dm, m.dms.at[:, cols_of(p)], m.dm.at[own_rows, :], p))
-    seq_peers(
-        lambda p: seq_start(s.dg, m.dgt.at[:, cols_of(p)], m.dq.at[own_rows, gate_cols], p)
-    )
-    seq_drain(s.dm, m.dms.at[:, 0:128])
-    seq_drain(s.dg, m.dgt.at[:, 0:128])
-    m.dm[own_rows, :] = m.dms[:, head_cols]
-    m.dq[own_rows, gate_cols] = m.dgt[:, head_cols]
+    for head in range(8):
+        cols = slice(head * 128, head * 128 + 128)
+        m.dgs[head, :, 0:128] = m.dms[:, cols]
+        m.dgs[head, :, 128:256] = m.dgt[:, cols]
+    seq_peers(lambda p: seq_start(s.dm, m.dgs.at[p], m.dmg.at[b], p))
+    drain(s.dm, m.dgs.at[pl.ds(0, 7)])
+    m.dmg[b] = m.dgs[b]
+
+    one_grad(nx, 0, m.dga)
+    fold_pass(
+        s.rg, gate_share, m.gpre.at[0], m.gland.at[0], fold_add(gate_share, m.gpre.at[0], 32), nx
+    )
+    one_grad(ny, 1, m.dua)
+    fold_pass(
+        s.ru, up_share, m.gpre.at[1], m.gland.at[1], fold_add(up_share, m.gpre.at[1], 32), ny
+    )
+    one_grad(a, 0, m.dga)
+    one_grad(a, 1, m.dua)
+
+    def down_grad(i):
+        cols = pl.ds(pl.multiple_of(i * 256, 256), 256)
+        m.ffd[block_rows(i, 256), :] = tn(m.inner[:, cols], m.df[...]).astype(BF16)
+
+    each(0, pad // 256, down_grad)
+    for i in range(4):
+        double = m.ffd[2 * i * share_rows : 2 * (i + 1) * share_rows, :].astype(F32)
+        for j in range(2):
+            m.gds[2 * i + j] = jnp.concatenate(
+                [double[j * share_rows : (j + 1) * share_rows, :], jnp.zeros((8, width), F32)],
+                axis=0,
+            ).astype(BF16)
+    down_x_share = lambda i: m.gds.at[2 * i]
+    down_y_share = lambda i: m.gds.at[2 * i + 1]
+    fold_start(s.rdx, down_x_share, m.dpre.at[0], m.dland.at[0], ny)
+    fold_start(s.rdy, down_y_share, m.dpre.at[1], m.dland.at[1], nx)
 
     def out_grad(i):
         cols = pl.ds(pl.multiple_of(i * 256, 256), 256)
-        m.gwos[i] = tn(m.mx[:, cols], m.dbr[...]).astype(BF16)
-
-    def out_grad_send(step):
-        i = lax.rem(a + step, 4)
-        out_grad(i)
-        xy_start(s.gwo, m.gwos.at[i], m.gwor.at[a], i)
-
-    each(1, 4, out_grad_send)
-    xy_drain(s.gwo, m.gwos.at[0])
-    out_grad(a)
-
-    up_gate_share = lambda zt: m.gus.at[zt, c]
-
-    def add_up_gate(zt):
-        def one(i):
-            j = lax.div(i, 4)
-            g = lax.rem(i, 4)
-            m.gus[zt, c, j, g] = (
-                m.gus[zt, c, j, g].astype(F32) + m.gur[zt, j, g].astype(F32)
-            ).astype(BF16)
-
-        each(0, 8, one)
-
-    def pass_up_gate(zt, slot):
-        def one(i):
-            j = lax.div(i, 4)
-            g = lax.rem(i, 4)
-            m.gus[zt, c, j, g] = (
-                m.gus[zt, c, j, g].astype(F32) + m.guz[slot, j, g].astype(F32)
-            ).astype(BF16)
-
-        each(0, 8, one)
-
-    rgu_copy.wait_recv()
-    z_peers(add_up_gate)
-    sum_start(s.rgu, up_gate_share, m.guz)
+        m.gwos[i] = tn(m.mx[:, cols], m.dbr[...]).astype(BF16).reshape(4, 2, 32, width)
+
+    each(0, 4, out_grad)
+    gos_copy = copy(m.gwos.at[:, :, 1 - c], m.gwor, s.gos[0].at[0], s.gos[1].at[0], (a, sib))
+    gos_copy.start()
+    finals.append(gos_copy.wait_send)
     m.pgrad[...] = jnp.zeros_like(m.pgrad)
 
     def attend_back_keys(i, extent):
         rows = block_rows(i, 128)
         keys = slice(0, extent)
-        d_mixed = m.dm[rows, :]
+        d_mixed = m.dmg[i, :, 0:128]
+        m.dm[rows, :] = d_mixed
+        m.dq[rows, gate_cols] = m.dmg[i, :, 128:256]
         d_joint = nt(d_mixed, m.v[keys, :])
         prob = m.probs[rows, keys].astype(F32)
         turned = prob * d_joint
@@ -862,20 +972,46 @@
 
     def attend_back_next(step):
         i = lax.rem(b + step, 8)
-        seq_wait(s.dm, m.dm.at[block_rows(i, 128), :], i)
-        seq_wait(s.dg, m.dq.at[block_rows(i, 128), gate_cols], i)
+        seq_wait(s.dm, m.dmg.at[i], i)
         attend_back(i)
 
     each(1, 4, attend_back_next)
-    sum_pass(s.rgd, down_share, m.gdz, pass_down)
-    each(4, 8, attend_back_next)
+    each(4, 6, attend_back_next)
+    def owner_all(fold, pair, share, place):
+        fold_finish(fold, m.gland.at[place], m.gus.at[place, pl.ds(0, 3)])
+
+        def owner_rows(p):
+            rows = block_rows(p, 32)
+            total = m.gus[place, a, rows, :].astype(F32) + m.gland[place, 0, rows, :].astype(F32)
+            m.gxs[p, place] = (total + m.gland[place, 1, rows, :].astype(F32)).astype(BF16)
+
+        def owner_send(p):
+            owner_rows(p)
+            all_start(pair, m.gxs.at[p, place], m.gxr.at[b, place], p)
+
+        seq_peers(owner_send)
+        drain(pair, m.gxs.at[pl.ds(0, 7), place])
+        owner_rows(b)
+        m.gxr[b, place] = m.gxs[b, place]
+
+    owner_all(s.rg, s.gxg, gate_share, 0)
+    each(6, 8, attend_back_next)
+    fold_pass(
+        s.rdx, down_x_share, m.dpre.at[0], m.dland.at[0],
+        fold_add(down_x_share, m.dpre.at[0], 32), nx,
+    )
+    fold_pass(
+        s.rdy, down_y_share, m.dpre.at[1], m.dland.at[1],
+        fold_add(down_y_share, m.dpre.at[1], 32), ny,
+    )
+    owner_all(s.ru, s.gxu, up_share, 1)
 
     m.fin0[0:32, :] = m.pgrad[...]
     for j in range(8):
         m.fin0[32 + j : 33 + j, :] = m.ggain[:, j * 128 : j * 128 + 128]
     m.fin1[a] = m.fin0[...]
-    xy_peers(lambda p: xy_start(s.fin1, m.fin0, m.fin1.at[a], p))
-    xy_drain(s.fin1, m.fin0)
+    xy_peers(lambda p: xy_all_start(s.fin1, m.fin0, m.fin1.at[a], p))
+    drain(s.fin1, m.fin1.at[pl.ds(0, 3)])
 
     query_turned = jnp.transpose(m.q[...].astype(F32)).astype(BF16)
     mixed_turned = jnp.transpose(m.dm[...].astype(F32)).astype(BF16)
@@ -888,63 +1024,104 @@
 
     each(0, 8, key_value_grad)
 
-    sum_pass(s.rgu, up_gate_share, m.guz, pass_up_gate)
+    def token_grad(i):
+        return nt(m.dq[block_rows(i, 128), :], m.wqk[...])
+
+    def token_sib(zt):
+        m.gts[zt, 1 - c] = token_grad(2 * zt + 1 - c).astype(BF16)
+        copy(
+            m.gts.at[zt, 1 - c], m.gtr.at[zt], s.gt[0].at[1], s.gt[1].at[4 + zt],
+            (a, sib),
+        ).start()
+
+    for zt in (near + (1 - inside) * (across - near), mirror, across + (1 - inside) * (near - across), z):
+        token_sib(zt)
+
+    fold_finish(s.rdx, m.dland.at[0], m.gds.at[pl.ds(0, 3)])
+    fold_finish(s.rdy, m.dland.at[1], m.gds.at[pl.ds(0, 3)])
+
+    def down_sum(j):
+        total = m.gds[2 * a + j].astype(F32) + m.dland[j, 0].astype(F32)
+        return total + m.dland[j, 1].astype(F32)
+
+    m.dsum[0] = down_sum(1 - part).astype(BF16)
+    far_copy = copy(m.dsum.at[0], m.dfar, s.gfd[0].at[0], s.gfd[1].at[0], (a, far))
+    far_copy.start()
+    finals.append(far_copy.wait_send)
+
+    token_share = lambda zt: m.gts.at[zt, c]
+
+    def token_line(zt):
+        mine = token_grad(2 * zt + c)
+        copy(
+            m.gtr.at[zt], m.gtr.at[zt], s.gt[0].at[1], s.gt[1].at[4 + zt], (a, sib)
+        ).wait_recv()
+        m.gts[zt, c] = (mine + m.gtr[zt].astype(F32)).astype(BF16)
+
+    def pass_token(zt, slot):
+        m.gts[zt, c] = (m.gts[zt, c].astype(F32) + m.yrecv[slot].astype(F32)).astype(BF16)
+
+    token_line(near + (1 - inside) * (across - near))
+
+    @pl.when(inner_chip)
+    def _():
+        sum_near(s.gt, token_share, m.yrecv)
+
+    @pl.when(jnp.logical_not(inner_chip))
+    def _():
+        sum_far(s.gt, token_share, m.yrecv, across, mirror, 1)
+
+    token_line(mirror)
+
+    @pl.when(jnp.logical_not(inner_chip))
+    def _():
+        sum_far(s.gt, token_share, m.yrecv, mirror, near, 2)
+
+    token_line(across + (1 - inside) * (near - across))
+
+    @pl.when(jnp.logical_not(inner_chip))
+    def _():
+        sum_near(s.gt, token_share, m.yrecv)
+
+    m.own[...] = token_grad(b)
+    finals.append(lambda: sent(s.gt[0].at[1], m.gtr))
+
     def head_weight_grad(i):
         cols = pl.ds(pl.multiple_of(i * 256, 256), 256)
         m.gws[i] = tn(m.x_all[:, cols], m.dq[...]).astype(BF16)
 
-    def head_weight_send(step):
-        i = lax.rem(a + step, 4)
-        head_weight_grad(i)
-        xy_start(s.gw, m.gws.at[i], m.gwr.at[a], i)
-
-    each(1, 4, head_weight_send)
-    xy_drain(s.gw, m.gws.at[0])
-    head_weight_grad(a)
-
-    def token_grad(i):
-        return nt(m.dq[block_rows(i, 128), :], m.wqk[...])
-
-    def token_sib(step):
-        zt = lax.rem(z + step, 4)
-        m.gts[zt, 1 - c] = token_grad(2 * zt + 1 - c).astype(BF16)
-        copy(
-            m.gts.at[zt, 1 - c], m.gtr.at[zt], s.gt[0].at[4 + zt], s.gt[1].at[4 + zt],
-            (a, sib),
-        ).start()
-
-    each(1, 5, token_sib)
-
-    token_share = lambda zt: m.gts.at[zt, c]
-
-    def token_line(step):
-        zt = lax.rem(z + step, 4)
-        mine = token_grad(2 * zt + c)
-        copy(
-            m.gtr.at[zt], m.gtr.at[zt], s.gt[0].at[4 + zt], s.gt[1].at[4 + zt], (a, sib)
-        ).wait_recv()
-        m.gts[zt, c] = (mine + m.gtr[zt].astype(F32)).astype(BF16)
-
-    def pass_token(zt, slot):
-        m.gts[zt, c] = (m.gts[zt, c].astype(F32) + m.yrecv[slot].astype(F32)).astype(BF16)
-
-    each(1, 4, token_line)
-    sum_start(s.gt, token_share, m.yrecv)
-    m.own[...] = token_grad(b)
-    finals.append(
-        lambda: each(
-            0, 4,
-            lambda zt: copy(
-                m.gtr.at[zt], m.gtr.at[zt], s.gt[0].at[4 + zt], s.gt[1].at[4 + zt], (a, sib)
-            ).wait_send(),
-        )
-    )
-
-    xy_peers(lambda p: xy_wait(s.fin1, m.fin1.at[p], p))
+    each(0, 4, head_weight_grad)
+    weight_x = lambda i: m.gws.at[i, pl.ds(0, 128), :]
+    weight_y = lambda i: m.gws.at[i, pl.ds(128, 128), :]
+    land_x = m.wland.at[:, pl.ds(0, 128), :]
+    land_y = m.wland.at[:, pl.ds(128, 128), :]
+    fold_start(s.rwx, weight_x, m.wpre.at[0], land_x, ny)
+    fold_start(s.rwy, weight_y, m.wpre.at[1], land_y, nx)
+
+    gos_copy.wait_recv()
+
+    def out_add(k):
+        i = lax.div(k, 4)
+        j = lax.rem(k, 4)
+        m.gwos[i, j, c] = (
+            m.gwos[i, j, c].astype(F32) + m.gwor[i, j].astype(F32)
+        ).astype(BF16)
+
+    each(0, 16, out_add)
+    out_x = lambda i: m.gwos.at[i, pl.ds(0, 2), c]
+    out_y = lambda i: m.gwos.at[i, pl.ds(2, 2), c]
+    oland_x = m.oland.at[:, pl.ds(0, 2)]
+    oland_y = m.oland.at[:, pl.ds(2, 2)]
+    fold_start(s.rox, out_x, m.opre.at[0], oland_x, ny)
+    fold_start(s.roy, out_y, m.opre.at[1], oland_y, nx)
+
+    fold_pass(s.rwx, weight_x, m.wpre.at[0], land_x, fold_add(weight_x, m.wpre.at[0], 32), nx)
+    fold_pass(s.rwy, weight_y, m.wpre.at[1], land_y, fold_add(weight_y, m.wpre.at[1], 32), ny)
+    all_wait(s.fin1, m.fin1.at[pl.ds(0, 3)])
     m.fin2s[...] = (m.fin1[0] + m.fin1[1]) + (m.fin1[2] + m.fin1[3])
     m.fin2[b] = m.fin2s[32:48, :]
-    seq_peers(lambda p: seq_start(s.fin2, m.fin2s.at[pl.ds(32, 16), :], m.fin2.at[b], p))
-    seq_drain(s.fin2, m.fin2.at[0])
+    seq_peers(lambda p: all_start(s.fin2, m.fin2s.at[pl.ds(32, 16), :], m.fin2.at[b], p))
+    drain(s.fin2, m.fin2.at[pl.ds(0, 7)])
     holder = 2 * a + lax.div(b, 4)
     keeps = lambda p: (lax.div(b, 2) == a) & (lax.div(p, 4) == c)
 
@@ -967,74 +1144,48 @@
     def _():
         m.pers[...] = m.fin2s[0:32, :]
 
+    fold_pass(s.rox, out_x, m.opre.at[0], oland_x, fold_add(out_x, m.opre.at[0], 1), nx)
+    fold_pass(s.roy, out_y, m.opre.at[1], oland_y, fold_add(out_y, m.opre.at[1], 1), ny)
     sum_pass(s.gt, token_share, m.yrecv, pass_token)
-    xy_peers(lambda p: xy_wait(s.gw, m.gwr.at[p], p))
-    a1, a2, a3 = lax.rem(a + 1, 4), lax.rem(a + 2, 4), lax.rem(a + 3, 4)
+    fold_finish(s.rwx, land_x, m.gws.at[pl.ds(0, 3), pl.ds(0, 128), :])
+    fold_finish(s.rwy, land_y, m.gws.at[pl.ds(0, 3), pl.ds(0, 128), :])
 
     def head_sum(p):
         rows = block_rows(p, 32)
-        total = m.gws[a, rows, :].astype(F32) + m.gwr[a1, rows, :].astype(F32)
-        total = total + m.gwr[a2, rows, :].astype(F32)
-        total = total + m.gwr[a3, rows, :].astype(F32)
-        m.gas[p] = total.astype(BF16)
+        total = m.gws[a, rows, :].astype(F32) + m.wland[0, rows, :].astype(F32)
+        m.gas[p] = (total + m.wland[1, rows, :].astype(F32)).astype(BF16)
 
     def head_sum_send(p):
         head_sum(p)
-        seq_start(s.gwa, m.gas.at[p], m.gar.at[b], p)
+        all_start(s.gwa, m.gas.at[p], m.gar.at[b], p)
 
     seq_peers(head_sum_send)
-    seq_drain(s.gwa, m.gas.at[0])
+    drain(s.gwa, m.gas.at[pl.ds(0, 7)])
     head_sum(b)
     m.gar[b] = m.gas[b]
 
-    xy_peers(lambda p: xy_wait(s.gwo, m.gwor.at[p], p))
+    fold_finish(s.rox, oland_x, m.gwos.at[pl.ds(0, 3), pl.ds(0, 2), 0])
+    fold_finish(s.roy, oland_y, m.gwos.at[pl.ds(0, 3), pl.ds(0, 2), 0])
 
     def out_sum(i):
-        rows = block_rows(i, 32)
-        total = m.gwos[a, rows, :].astype(F32) + m.gwor[a1, rows, :].astype(F32)
-        total = total + m.gwor[a2, rows, :].astype(F32)
-        total = total + m.gwor[a3, rows, :].astype(F32)
-        m.gos[lax.div(i, 2), lax.rem(i, 2)] = total.astype(BF16)
-
-    each(0, 8, out_sum)
-    rgo_copy = copy(m.gos.at[:, 1 - c], m.gor, s.rgo[0].at[4], s.rgo[1].at[4], (a, sib))
-    rgo_copy.start()
-
-    sum_finish(s.rgu, up_gate_share, m.guz)
-
-    def up_gate_sum(i):
-        j = lax.div(i, 4)
-        g = lax.rem(i, 4)
-        total = m.gus[z, c, j, g].astype(F32) + m.gur[z, j, g].astype(F32)
-        total = total + landed(m.guz, (j, g))
-        m.gux[g, j] = total.astype(BF16)
-
-    each(0, 8, up_gate_sum)
-    xy_peers(lambda p: xy_start(s.gfx, m.gux.at[p], m.guxr.at[a], p))
-    xy_drain(s.gfx, m.gux.at[0])
-    m.guxr[a] = m.gux[a]
-
-    rgo_copy.wait_recv()
-    out_share = lambda zt: m.gos.at[zt, c]
-
-    def add_out(zt):
-        m.gos[zt, c] = (m.gos[zt, c].astype(F32) + m.gor[zt].astype(F32)).astype(BF16)
+        total = m.gwos[a, i, c].astype(F32) + m.oland[0, i].astype(F32)
+        m.gos[i] = (total + m.oland[1, i].astype(F32)).astype(BF16)
+
+    each(0, 4, out_sum)
+    out_share = lambda zt: m.gos.at[zt]
 
     def pass_out(zt, slot):
-        m.gos[zt, c] = (m.gos[zt, c].astype(F32) + m.goz[slot].astype(F32)).astype(BF16)
-
-    z_peers(add_out)
+        m.gos[zt] = (m.gos[zt].astype(F32) + m.goz[slot].astype(F32)).astype(BF16)
+
     sum_start(s.rgo, out_share, m.goz)
-    sum_finish(s.rgd, down_share, m.gdz)
-    some = slice(0, share_rows)
-    fd_o[...] = (
-        m.gds[z, c, some, :].astype(F32) + m.gdr[z, some, :].astype(F32)
-    ) + landed(m.gdz, (some, slice(None)))
+    own_half = down_sum(part)
+    far_copy.wait_recv()
+    fd_o[...] = own_half[0:share_rows, :] + m.dfar[0:share_rows, :].astype(F32)
     sum_pass(s.rgo, out_share, m.goz, pass_out)
 
-    sum_finish(s.gt, token_share, m.yrecv)
+    sum_finish(s.gt, m.yrecv, m.yrecv.at[pl.ds(0, 3)])
     copy(
-        m.gtr.at[z], m.gtr.at[z], s.gt[0].at[4 + z], s.gt[1].at[4 + z], (a, sib)
+        m.gtr.at[z], m.gtr.at[z], s.gt[0].at[1], s.gt[1].at[4 + z], (a, sib)
     ).wait_recv()
 
     def token_sum(i):
@@ -1045,16 +1196,17 @@
 
     each(0, 4, token_sum)
 
-    seq_peers(lambda p: seq_wait(s.gwa, m.gar.at[p], p))
+    all_wait(s.gwa, m.gar.at[pl.ds(0, 7)])
     gar_o[...] = m.gar[...]
 
-    xy_peers(lambda p: xy_wait(s.gfx, m.guxr.at[p], p))
-    gux_o[...] = m.guxr[...]
-
-    sum_finish(s.rgo, out_share, m.goz)
-    gwo_o[...] = (m.gos[z, c].astype(F32) + m.gor[z].astype(F32)) + landed(m.goz, ())
-
-    seq_peers(lambda p: seq_wait(s.fin2, m.fin2.at[p], p))
+    all_wait(s.gxg, m.gxr.at[pl.ds(0, 7), 0])
+    all_wait(s.gxu, m.gxr.at[pl.ds(0, 7), 1])
+    gux_o[...] = m.gxr[...]
+
+    sum_finish(s.rgo, m.goz, m.goz.at[pl.ds(0, 3)])
+    gwo_o[...] = m.gos[z].astype(F32) + landed(m.goz, ())
+
+    all_wait(s.fin2, m.fin2.at[pl.ds(0, 7)])
     everything = jnp.sum(m.fin2[...], axis=0)
     fin_o[0:8, :] = everything[0:8, :]
     loss = jnp.sum(everything[8:9, :]) / (2.0 * width * valid_total)
@@ -1066,9 +1218,6 @@
 
     pers_o[...] = m.pers[...]
 
-    rgd_copy.wait_send()
-    rgu_copy.wait_send()
-    rgo_copy.wait_send()
     for last in finals:
         last()
 
@@ -1101,9 +1250,13 @@
         gk_o[:, cols] = gar[head, :, 128:256].astype(F32)
         gv_o[:, cols] = gar[head, :, 256:384].astype(F32)
         gwg_o[:, cols] = gar[head, :, 384:512].astype(F32)
-    for part in range(4):
-        fg_o[:, part * hidden : (part + 1) * hidden] = gux[part, 0, :, 0:hidden].astype(F32)
-        fu_o[:, part * hidden : (part + 1) * hidden] = gux[part, 1, :, 0:hidden].astype(F32)
+    run = hidden // 8
+    for place, target in enumerate((fg_o, fu_o)):
+        for group in range(4):
+            total = gux[group, place].astype(F32) + gux[group + 4, place].astype(F32)
+            for i in range(8):
+                start = run * (4 * i + group)
+                target[:, start : start + run] = total[:, run * i : run * i + run]
 
 
 def local_block(
@@ -1126,7 +1279,7 @@
         shape((32, width), F32),
         shape((16, 128), F32),
         shape((32, 128), F32),
-        shape((4, 2, 32, pad), BF16),
+        shape((8, 2, 32, pad), BF16),
         shape((share, width), F32),
     )
     scratch = [pltpu.VMEM(*table[name]) for name in names]

time: 226 us -> 216 us (0.956)
  Pallas kernels: 225 us -> 215 us
    pallas_call x1, Pallas kernels: 222 us -> 211 us  [local_block(): pl.pallas_call(functools.partial(block_kernel, names, width, hidden, doc_...]
where the time goes in v4:
time: 216 us; the launch traced here: 215 us
  Pallas kernels  215 us (100%)
    pallas_call x1, Pallas kernels, local_block(): pl.pallas_call(functools.partial(block_kernel, names, width, hidden, doc_...  211 us

profile of v4, /device:TPU:0, one launch (start us, length us, event | category | flops | bytes accessed | tf_op | source)
XLA Modules:
  0.0 215.4 jit_solution(17851780340000839883)
XLA Ops:
  0.7 211.2 %block.1 = (bf16[128,1024]{1,0:T(8,128)(2,1)}, f32[128,1024]{1,0:T(8,128)}, bf16[8,32,512]{2,1,0:T(8,128)(2,1)}, f32[32,1024]{1,0:T(8,128)}, f32[16,128]{1,0:T(8...) custom-call(bf16[128,1024]{1,0:T(8,128)(2,1)} %bitcast.8, ...), custom_call_target="tpu_custom_call" | custom-call | tf_op jit(solution)/shard_map/block/pallas_call | solution.py:1288
  211.8 3.5 %finish.1 = (bf16[128,1024]{1,0:T(8,128)(2,1)}, f32[1,1]{1,0:T(1,128)}, f32[128,1024]{1,0:T(8,128)}, f32[32,1024]{1,0:T(8,128)}, f32[32,1024]{1,0:T(8,128)}, /*i...) custom-call(bf16[128,1024]{1,0:T(8,128)(2,1)} %get-tuple-element.36., ...), custom_call_target="tpu_custom_call" | custom-call | tf_op jit(solution)/shard_map/finish/pallas_call | solution.py:1310

commit v5 on v4

--- a/solution.py
+++ b/solution.py
@@ -393,10 +393,10 @@
     wo_place = lambda zs: m.wo_all.at[a, zs, c]
     line_start_near(s.wo, wo, wo_place)
     line_start_far(s.wo, wo, wo_place, m.wo_all.at[0, :, 0], m.wo_all.at[0, pl.ds(0, 2), 0])
-    line_start_near(s.x, tok, x_place)
     line_start_far(
         s.x, tok, x_place, m.x_all.at[pl.ds(0, 512), :], m.x_all.at[pl.ds(0, 256), :]
     )
+    line_start_near(s.x, tok, x_place)
     pass_copy(s.x, tok, x_view(b), z).start()
     finals.append(lambda: sent(s.x[0].at[1], m.x_all.at[pl.ds(0, 512), :]))
     down_x = lambda i: m.fdp.at[2 * i]
@@ -439,8 +439,6 @@
     @pl.when(jnp.logical_not(inner_chip))
     def _():
         columns(s.fxg, 0)
-        columns(s.fxu, 1)
-        down_copy.start()
 
 
     all_wait(s.w1, m.wqk.at[pl.ds(0, 224), :])
@@ -514,7 +512,6 @@
     wo_pass(a, wo_half(a)).start()
     finals.append(lambda: sent(s.wo[0].at[1], m.wo_all.at[:, :, 0]))
     chips = tuple(2 * zs + core for zs in order for core in range(2))
-    pieces_on((sib,) + chips[0:2], s.fxg, s.fgx, 0)
 
     gather_line(s.x, x_view, order[1])
     gather_line(s.x, x_view, order[2])
@@ -523,8 +520,8 @@
     @pl.when(inner_chip)
     def _():
         columns_near(s.fxg, 0)
-        columns(s.fxu, 1)
-        down_copy.start()
+
+    columns(s.fxu, 1)
 
     project(2 * order[1] + c)
     project(2 * order[2] + c)
@@ -611,18 +608,25 @@
 
     attend = lambda i: by_extent(i, attend_keys)
 
-    def attend_send(step):
+    pieces_on((sib,) + chips[0:2], s.fxg, s.fgx, 0)
+
+    def attend_step(step):
         i = lax.rem(b + step, 8)
         attend(i)
-        all_start(s.mx, m.mgs.at[block_rows(i, 128), :], m.mg.at[b], i)
-
-    each(1, 4, attend_send)
-    pieces_on(chips[2:6], s.fxg, s.fgx, 0)
-    pieces_on((sib,) + chips[0:2], s.fxu, s.fux, 1)
-    each(4, 8, attend_send)
+
+        @pl.when(step < 8)
+        def _():
+            all_start(s.mx, m.mgs.at[block_rows(i, 128), :], m.mg.at[b], i)
+
+        @pl.when(step == 3)
+        def _():
+            pieces_on(chips[2:6], s.fxg, s.fgx, 0)
+            pieces_on((sib,) + chips[0:2], s.fxu, s.fux, 1)
+
+    each(1, 9, attend_step)
     drain(s.mx, m.mgs.at[pl.ds(0, 896), :])
-    attend(b)
     m.mg[b] = m.mgs[own_rows, :]
+    down_copy.start()
     quad_pass(s.fgx, lambda i: m.fgu.at[0, i], nx, ny)
     pieces_on(chips[2:6], s.fxu, s.fux, 1)
     copy(far_down, far_down, s.fd[0].at[0], s.fd[1].at[0], (a, far)).wait_recv()
@@ -968,17 +972,8 @@
 
     attend_back = lambda i: by_extent(i, attend_back_keys)
 
-    attend_back(b)
-
-    def attend_back_next(step):
-        i = lax.rem(b + step, 8)
-        seq_wait(s.dm, m.dmg.at[i], i)
-        attend_back(i)
-
-    each(1, 4, attend_back_next)
-    each(4, 6, attend_back_next)
     def owner_all(fold, pair, share, place):
-        fold_finish(fold, m.gland.at[place], m.gus.at[place, pl.ds(0, 3)])
+        landed_all(fold[1].at[1], m.gland.at[place])
 
         def owner_rows(p):
             rows = block_rows(p, 32)
@@ -990,12 +985,26 @@
             all_start(pair, m.gxs.at[p, place], m.gxr.at[b, place], p)
 
         seq_peers(owner_send)
-        drain(pair, m.gxs.at[pl.ds(0, 7), place])
         owner_rows(b)
         m.gxr[b, place] = m.gxs[b, place]
 
-    owner_all(s.rg, s.gxg, gate_share, 0)
-    each(6, 8, attend_back_next)
+    def attend_back_step(step):
+        i = lax.rem(b + step, 8)
+
+        @pl.when(step > 0)
+        def _():
+            seq_wait(s.dm, m.dmg.at[i], i)
+
+        @pl.when(step == 6)
+        def _():
+            owner_all(s.rg, s.gxg, gate_share, 0)
+
+        attend_back(i)
+
+    each(0, 8, attend_back_step)
+    for place, (fold, pair) in enumerate(((s.rg, s.gxg), (s.ru, s.gxu))):
+        drain(fold, m.gus.at[place, pl.ds(0, 3)])
+        drain(pair, m.gxs.at[pl.ds(0, 7), place])
     fold_pass(
         s.rdx, down_x_share, m.dpre.at[0], m.dland.at[0],
         fold_add(down_x_share, m.dpre.at[0], 32), nx,
@@ -1023,68 +1032,6 @@
         m.dq[rows, 256:384] = jnp.transpose(nn(mixed_turned, m.both[:, cols])).astype(BF16)
 
     each(0, 8, key_value_grad)
-
-    def token_grad(i):
-        return nt(m.dq[block_rows(i, 128), :], m.wqk[...])
-
-    def token_sib(zt):
-        m.gts[zt, 1 - c] = token_grad(2 * zt + 1 - c).astype(BF16)
-        copy(
-            m.gts.at[zt, 1 - c], m.gtr.at[zt], s.gt[0].at[1], s.gt[1].at[4 + zt],
-            (a, sib),
-        ).start()
-
-    for zt in (near + (1 - inside) * (across - near), mirror, across + (1 - inside) * (near - across), z):
-        token_sib(zt)
-
-    fold_finish(s.rdx, m.dland.at[0], m.gds.at[pl.ds(0, 3)])
-    fold_finish(s.rdy, m.dland.at[1], m.gds.at[pl.ds(0, 3)])
-
-    def down_sum(j):
-        total = m.gds[2 * a + j].astype(F32) + m.dland[j, 0].astype(F32)
-        return total + m.dland[j, 1].astype(F32)
-
-    m.dsum[0] = down_sum(1 - part).astype(BF16)
-    far_copy = copy(m.dsum.at[0], m.dfar, s.gfd[0].at[0], s.gfd[1].at[0], (a, far))
-    far_copy.start()
-    finals.append(far_copy.wait_send)
-
-    token_share = lambda zt: m.gts.at[zt, c]
-
-    def token_line(zt):
-        mine = token_grad(2 * zt + c)
-        copy(
-            m.gtr.at[zt], m.gtr.at[zt], s.gt[0].at[1], s.gt[1].at[4 + zt], (a, sib)
-        ).wait_recv()
-        m.gts[zt, c] = (mine + m.gtr[zt].astype(F32)).astype(BF16)
-
-    def pass_token(zt, slot):
-        m.gts[zt, c] = (m.gts[zt, c].astype(F32) + m.yrecv[slot].astype(F32)).astype(BF16)
-
-    token_line(near + (1 - inside) * (across - near))
-
-    @pl.when(inner_chip)
-    def _():
-        sum_near(s.gt, token_share, m.yrecv)
-
-    @pl.when(jnp.logical_not(inner_chip))
-    def _():
-        sum_far(s.gt, token_share, m.yrecv, across, mirror, 1)
-
-    token_line(mirror)
-
-    @pl.when(jnp.logical_not(inner_chip))
-    def _():
-        sum_far(s.gt, token_share, m.yrecv, mirror, near, 2)
-
-    token_line(across + (1 - inside) * (near - across))
-
-    @pl.when(jnp.logical_not(inner_chip))
-    def _():
-        sum_near(s.gt, token_share, m.yrecv)
-
-    m.own[...] = token_grad(b)
-    finals.append(lambda: sent(s.gt[0].at[1], m.gtr))
 
     def head_weight_grad(i):
         cols = pl.ds(pl.multiple_of(i * 256, 256), 256)
@@ -1098,6 +1045,68 @@
     fold_start(s.rwx, weight_x, m.wpre.at[0], land_x, ny)
     fold_start(s.rwy, weight_y, m.wpre.at[1], land_y, nx)
 
+    def token_grad(i):
+        return nt(m.dq[block_rows(i, 128), :], m.wqk[...])
+
+    def token_sib(zt):
+        m.gts[zt, 1 - c] = token_grad(2 * zt + 1 - c).astype(BF16)
+        copy(
+            m.gts.at[zt, 1 - c], m.gtr.at[zt], s.gt[0].at[1], s.gt[1].at[4 + zt],
+            (a, sib),
+        ).start()
+
+    for zt in (near + (1 - inside) * (across - near), mirror, across + (1 - inside) * (near - across), z):
+        token_sib(zt)
+
+    fold_finish(s.rdx, m.dland.at[0], m.gds.at[pl.ds(0, 3)])
+    fold_finish(s.rdy, m.dland.at[1], m.gds.at[pl.ds(0, 3)])
+
+    def down_sum(j):
+        total = m.gds[2 * a + j].astype(F32) + m.dland[j, 0].astype(F32)
+        return total + m.dland[j, 1].astype(F32)
+
+    m.dsum[0] = down_sum(1 - part).astype(BF16)
+    far_copy = copy(m.dsum.at[0], m.dfar, s.gfd[0].at[0], s.gfd[1].at[0], (a, far))
+    far_copy.start()
+    finals.append(far_copy.wait_send)
+
+    token_share = lambda zt: m.gts.at[zt, c]
+
+    def token_line(zt):
+        mine = token_grad(2 * zt + c)
+        copy(
+            m.gtr.at[zt], m.gtr.at[zt], s.gt[0].at[1], s.gt[1].at[4 + zt], (a, sib)
+        ).wait_recv()
+        m.gts[zt, c] = (mine + m.gtr[zt].astype(F32)).astype(BF16)
+
+    def pass_token(zt, slot):
+        m.gts[zt, c] = (m.gts[zt, c].astype(F32) + m.yrecv[slot].astype(F32)).astype(BF16)
+
+    token_line(near + (1 - inside) * (across - near))
+
+    @pl.when(inner_chip)
+    def _():
+        sum_near(s.gt, token_share, m.yrecv)
+
+    @pl.when(jnp.logical_not(inner_chip))
+    def _():
+        sum_far(s.gt, token_share, m.yrecv, across, mirror, 1)
+
+    token_line(mirror)
+
+    @pl.when(jnp.logical_not(inner_chip))
+    def _():
+        sum_far(s.gt, token_share, m.yrecv, mirror, near, 2)
+
+    token_line(across + (1 - inside) * (near - across))
+
+    @pl.when(jnp.logical_not(inner_chip))
+    def _():
+        sum_near(s.gt, token_share, m.yrecv)
+
+    m.own[...] = token_grad(b)
+    finals.append(lambda: sent(s.gt[0].at[1], m.gtr))
+
     gos_copy.wait_recv()
 
     def out_add(k):
@@ -1115,6 +1124,7 @@
     fold_start(s.rox, out_x, m.opre.at[0], oland_x, ny)
     fold_start(s.roy, out_y, m.opre.at[1], oland_y, nx)
 
+    sum_pass(s.gt, token_share, m.yrecv, pass_token)
     fold_pass(s.rwx, weight_x, m.wpre.at[0], land_x, fold_add(weight_x, m.wpre.at[0], 32), nx)
     fold_pass(s.rwy, weight_y, m.wpre.at[1], land_y, fold_add(weight_y, m.wpre.at[1], 32), ny)
     all_wait(s.fin1, m.fin1.at[pl.ds(0, 3)])
@@ -1146,7 +1156,6 @@
 
     fold_pass(s.rox, out_x, m.opre.at[0], oland_x, fold_add(out_x, m.opre.at[0], 1), nx)
     fold_pass(s.roy, out_y, m.opre.at[1], oland_y, fold_add(out_y, m.opre.at[1], 1), ny)
-    sum_pass(s.gt, token_share, m.yrecv, pass_token)
     fold_finish(s.rwx, land_x, m.gws.at[pl.ds(0, 3), pl.ds(0, 128), :])
     fold_finish(s.rwy, land_y, m.gws.at[pl.ds(0, 3), pl.ds(0, 128), :])
 

time: 216 us -> 207 us (0.958)
  Pallas kernels: 215 us -> 206 us
    pallas_call x1, Pallas kernels: 211 us -> 203 us  [local_block(): pl.pallas_call(functools.partial(block_kernel, names, width, hidden, doc_...]
where the time goes in v5:
time: 207 us
  Pallas kernels  206 us (100%)
    pallas_call x1, Pallas kernels, local_block(): pl.pallas_call(functools.partial(block_kernel, names, width, hidden, doc_...  203 us

profile of v5, /device:TPU:0, one launch (start us, length us, event | category | flops | bytes accessed | tf_op | source)
XLA Modules:
  0.0 207.2 jit_solution(348119186682406375)
XLA Ops:
  0.7 203.0 %block.1 = (bf16[128,1024]{1,0:T(8,128)(2,1)}, f32[128,1024]{1,0:T(8,128)}, bf16[8,32,512]{2,1,0:T(8,128)(2,1)}, f32[32,1024]{1,0:T(8,128)}, f32[16,128]{1,0:T(8...) custom-call(bf16[128,1024]{1,0:T(8,128)(2,1)} %bitcast.8, ...), custom_call_target="tpu_custom_call" | custom-call | tf_op jit(solution)/shard_map/block/pallas_call | solution.py:1297
  203.6 3.5 %finish.1 = (bf16[128,1024]{1,0:T(8,128)(2,1)}, f32[1,1]{1,0:T(1,128)}, f32[128,1024]{1,0:T(8,128)}, f32[32,1024]{1,0:T(8,128)}, f32[32,1024]{1,0:T(8,128)}, /*i...) custom-call(bf16[128,1024]{1,0:T(8,128)(2,1)} %get-tuple-element.36., ...), custom_call_target="tpu_custom_call" | custom-call | tf_op jit(solution)/shard_map/finish/pallas_call | solution.py:1319

commit v6 on v5

--- a/solution.py
+++ b/solution.py
@@ -68,7 +68,7 @@
     fin2=8, pers=8, sc=8, y=8, df=8, ds=8, fd=1, gfd=1, gos=1,
 )
 XY_FLAGS = dict(
-    t1=4, p1=4, w2=4, wox=4, fgx=4, fux=4, fdx=4, fdy=4, rg=3, ru=3, rdx=3, rdy=3, rox=3, roy=3,
+    t1=4, p1=4, w2=4, wox=4, fgx=4, fux=4, fdx=4, fdy=4, rga=3, rgb=3, rua=3, rub=3, rdx=3, rdy=3, rox=3, roy=3,
     rwx=3, rwy=3, fin1=4,
 )
 FLAGS = SEQ_FLAGS | XY_FLAGS
@@ -130,9 +130,9 @@
         dmg=((8, block, 2 * HD), BF16),
         dq=((length, 512), BF16),
         ggain=((1, width), F32),
-        gus=((2, 4, 256, hidden_pad), BF16),
-        gpre=((2, 256, hidden_pad), BF16),
-        gland=((2, 2, 256, hidden_pad), BF16),
+        gus=((2, 4, 4, 2, 32, hidden_pad), BF16),
+        gpre=((2, 2, 4, 32, hidden_pad), BF16),
+        gland=((2, 2, 2, 4, 32, hidden_pad), BF16),
         gxs=((8, 2, 32, hidden_pad), BF16),
         gxr=((8, 2, 32, hidden_pad), BF16),
         gds=((8, 96, width), BF16),
@@ -356,6 +356,9 @@
     xy_peers(lambda p: xy_all_start(s.t1, m.tile.at[p], m.t1.at[a], p))
     xy_peers(lambda p: xy_all_start(s.p1, m.pin, m.p1.at[a], p))
     seq_peers(lambda p: all_start(s.w1, m.wcs.at[p], m.wqk.at[piece, :], p))
+    wo_place = lambda zs: m.wo_all.at[a, zs, c]
+    line_start_near(s.wo, wo, wo_place)
+    line_start_far(s.wo, wo, wo_place, m.wo_all.at[0, :, 0], m.wo_all.at[0, pl.ds(0, 2), 0])
     all_wait(s.t1, m.t1.at[pl.ds(0, 3)])
     all_wait(s.p1, m.p1.at[pl.ds(0, 3)])
     for group in range(4):
@@ -390,9 +393,6 @@
     drain(s.w1, m.wcs.at[pl.ds(0, 7)])
     x_view = lambda i: m.x_all.at[block_rows(i, 128), :]
     x_place = lambda zs: x_view(2 * zs + c)
-    wo_place = lambda zs: m.wo_all.at[a, zs, c]
-    line_start_near(s.wo, wo, wo_place)
-    line_start_far(s.wo, wo, wo_place, m.wo_all.at[0, :, 0], m.wo_all.at[0, pl.ds(0, 2), 0])
     line_start_far(
         s.x, tok, x_place, m.x_all.at[pl.ds(0, 512), :], m.x_all.at[pl.ds(0, 256), :]
     )
@@ -860,19 +860,34 @@
 
         return add
 
-    gate_share = lambda i: m.gus.at[0, i]
-    up_share = lambda i: m.gus.at[1, i]
+    folds = ((s.rga, s.rgb), (s.rua, s.rub))
+    weight_share = lambda place, core: lambda i: m.gus.at[place, i, :, core]
 
     def one_grad(i, place, grads):
         cols = pl.ds(pl.multiple_of(i * 256, 256), 256)
-        m.gus[place, i] = tn(m.sc[:, cols], grads[...]).astype(BF16)
+        m.gus[place, i] = tn(m.sc[:, cols], grads[...]).astype(BF16).reshape(4, 2, 32, pad)
+
+    def weight_start(place, core):
+        fold_start(
+            folds[place][core], weight_share(place, core), m.gpre.at[place, core],
+            m.gland.at[place, core], (ny, nx)[place],
+        )
+
+    def weight_pass(place, core):
+        share, pre = weight_share(place, core), m.gpre.at[place, core]
+        fold_pass(
+            folds[place][core], share, pre, m.gland.at[place, core], fold_add(share, pre, 1),
+            (nx, ny)[place],
+        )
 
     one_grad(diagonal, 0, m.dga)
     one_grad(ny, 0, m.dga)
-    fold_start(s.rg, gate_share, m.gpre.at[0], m.gland.at[0], ny)
+    weight_start(0, 0)
     one_grad(diagonal, 1, m.dua)
     one_grad(nx, 1, m.dua)
-    fold_start(s.ru, up_share, m.gpre.at[1], m.gland.at[1], nx)
+    weight_start(1, 0)
+    weight_start(0, 1)
+    weight_start(1, 1)
 
     half_land(s.ds, 0)
     m.ggain[...] = jnp.zeros_like(m.ggain)
@@ -907,15 +922,13 @@
     m.dmg[b] = m.dgs[b]
 
     one_grad(nx, 0, m.dga)
-    fold_pass(
-        s.rg, gate_share, m.gpre.at[0], m.gland.at[0], fold_add(gate_share, m.gpre.at[0], 32), nx
-    )
+    weight_pass(0, 0)
     one_grad(ny, 1, m.dua)
-    fold_pass(
-        s.ru, up_share, m.gpre.at[1], m.gland.at[1], fold_add(up_share, m.gpre.at[1], 32), ny
-    )
+    weight_pass(1, 0)
     one_grad(a, 0, m.dga)
     one_grad(a, 1, m.dua)
+    weight_pass(0, 1)
+    weight_pass(1, 1)
 
     def down_grad(i):
         cols = pl.ds(pl.multiple_of(i * 256, 256), 256)
@@ -972,21 +985,26 @@
 
     attend_back = lambda i: by_extent(i, attend_back_keys)
 
-    def owner_all(fold, pair, share, place):
-        landed_all(fold[1].at[1], m.gland.at[place])
-
-        def owner_rows(p):
-            rows = block_rows(p, 32)
-            total = m.gus[place, a, rows, :].astype(F32) + m.gland[place, 0, rows, :].astype(F32)
-            m.gxs[p, place] = (total + m.gland[place, 1, rows, :].astype(F32)).astype(BF16)
-
-        def owner_send(p):
-            owner_rows(p)
-            all_start(pair, m.gxs.at[p, place], m.gxr.at[b, place], p)
-
-        seq_peers(owner_send)
-        owner_rows(b)
-        m.gxr[b, place] = m.gxs[b, place]
+    def owners(core):
+        for place, pair in enumerate((s.gxg, s.gxu)):
+            landed_all(folds[place][core][1].at[1], m.gland.at[place, core])
+
+            def one(zt):
+                p = 2 * zt + core
+                total = m.gus[place, a, zt, core].astype(F32)
+                total = total + m.gland[place, core, 0, zt].astype(F32)
+                total = total + m.gland[place, core, 1, zt].astype(F32)
+                m.gxs[p, place] = total.astype(BF16)
+
+                @pl.when(p != b)
+                def _():
+                    all_start(pair, m.gxs.at[p, place], m.gxr.at[b, place], p)
+
+                @pl.when(p == b)
+                def _():
+                    m.gxr[b, place] = m.gxs[b, place]
+
+            each(1, 5, lambda step: one(lax.rem(z + step, 4)))
 
     def attend_back_step(step):
         i = lax.rem(b + step, 8)
@@ -995,15 +1013,13 @@
         def _():
             seq_wait(s.dm, m.dmg.at[i], i)
 
-        @pl.when(step == 6)
-        def _():
-            owner_all(s.rg, s.gxg, gate_share, 0)
-
+        pl.when(step == 2)(lambda: owners(0))
         attend_back(i)
 
     each(0, 8, attend_back_step)
-    for place, (fold, pair) in enumerate(((s.rg, s.gxg), (s.ru, s.gxu))):
-        drain(fold, m.gus.at[place, pl.ds(0, 3)])
+    for place, pair in enumerate((s.gxg, s.gxu)):
+        for core in range(2):
+            drain(folds[place][core], m.gus.at[place, pl.ds(0, 3), :, core])
         drain(pair, m.gxs.at[pl.ds(0, 7), place])
     fold_pass(
         s.rdx, down_x_share, m.dpre.at[0], m.dland.at[0],
@@ -1013,7 +1029,7 @@
         s.rdy, down_y_share, m.dpre.at[1], m.dland.at[1],
         fold_add(down_y_share, m.dpre.at[1], 32), ny,
     )
-    owner_all(s.ru, s.gxu, up_share, 1)
+    owners(1)
 
     m.fin0[0:32, :] = m.pgrad[...]
     for j in range(8):

time: 207 us -> 206 us (level)
  no operation moved by 1% of the time
where the time goes in v6:
time: 206 us
  Pallas kernels  206 us (100%)
    pallas_call x1, Pallas kernels, local_block(): pl.pallas_call(functools.partial(block_kernel, names, width, hidden, doc_...  202 us

profile of v6, /device:TPU:0, one launch (start us, length us, event | category | flops | bytes accessed | tf_op | source)
XLA Modules:
  0.0 206.2 jit_solution(13114888076886024629)
XLA Ops:
  0.7 202.0 %block.1 = (bf16[128,1024]{1,0:T(8,128)(2,1)}, f32[128,1024]{1,0:T(8,128)}, bf16[8,32,512]{2,1,0:T(8,128)(2,1)}, f32[32,1024]{1,0:T(8,128)}, f32[16,128]{1,0:T(8...) custom-call(bf16[128,1024]{1,0:T(8,128)(2,1)} %bitcast.8, ...), custom_call_target="tpu_custom_call" | custom-call | tf_op jit(solution)/shard_map/block/pallas_call | solution.py:1313
  202.7 3.5 %finish.1 = (bf16[128,1024]{1,0:T(8,128)(2,1)}, f32[1,1]{1,0:T(1,128)}, f32[128,1024]{1,0:T(8,128)}, f32[32,1024]{1,0:T(8,128)}, f32[32,1024]{1,0:T(8,128)}, /*i...) custom-call(bf16[128,1024]{1,0:T(8,128)(2,1)} %get-tuple-element.36., ...), custom_call_target="tpu_custom_call" | custom-call | tf_op jit(solution)/shard_map/finish/pallas_call | solution.py:1335
